TPU v7x, 32 devices: a whole 2x2x4 slice. The times are simulated.
32 devices in a mesh: rows: 8 (over y, x, core), batch: 4 (over z).
Axes of the slice: x: 2, y: 2, z: 4, core: 2. Of those that a mesh axis runs over, the one named last changes fastest.
Arguments:
- layer_input: bfloat16 [8, 128, 128, 256], P('batch', 'rows'), may hold values from -6 to 6
- hidden_state: bfloat16 [8, 128, 128, 256], P('batch', 'rows'), may hold values from -6 to 6
- crop_rows: int32 [8], P('batch'), may hold values from 113 to 128, as said below
- crop_cols: int32 [8], P('batch'), may hold values from 64 to 128, as said below
- first_gain: float32 [256], replicated, may hold values from 0.1 to 1.9
- first_shift: float32 [256], replicated, may hold values from -3 to 3
- qkv_weight: float32 [256, 768], P(('rows', 'batch')), may hold values from -0.375 to 0.375
- bias_table: float32 [225, 8], replicated, may hold values from -4 to 4
- output_weight: float32 [256, 256], P(('rows', 'batch')), may hold values from -1 to 1
- output_bias: float32 [256], replicated, may hold values from -3 to 3
- second_gain: float32 [256], replicated, may hold values from 0.1 to 1.9
- second_shift: float32 [256], replicated, may hold values from -3 to 3
- up_weight: float32 [256, 1024], P(('rows', 'batch')), may hold values from -0.375 to 0.375
- up_bias: float32 [1024], replicated, may hold values from -3 to 3
- down_weight: float32 [1024, 256], P(('rows', 'batch')), may hold values from -0.1875 to 0.1875
- down_bias: float32 [256], replicated, may hold values from -3 to 3
- conv_weight: float32 [4608, 256], P(('rows', 'batch')), may hold values from -0.09375 to 0.09375
- conv_bias: float32 [256], replicated, may hold values from -3 to 3
- cotangent: bfloat16 [8, 128, 128, 256], P('batch', 'rows'), may hold values from -6 to 6
Outputs:
- layer_output: bfloat16 [8, 128, 128, 256], P('batch', 'rows')
- input_grad: float32 [8, 128, 128, 256], P('batch', 'rows')
- hidden_grad: float32 [8, 128, 128, 256], P('batch', 'rows')
- first_gain_grad: float32 [256], replicated
- first_shift_grad: float32 [256], replicated
- qkv_weight_grad: float32 [256, 768], P(('rows', 'batch'))
- bias_table_grad: float32 [225, 8], replicated
- output_weight_grad: float32 [256, 256], P(('rows', 'batch'))
- output_bias_grad: float32 [256], replicated
- second_gain_grad: float32 [256], replicated
- second_shift_grad: float32 [256], replicated
- up_weight_grad: float32 [256, 1024], P(('rows', 'batch'))
- up_bias_grad: float32 [1024], replicated
- down_weight_grad: float32 [1024, 256], P(('rows', 'batch'))
- down_bias_grad: float32 [256], replicated
- conv_weight_grad: float32 [4608, 256], P(('rows', 'batch'))
- conv_bias_grad: float32 [256], replicated
Inputs may be any that keep to these rules, and one draw needn't show every extreme that they name: `crop_rows`: every crop reaches into the last 16 rows of the grid; one crop of the batch has all 128 rows. `crop_cols`: some crop has all 128 columns.
All inputs are finite; a program needn't handle non-finite values.
Results may differ from a plain program's by a relative error of at most 0.012.
The roundings to bfloat16 on the way count: a program that leaves them out, or rounds other values in their place, can miss the bound.
Values may be sent and summed in bfloat16 or wider, within the bound.
No kernel may reach another device: no remote copies, remote signals or barrier semaphores. Data moves between devices by JAX's collectives and lax.ppermute only.
A program may use at most 320 MiB of HBM per device.

v0:
```python
import functools

import jax
import jax.numpy as jnp
import numpy as np
from jax import lax
from jax.experimental import pallas as pl
from jax.experimental.pallas import tpu as pltpu
from jax.sharding import PartitionSpec as P

WIN = 8
EPSILON = 1e-05
MASKED = -100.0
HIGHEST = lax.Precision.HIGHEST
AXES = ("rows", "batch")
BF = jnp.bfloat16
F32 = jnp.float32
VMEM_LIMIT = 56 * 1024 * 1024
LOG2E = 1.4426950408889634


def dot(left, right):
    return jnp.dot(left, right, preferred_element_type=F32)


def dot_nt(left, right):
    return lax.dot_general(left, right, (((1,), (1,)), ((), ())), preferred_element_type=F32)


def dot_tn(left, right):
    return lax.dot_general(left, right, (((0,), (0,)), ((), ())), preferred_element_type=F32)


def iota(shape, dim):
    return lax.broadcasted_iota(jnp.int32, shape, dim)


def device_index():
    return lax.axis_index("rows") * lax.axis_size("batch") + lax.axis_index("batch")


def device_count():
    return lax.axis_size("rows") * lax.axis_size("batch")


def after(x, *others):
    return lax.optimization_barrier((x, *others))[0]


def bit_groups():
    batch, rows = lax.axis_size("batch"), lax.axis_size("rows")
    batch_bits = [1 << k for k in range(batch.bit_length() - 1)]
    row_bits = [batch << k for k in range(rows.bit_length() - 1)]
    chips = row_bits[1:]
    groups = [batch_bits[k : k + 2] for k in range(0, len(batch_bits), 2)]
    groups += [chips[k : k + 2] for k in range(0, len(chips), 2)]
    return groups + [row_bits[:1]]


def gather_steps(x, other):
    devices = device_count()
    held = x[None]
    places = [0]
    for group in bit_groups():
        masks = [0]
        for bit in group:
            masks = masks + [m | bit for m in masks]
        if group == bit_groups()[-1]:
            held = after(held, other)
        pieces = [held]
        for mask in masks[1:]:
            pieces.append(lax.ppermute(held, AXES, [(i, i ^ mask) for i in range(devices)]))
        held = jnp.concatenate(pieces, 0)
        places = [p ^ m for m in masks for p in places]
    order = np.zeros(devices, np.int32)
    for place, mask in enumerate(places):
        order[mask] = place
    return held, jnp.asarray(order)[jnp.arange(devices) ^ device_index()]


def scatter_pairs(x):
    rows, batch = lax.axis_size("rows"), lax.axis_size("batch")
    core = lax.axis_index("rows") % 2
    by_core = x.reshape((rows // 2, 2, batch) + x.shape[1:])
    mine = lax.dynamic_index_in_dim(by_core, core, 1, False)
    other = lax.dynamic_index_in_dim(by_core, 1 - core, 1, False)
    other = lax.ppermute(other, "rows", [(i, i ^ 1) for i in range(rows)])
    pairs = (mine.astype(F32) + other.astype(F32)).astype(BF)
    pairs = pairs.reshape((rows // 2 * batch,) + x.shape[1:])
    groups = [
        [(2 * chip + k) * batch + b for chip in range(rows // 2) for b in range(batch)]
        for k in range(2)
    ]
    return pairs, lambda a: lax.all_to_all(a, AXES, 0, 0, axis_index_groups=groups, tiled=True)


def gather_copies(copies):
    return lax.all_to_all(copies, AXES, 0, 0, tiled=True)


def with_vectors(parts, vectors):
    rows = parts[0].shape[1]
    flat = vectors.reshape(1, rows, -1)
    flat = jnp.broadcast_to(flat, (parts[0].shape[0],) + flat.shape[1:])
    return jnp.concatenate(list(parts) + [flat], 2)


def ring(x, by):
    devices = lax.axis_size("rows")
    return lax.ppermute(x, "rows", [(i, (i + by) % devices) for i in range(devices)])


def norm_parts(x):
    centred = x - jnp.mean(x, -1, keepdims=True)
    rstd = lax.rsqrt(jnp.mean(centred * centred, -1, keepdims=True) + EPSILON)
    return centred * rstd, rstd


def norm_back(dy, xhat, rstd, gain):
    scaled = dy * gain
    first = jnp.mean(scaled, -1, keepdims=True)
    second = jnp.mean(scaled * xhat, -1, keepdims=True)
    return (scaled - first - xhat * second) * rstd


def head_mask():
    rows, lanes = np.arange(256)[:, None], np.arange(256)[None, :]
    return (rows // 64 == (lanes % 128) // 32).astype(np.float32)


def pair_of(ref, pair, column):
    first = ref[pl.ds(pair * 128, 64), column : column + 128]
    second = ref[pl.ds(pair * 128 + 64, 64), column : column + 128]
    return jnp.concatenate([first, second], 1)


def blocks_of(ref, pair, column):
    first = ref[pl.ds(pair * 128, 64), column : column + 128]
    second = ref[pl.ds(pair * 128 + 64, 64), column : column + 128]
    nothing = jnp.zeros_like(first)
    return jnp.concatenate(
        [jnp.concatenate([first, nothing], 1), jnp.concatenate([nothing, second], 1)], 0
    )


def spread_heads(pair, mask):
    return jnp.concatenate([pair] * 4, 0) * mask


def offset_places(turned):
    rows, lanes = np.arange(256)[:, None], np.arange(128)[None, :] % 64
    row, col = lanes // WIN, lanes % WIN
    if turned:
        row, col = WIN - 1 - row, WIN - 1 - col
    return (rows == row * (2 * WIN - 1) + col).astype(np.float32)


def three_parts(x):
    high = x.astype(BF)
    rest = x - high.astype(F32)
    middle = rest.astype(BF)
    return high, middle, (rest - middle.astype(F32)).astype(BF)


def spread_bias(table, places, bias, factor):
    line = 2 * WIN - 1
    for head in range(8):
        row = jnp.broadcast_to(table[head : head + 1], (WIN, 256))
        turns = []
        for r in range(WIN):
            by = 256 - (WIN - 1 - r) * line - (WIN - 1)
            turns.append(pltpu.roll(row, by, 1, stride=1, stride_axis=0))
        wide = jnp.concatenate(turns, 0)
        total = 0.0
        for part in three_parts(wide):
            total = total + dot(part, places[...])
        bias[head * 64 : head * 64 + 64] = total * factor


def collect_bias(grad, places):
    line = 2 * WIN - 1
    wide = 0.0
    for part in three_parts(grad):
        wide = wide + dot(part, places)
    out = []
    for head in range(8):
        total = jnp.zeros((WIN, 256), F32)
        for r in range(WIN):
            at = head * 64 + r * WIN
            total = total + pltpu.roll(wide[at : at + WIN], r * line, 1, stride=1, stride_axis=0)
        out.append(jnp.sum(total, 0, keepdims=True))
    return jnp.concatenate(out, 0)


def attn_forward_body(
    height, scale, step_of, place, above, upper, lower, gain, shift, weight, table, places, mask,
    x_out, norm_out, xhat_out, rstd_out, qkv_out, prob_out, mix_out, xs, bias,
):
    sample, band = step_of(pl.program_id(0))
    columns = lower.shape[2]

    @pl.when(pl.program_id(0) == 0)
    def _():
        spread_bias(table, places, bias, 1.0 / scale)

    def rows_from(ref, first):
        def rows_in(r, _):
            x = pltpu.roll(ref[0, r].astype(F32), WIN // 2, 0)
            xs[:, first + r] = x.reshape(columns // WIN, WIN, 256)
            return 0

        lax.fori_loop(0, WIN // 2, rows_in, 0, unroll=True)

    @pl.when(band == 0)
    def _():
        rows_from(above, 0)

    @pl.when(band > 0)
    def _():
        rows_from(upper, 0)

    rows_from(lower, WIN // 2)

    def norm_in(k, _):
        tokens = pl.ds(k * 128, 128)
        x = xs[pl.ds(k * 2, 2)].reshape(128, 256)
        xhat, rstd = norm_parts(x)
        x_out[tokens] = x.astype(BF)
        xhat_out[tokens] = xhat.astype(BF)
        rstd_out[tokens] = jnp.broadcast_to(rstd, (128, 128))
        norm_out[tokens] = (xhat * gain[...] + shift[...]).astype(BF)
        return 0

    lax.fori_loop(0, columns // 16, norm_in, 0, unroll=8)
    for k in range(0, columns * WIN, 256):
        qkv_out[k : k + 256] = dot(norm_out[k : k + 256], weight[...]).astype(BF)

    key_at, query_at = iota((64, 128), 0), iota((64, 128), 1)
    window_at = query_at // 64
    query_at = query_at % 64
    row_base = place[0] + band * WIN
    key_row, query_row = key_at // WIN + row_base, query_at // WIN + row_base
    key_row = jnp.where(key_row < 0, key_row + height, key_row)
    query_row = jnp.where(query_row < 0, query_row + height, query_row)
    rows_differ = (key_row >= height - WIN // 2) != (query_row >= height - WIN // 2)
    row_bad = key_row >= place[1 + sample]

    def attend(pair, _):
        key_col = (pair * 2 + window_at) * WIN + key_at % WIN - WIN // 2
        query_col = (pair * 2 + window_at) * WIN + query_at % WIN - WIN // 2
        key_col = jnp.where(key_col < 0, key_col + columns, key_col)
        query_col = jnp.where(query_col < 0, query_col + columns, query_col)
        cols_differ = (key_col >= columns - WIN // 2) != (query_col >= columns - WIN // 2)
        bad = row_bad | (key_col >= place[3 + sample])
        minus = jnp.where(rows_differ | cols_differ, MASKED / scale, 0.0) + jnp.where(
            bad, MASKED / scale, 0.0
        )
        for half in range(2):
            keys = spread_heads(pair_of(qkv_out, pair, 256 + 128 * half), mask[...])
            queries = blocks_of(qkv_out, pair, 128 * half)
            scores = dot_nt(keys, queries).reshape(4, 64, 128)
            scores = scores + (bias[256 * half : 256 * half + 256].reshape(4, 64, 128) + minus[None])
            top = jnp.max(scores, 1, keepdims=True)
            raised = jnp.exp2((scores - top) * (scale * LOG2E))
            probs = raised * (1.0 / jnp.sum(raised, 1, keepdims=True))
            probs = probs.reshape(256, 128).astype(BF)
            prob_out[pair, 256 * half : 256 * half + 256] = probs
        return 0

    def mix(pair, _):
        for half in range(2):
            probs = prob_out[pair, 256 * half : 256 * half + 256]
            values = spread_heads(pair_of(qkv_out, pair, 512 + 128 * half), mask[...])
            mixed = dot_tn(probs, values).astype(BF)
            mix_out[pl.ds(pair * 128, 64), 128 * half : 128 * half + 128] = mixed[:64, :128]
            mix_out[pl.ds(pair * 128 + 64, 64), 128 * half : 128 * half + 128] = mixed[64:, 128:]
        return 0

    lax.fori_loop(0, columns // 16, attend, 0, unroll=8)
    lax.fori_loop(0, columns // 16, mix, 0, unroll=8)


def const_spec(shape):
    return pl.BlockSpec(shape, lambda *_: (0,) * len(shape))


SMALL_COST = pl.CostEstimate(flops=10**6, bytes_accessed=10**4, transcendentals=0)


def params():
    return pltpu.CompilerParams(vmem_limit_bytes=VMEM_LIMIT)


SMEM_SPEC = pl.BlockSpec(memory_space=pltpu.SMEM)


def band_steps(samples, bands):
    def step_of(step):
        return step % samples, bands[0] + step // samples

    return step_of, samples * len(bands)


def attn_forward(place, above, own, gain, shift, weight, table, places, mask, height, scale):
    samples, grid_rows, columns, width = own.shape
    half = WIN // 2
    bands = grid_rows // WIN
    tokens = WIN * columns
    steps = samples * bands

    def step_of(step):
        return step // bands, step % bands

    def row_block(step):
        return (step, 0)

    total = steps * tokens
    return pl.pallas_call(
        functools.partial(attn_forward_body, height, scale, step_of),
        grid=(steps,),
        in_specs=[
            SMEM_SPEC,
            pl.BlockSpec((1, half, columns, width), lambda s: (step_of(s)[0], 0, 0, 0)),
            pl.BlockSpec(
                (1, half, columns, width),
                lambda s: (step_of(s)[0], jnp.maximum(2 * step_of(s)[1] - 1, 0), 0, 0),
            ),
            pl.BlockSpec(
                (1, half, columns, width), lambda s: (step_of(s)[0], 2 * step_of(s)[1], 0, 0)
            ),
            const_spec((1, width)),
            const_spec((1, width)),
            const_spec(weight.shape),
            const_spec(table.shape),
            const_spec(places.shape),
            const_spec(mask.shape),
        ],
        out_specs=[
            pl.BlockSpec((tokens, width), row_block),
            pl.BlockSpec((tokens, width), row_block),
            pl.BlockSpec((tokens, width), row_block),
            pl.BlockSpec((tokens, 128), row_block),
            pl.BlockSpec((tokens, 3 * width), row_block),
            pl.BlockSpec((columns // 16, 512, 128), lambda s: (s, 0, 0)),
            pl.BlockSpec((tokens, width), row_block),
        ],
        out_shape=[
            jax.ShapeDtypeStruct((total, width), BF),
            jax.ShapeDtypeStruct((total, width), BF),
            jax.ShapeDtypeStruct((total, width), BF),
            jax.ShapeDtypeStruct((total, 128), F32),
            jax.ShapeDtypeStruct((total, 3 * width), BF),
            jax.ShapeDtypeStruct((total // 128, 512, 128), BF),
            jax.ShapeDtypeStruct((total, width), BF),
        ],
        scratch_shapes=[
            pltpu.VMEM((columns // WIN, WIN, WIN, width), F32),
            pltpu.VMEM((512, 128), F32),
        ],
        compiler_params=params(),
        cost_estimate=SMALL_COST,
        name="attn_forward",
    )(place, above, own, own, gain, shift, weight, table, places, mask)


def gelu_parts(x):
    share = 0.5 + 0.5 * lax.erf(x * 0.7071067811865476)
    bell = jnp.exp2(x * x * (-0.5 * LOG2E))
    return x * share, share + x * (bell * 0.3989422804014327)


def ffn_forward_body(
    height, step_of, place, x_ref, mix, out_w, out_b, gain, shift, up_w, up_b, down_w, down_b,
    norm_out, xhat_out, rstd_out, act_out, slope_out, sum_out, first_rows, sums,
):
    sample, band = step_of(pl.program_id(0))
    columns = sum_out.shape[2]
    chunk = 256
    chunks = columns * WIN // chunk

    def attend_sum(k, _):
        tokens = pl.ds(k * chunk, chunk)
        first = x_ref[tokens].astype(F32) + dot(mix[tokens], out_w[...]) + out_b[...]
        sums[pl.ds(k * (chunk // 64), chunk // 64)] = first.reshape(chunk // 64, WIN, WIN, 256)
        xhat, rstd = norm_parts(first)
        norm_out[tokens] = (xhat * gain[...] + shift[...]).astype(BF)
        xhat_out[tokens] = xhat.astype(BF)
        rstd_out[tokens] = jnp.broadcast_to(rstd, (chunk, 128))
        return 0

    def raise_up(k, _):
        tokens = pl.ds(k * chunk, chunk)
        for f in range(0, 1024, 256):
            raised = dot(norm_out[tokens], up_w[:, f : f + 256]) + up_b[:, f : f + 256]
            act, slope = gelu_parts(raised)
            act_out[tokens, f : f + 256] = act.astype(BF)
            slope_out[tokens, f : f + 256] = slope.astype(BF)
        return 0

    def put_down(k, _):
        tokens = pl.ds(k * chunk, chunk)
        windows = pl.ds(k * (chunk // 64), chunk // 64)
        second = dot(act_out[tokens], down_w[...]) + down_b[...]
        sums[windows] += second.reshape(chunk // 64, WIN, WIN, 256)
        return 0

    lax.fori_loop(0, chunks, attend_sum, 0, unroll=True)
    lax.fori_loop(0, chunks, raise_up, 0, unroll=True)
    lax.fori_loop(0, chunks, put_down, 0, unroll=True)
    column = iota((columns, 1), 0)

    def rows_out(r, _):
        row = place[0] + band * WIN + r
        row = jnp.where(row < 0, row + height, row)
        limit = jnp.where(row < place[1 + sample], place[3 + sample], 0)
        back = pltpu.roll(sums[:, r].reshape(columns, 256), columns - WIN // 2, 0)
        sum_out[0, r] = jnp.where(column < limit, back, 0.0).astype(BF)
        return 0

    lax.fori_loop(0, WIN, rows_out, 0, unroll=True)

    @pl.when(band == 0)
    def _():
        first_rows[0] = sum_out[0, : WIN // 2 + 1]


def ffn_forward(place, x, mix, out_w, out_b, gain, shift, up_w, up_b, down_w, down_b, height, shape):
    samples, grid_rows, columns, width = shape
    bands = grid_rows // WIN
    tokens = WIN * columns
    steps = samples * bands
    hidden = up_w.shape[1]
    total = steps * tokens

    def step_of(step):
        return step // bands, step % bands

    def row_block(step):
        return (step, 0)

    rows = [width, width, 128, hidden, hidden]
    types = [BF, BF, F32, BF, BF]
    return pl.pallas_call(
        functools.partial(ffn_forward_body, height, step_of),
        grid=(steps,),
        in_specs=[SMEM_SPEC]
        + [pl.BlockSpec((tokens, width), row_block)] * 2
        + [const_spec(a.shape) for a in (out_w, out_b, gain, shift, up_w, up_b, down_w, down_b)],
        out_specs=[pl.BlockSpec((tokens, n), row_block) for n in rows]
        + [
            pl.BlockSpec((1, WIN, columns, width), lambda s: (*step_of(s), 0, 0)),
            pl.BlockSpec((1, WIN // 2 + 1, columns, width), lambda s: (step_of(s)[0], 0, 0, 0)),
        ],
        out_shape=[jax.ShapeDtypeStruct((total, n), t) for n, t in zip(rows, types)]
        + [
            jax.ShapeDtypeStruct(shape, BF),
            jax.ShapeDtypeStruct((samples, WIN // 2 + 1, columns, width), BF),
        ],
        scratch_shapes=[pltpu.VMEM((columns // WIN, WIN, WIN, width), F32)],
        compiler_params=params(),
        cost_estimate=SMALL_COST,
        name="ffn_forward",
    )(place, x, mix, out_w, out_b, gain, shift, up_w, up_b, down_w, down_b)


def column_sum(x):
    return jnp.sum(x, 0, keepdims=True)


def ffn_backward_body(
    height, step_of, place, above, own, act, slope, normed, xhat_ref, rstd_ref, mix, conv_w,
    out_w, gain, up_w, down_w, first_out, mixed_out, down_out, up_out, out_out, vec_out,
    taps, turned, branch, low, raised_s, attn, down_acc, up_acc, out_acc, vec,
):
    step = pl.program_id(0)
    sample, band = step_of(step)
    columns = own.shape[2]
    tokens = columns * WIN
    half = WIN // 2
    column = iota((columns, 1), 0)

    @pl.when(step == 0)
    def _():
        for ref in (down_acc, up_acc, out_acc, vec):
            ref[...] = jnp.zeros_like(ref)
        for k in range(9):
            at = 256 * (k % 3)
            turned[k // 3, :, at : at + 256] = conv_w[k, 0]

    start = place[0] + half
    not_first = start != 0
    lanes = (0, 256, 512)

    @pl.when(band == 0)
    def _():
        before = jnp.where(not_first, start, height) - half - 1
        put_rows(above, half + 1, 0, sample, place, before, taps, 0, lanes)
        put_taps(own[0, 0], row_limit(place, sample, start, not_first), taps, half + 1, lanes)
        limit = row_limit(place, sample, start - 1, not_first)
        put_taps(above[0, ABOVE_LAST], limit, taps, half + 2, lanes)
        put_rows(own, half + 1, 0, sample, place, start, taps, half + 3, lanes)

    @pl.when(band > 0)
    def _():
        for group in range(2):
            first = band * WIN + (group - 1) * half - 1
            put_rows(own, half + 2, first, sample, place, start + first, taps, group * (half + 2), lanes)

    for group in range(2):
        total = 0.0
        for a in range(3):
            at = group * (half + 2) + 2 - a
            piece = taps[at : at + half].reshape(half * columns, 768)
            total = total + dot_nt(piece, turned[a])
        for k in range(half):
            row = place[0] + band * WIN + group * half + k
            row = jnp.where(row < 0, row + height, row)
            limit = row_limit(place, sample, row)
            part = jnp.where(column < limit, total[k * columns : (k + 1) * columns], 0.0)
            part = pltpu.roll(part, half, 0)
            branch[:, group * half + k] = part.reshape(columns // WIN, WIN, 256)

    chunk = 256
    windows = chunk // 64
    for k in range(tokens // chunk):
        at = slice(k * chunk, (k + 1) * chunk)
        upper = branch[k * windows : (k + 1) * windows].reshape(chunk, 256)
        low[at] = upper.astype(BF)
        vec[0:1] += column_sum(upper.astype(BF).astype(F32))
    for k in range(tokens // chunk):
        at = slice(k * chunk, (k + 1) * chunk)
        for f in range(0, 1024, 256):
            wide = slice(f, f + 256)
            raised = (dot_nt(low[at], down_w[wide]) * slope[at, wide].astype(F32)).astype(BF)
            raised_s[at, wide] = raised
            row = 4 + f // 256
            vec[row : row + 1] += column_sum(raised.astype(F32))
    for k in range(tokens // chunk):
        at = slice(k * chunk, (k + 1) * chunk)
        dy = dot_nt(raised_s[at], up_w[...])
        xhat = xhat_ref[at].astype(F32)
        rstd = rstd_ref[at]
        rstd = jnp.concatenate([rstd, rstd], 1)
        upper = branch[k * windows : (k + 1) * windows].reshape(chunk, 256)
        first = upper + norm_back(dy, xhat, rstd, gain[...])
        first_out[at] = first
        attn[at] = first.astype(BF)
        vec[1:2] += column_sum(dy * xhat)
        vec[2:3] += column_sum(dy)
        vec[3:4] += column_sum(first.astype(BF).astype(F32))
    for k in range(tokens // chunk):
        at = slice(k * chunk, (k + 1) * chunk)
        mixed_out[at] = dot_nt(attn[at], out_w[...]).astype(BF)
    low_t = low[...].T
    normed_t = normed[...].T
    for f in range(0, 1024, 256):
        wide = slice(f, f + 256)
        down_acc[:, wide] += dot(low_t, act[:, wide])
        up_acc[:, wide] += dot(normed_t, raised_s[:, wide])
    out_acc[...] += dot(mix[...].T, attn[...])

    @pl.when(step == pl.num_programs(0) - 1)
    def _():
        for f in range(0, 1024, 256):
            wide = slice(f, f + 256)
            down_out[wide] = down_acc[:, wide].T.astype(BF)
            up_out[:, wide] = up_acc[:, wide].astype(BF)
        out_out[...] = out_acc[...].astype(BF)
        vec_out[...] = vec[...].astype(BF)


def ffn_backward(
    place, above, own, act, slope, normed, xhat, rstd, mix, conv_w, out_w, gain, up_w, down_w, height
):
    samples, grid_rows, columns, width = own.shape
    bands = grid_rows // WIN
    tokens = WIN * columns
    steps = samples * bands
    total = steps * tokens
    hidden = up_w.shape[1]

    def step_of(step):
        return step // bands, step % bands

    def row_block(step):
        return (step, 0)

    def sample_block(step):
        return (step_of(step)[0], 0, 0, 0)

    rows = (act, slope, normed, xhat, rstd, mix)
    return pl.pallas_call(
        functools.partial(ffn_backward_body, height, step_of),
        grid=(steps,),
        in_specs=[
            SMEM_SPEC,
            pl.BlockSpec((1,) + above.shape[1:], sample_block),
            pl.BlockSpec((1,) + own.shape[1:], sample_block),
        ]
        + [pl.BlockSpec((tokens, a.shape[1]), row_block) for a in rows]
        + [pl.BlockSpec((9, 1, width, width), lambda s: (0, 0, 0, 0))]
        + [const_spec(a.shape) for a in (out_w, gain, up_w, down_w)],
        out_specs=[
            pl.BlockSpec((tokens, width), row_block),
            pl.BlockSpec((tokens, width), row_block),
            const_spec((hidden, width)),
            const_spec((width, hidden)),
            const_spec((width, width)),
            const_spec((8, width)),
        ],
        out_shape=[
            jax.ShapeDtypeStruct((total, width), F32),
            jax.ShapeDtypeStruct((total, width), BF),
            jax.ShapeDtypeStruct((hidden, width), BF),
            jax.ShapeDtypeStruct((width, hidden), BF),
            jax.ShapeDtypeStruct((width, width), BF),
            jax.ShapeDtypeStruct((8, width), BF),
        ],
        scratch_shapes=[
            pltpu.VMEM((WIN + 4, columns, 3 * width), BF),
            pltpu.VMEM((3, width, 3 * width), BF),
            pltpu.VMEM((columns // WIN, WIN, WIN, width), F32),
            pltpu.VMEM((tokens, width), BF),
            pltpu.VMEM((tokens, hidden), BF),
            pltpu.VMEM((tokens, width), BF),
            pltpu.VMEM((width, hidden), F32),
            pltpu.VMEM((width, hidden), F32),
            pltpu.VMEM((width, width), F32),
            pltpu.VMEM((8, width), F32),
        ],
        compiler_params=params(),
        cost_estimate=pl.CostEstimate(
            flops=2 * 10**10, bytes_accessed=10**7, transcendentals=0
        ),
        name="ffn_backward",
    )(place, above, own, *rows, conv_w, out_w, gain, up_w, down_w)


def attn_backward_body(
    scale, step_of, mixed, qkv, prob, normed, xhat_ref, rstd_ref, first, weight, gain, mask, conv_vec,
    places, input_out, up_out, qkv_out, vec_out, qkv_acc, table_acc, vec_acc, grads, score_grads, sums,
):
    step = pl.program_id(0)
    _, band = step_of(step)
    columns = input_out.shape[2]
    half = WIN // 2

    @pl.when(step == 0)
    def _():
        for ref in (qkv_acc, table_acc, vec_acc):
            ref[...] = jnp.zeros_like(ref)

    attn_backward_step(
        scale, mixed, qkv, prob, normed, xhat_ref, rstd_ref, first, weight, gain, mask,
        qkv_acc, table_acc, vec_acc, grads, score_grads, sums,
    )

    def row_out(r):
        return pltpu.roll(sums[:, r].reshape(columns, 256), columns - half, 0)

    @pl.when(band == 0)
    def _():
        for r in range(half):
            up_out[0, r] = row_out(r).astype(BF)
            input_out[0, r] = row_out(half + r)

    @pl.when(band > 0)
    def _():
        for r in range(WIN):
            input_out[0, band * WIN - half + r] = row_out(r)

    @pl.when(step == pl.num_programs(0) - 1)
    def _():
        for f in range(0, 768, 256):
            qkv_out[:, f : f + 256] = qkv_acc[:, f : f + 256].astype(BF)
        table = collect_bias(table_acc[...], places[...])
        rest = jnp.concatenate([vec_acc[0:2], conv_vec[0:1], jnp.zeros((5, 256), F32)], 0)
        vec_out[...] = jnp.concatenate([table, rest], 1).astype(BF)


def attn_backward_step(
    scale, mixed, qkv, prob, normed, xhat_ref, rstd_ref, first, weight, gain, mask,
    qkv_acc, table_acc, vec_acc, grads, score_grads, sums,
):
    tokens = qkv.shape[0]
    columns = tokens // WIN

    def attend(pair, _):
        head_at = mask[...]
        for half in range(2):
            lanes = slice(256 * half, 256 * half + 256)
            low = prob[pair, lanes]
            mixed_blocks = blocks_of(mixed, pair, 128 * half)
            values = spread_heads(pair_of(qkv, pair, 512 + 128 * half), head_at)
            prob_grad = dot_nt(values, mixed_blocks).reshape(4, 64, 128)
            probs = low.astype(F32).reshape(4, 64, 128)
            shared = jnp.sum(prob_grad * probs, 1, keepdims=True)
            score_grad = (probs * (prob_grad - shared)).astype(BF).reshape(256, 128)
            table_acc[lanes] += score_grad.astype(F32)
            score_grads[pair, lanes] = score_grad
        return 0

    def project(pair, _):
        head_at = mask[...]
        for half in range(2):
            lanes = slice(256 * half, 256 * half + 256)
            low = prob[pair, lanes]
            mixed_blocks = blocks_of(mixed, pair, 128 * half)
            score_grad = score_grads[pair, lanes]
            keys = spread_heads(pair_of(qkv, pair, 256 + 128 * half), head_at)
            queries = blocks_of(qkv, pair, 128 * half)
            query_grad = (dot_tn(score_grad, keys) * scale).astype(BF)
            out = slice(128 * half, 128 * half + 128)
            grads[pl.ds(pair * 128, 64), out] = query_grad[:64, :128]
            grads[pl.ds(pair * 128 + 64, 64), out] = query_grad[64:, 128:]
            wide = head_at.astype(F32)
            key_grad = (dot(score_grad, queries) * wide).reshape(4, 64, 256)
            key_grad = (jnp.sum(key_grad, 0) * scale).astype(BF)
            out = slice(256 + 128 * half, 256 + 128 * half + 128)
            grads[pl.ds(pair * 128, 64), out] = key_grad[:, :128]
            grads[pl.ds(pair * 128 + 64, 64), out] = key_grad[:, 128:]
            value_grad = (dot(low, mixed_blocks) * wide).reshape(4, 64, 256)
            value_grad = jnp.sum(value_grad, 0).astype(BF)
            out = slice(512 + 128 * half, 512 + 128 * half + 128)
            grads[pl.ds(pair * 128, 64), out] = value_grad[:, :128]
            grads[pl.ds(pair * 128 + 64, 64), out] = value_grad[:, 128:]
        return 0

    lax.fori_loop(0, columns // 16, attend, 0, unroll=8)
    lax.fori_loop(0, columns // 16, project, 0, unroll=8)
    for f in range(0, 768, 256):
        qkv_acc[:, f : f + 256] += dot_tn(normed[...], grads[:, f : f + 256])

    def part(k, _):
        at = pl.ds(k * 256, 256)
        dy = dot_nt(grads[at], weight[...])
        xhat = xhat_ref[at].astype(F32)
        rstd = rstd_ref[at]
        rstd = jnp.concatenate([rstd, rstd], 1)
        total = first[at] + norm_back(dy, xhat, rstd, gain[...])
        sums[pl.ds(k * 4, 4)] = total.reshape(4, WIN, WIN, 256)
        vec_acc[0:1] += column_sum(dy * xhat)
        vec_acc[1:2] += column_sum(dy)
        return 0

    lax.fori_loop(0, tokens // 256, part, 0, unroll=True)


def attn_backward(
    mixed, qkv, prob, normed, xhat, rstd, first, weight, gain, mask, conv_vec, places, scale, shape
):
    samples, grid_rows, columns, width = shape
    bands = grid_rows // WIN
    tokens = WIN * columns
    half = WIN // 2

    def step_of(step):
        return step // bands, step % bands

    def row_block(step):
        return (step, 0)

    def sample_block(step):
        return (step_of(step)[0], 0, 0, 0)

    rows = (mixed, qkv, prob, normed, xhat, rstd, first)
    consts = (weight, gain, mask, conv_vec, places)
    in_specs = [pl.BlockSpec((tokens, a.shape[1]), row_block) for a in rows]
    in_specs[2] = pl.BlockSpec((columns // 16, 512, 128), lambda s: (s, 0, 0))
    in_specs += [const_spec(a.shape) for a in consts]
    return pl.pallas_call(
        functools.partial(attn_backward_body, scale, step_of),
        grid=(samples * bands,),
        in_specs=in_specs,
        out_specs=[
            pl.BlockSpec((1,) + shape[1:], sample_block),
            pl.BlockSpec((1, half, columns, width), sample_block),
            const_spec((width, 3 * width)),
            const_spec((8, 2 * width)),
        ],
        out_shape=[
            jax.ShapeDtypeStruct(shape, F32),
            jax.ShapeDtypeStruct((samples, half, columns, width), BF),
            jax.ShapeDtypeStruct((width, 3 * width), BF),
            jax.ShapeDtypeStruct((8, 2 * width), BF),
        ],
        scratch_shapes=[
            pltpu.VMEM((width, 3 * width), F32),
            pltpu.VMEM((512, 128), F32),
            pltpu.VMEM((8, width), F32),
            pltpu.VMEM((tokens, 3 * width), BF),
            pltpu.VMEM((columns // 16, 512, 128), BF),
            pltpu.VMEM((columns // WIN, WIN, WIN, width), F32),
        ],
        compiler_params=params(),
        cost_estimate=SMALL_COST,
        name="attn_backward",
    )(*rows, *consts)


def shifted(row, column, by):
    columns = row.shape[0]
    moved = pltpu.roll(row, by % columns, 0)
    edge = 0 if by == 1 else columns - 1
    return jnp.where(column == edge, 0.0, moved)


def pack_near_body(qkv, out_w, up, down, near):
    rows = qkv.shape[0]
    at = 0
    for ref in (qkv, out_w, up):
        near[:, at : at + ref.shape[1]] = ref[...].astype(BF)
        at += ref.shape[1]
    for k in range(down.shape[0] // rows):
        near[:, at : at + down.shape[1]] = down[k * rows : (k + 1) * rows].astype(BF)
        at += down.shape[1]


def pack_near(qkv, out_w, up, down):
    rows = qkv.shape[0]
    lanes = (qkv.size + out_w.size + up.size + down.size) // rows
    return pl.pallas_call(
        pack_near_body,
        out_shape=jax.ShapeDtypeStruct((rows, lanes), BF),
        compiler_params=params(),
        cost_estimate=SMALL_COST,
        name="pack_near",
    )(qkv, out_w, up, down)


def unpack_near_body(order, held, qkv, out_w, up, down):
    devices, rows, _ = held.shape
    count = max(16 // rows, 1)

    def some(k, _):
        pieces = [held[order[k * count + n]] for n in range(count)]
        at = 0
        place = pl.ds(pl.multiple_of(k * count * rows, count * rows), count * rows)
        for ref in (qkv, out_w, up):
            lanes = slice(at, at + ref.shape[1])
            ref[place] = jnp.concatenate([piece[:, lanes] for piece in pieces], 0)
            at = lanes.stop
        width = down.shape[1]
        parts = down.shape[0] // (devices * rows)
        tall = [
            piece[:, at + n * width : at + (n + 1) * width] for piece in pieces for n in range(parts)
        ]
        size = count * rows * parts
        down[pl.ds(pl.multiple_of(k * size, size), size)] = jnp.concatenate(tall, 0)
        return 0

    lax.fori_loop(0, devices // count, some, 0, unroll=4)


def unpack_near(order, held, weights):
    devices = held.shape[0]
    return pl.pallas_call(
        unpack_near_body,
        in_specs=[SMEM_SPEC, pl.BlockSpec(memory_space=pltpu.VMEM)],
        out_shape=[jax.ShapeDtypeStruct((devices * w.shape[0], w.shape[1]), BF) for w in weights],
        compiler_params=params(),
        cost_estimate=SMALL_COST,
        name="unpack_near",
    )(order, held)


def copies_body(x, out):
    low = x[...].astype(BF)
    for k in range(out.shape[0]):
        out[k] = low


def make_copies(x, count):
    return pl.pallas_call(
        copies_body,
        out_shape=jax.ShapeDtypeStruct((count,) + x.shape, BF),
        compiler_params=params(),
        cost_estimate=SMALL_COST,
        name="make_copies",
    )(x)


def row_limit(place, sample, row, allowed=True):
    return jnp.where((row < place[1 + sample]) & allowed, place[3 + sample], 0)


def put_taps(row, limit, target, at, lanes):
    column = iota((row.shape[0], 1), 0)
    wide = jnp.where(column < limit, row.astype(F32), 0.0)
    target[at, :, lanes[0] : lanes[0] + 256] = shifted(wide, column, -1).astype(BF)
    target[at, :, lanes[1] : lanes[1] + 256] = wide.astype(BF)
    target[at, :, lanes[2] : lanes[2] + 256] = shifted(wide, column, 1).astype(BF)


def put_rows(source, count, first, sample, place, row, target, at, lanes):
    def one(r, _):
        put_taps(source[0, first + r], row_limit(place, sample, row + r), target, at + r, lanes)
        return 0

    lax.fori_loop(0, count, one, 0, unroll=True)


ABOVE_LAST = WIN // 2
ABOVE_HIDDEN = WIN // 2 + 1


def own_taps(height, place, above, own, below, taps, at):
    sample = pl.program_id(0)
    rows = own.shape[1]
    start = place[0] + WIN // 2
    lanes = (0, 256, 512)
    limit = row_limit(place, sample, start - 1, start != 0)
    put_taps(above[0, ABOVE_LAST], limit, taps, at, lanes)
    put_rows(own, rows, 0, sample, place, start, taps, at + 1, lanes)
    limit = row_limit(place, sample, start + rows, start + rows != height)
    put_taps(below[0, 0], limit, taps, at + rows + 1, lanes)


def weight_sums(groups, source, taps, acc):
    columns = taps.shape[1]
    for start, target, rows in groups:
        turned = source(target, rows).T
        for a in range(3):
            piece = taps[start + 2 - a : start + 2 - a + rows].reshape(rows * columns, 768)
            acc[a] += dot(turned, piece)


def conv_weight_body(
    height, place, above, own, below, sums, hidden, out, vec, taps, held, acc, acc_hidden
):
    sample = pl.program_id(0)

    @pl.when(sample == 0)
    def _():
        for ref in (acc, acc_hidden, vec):
            ref[...] = jnp.zeros_like(ref)

    rows, columns = own.shape[1:3]
    half = WIN // 2
    column = iota((columns, 1), 0)
    start = place[0] + half
    not_first = start != 0

    before = jnp.where(not_first, start, height) - half - 1
    put_rows(above, half + 1, 0, sample, place, before, taps, 0, (0, 256, 512))
    limit = row_limit(place, sample, start, not_first)
    put_taps(own[0, 0], limit, taps, half + 1, (0, 256, 512))
    own_taps(height, place, above, own, below, taps, half + 2)

    def one(r, _):
        limit = row_limit(place, sample, start + r)
        held[r] = jnp.where(column < limit, hidden[0, r].astype(F32), 0.0).astype(BF)
        vec[0:1] += jnp.sum(taps[half + 3 + r, :, 256:512].astype(F32), 0, keepdims=True)
        return 0

    lax.fori_loop(0, rows, one, 0, unroll=4)
    groups = ((0, 0, half), (half + 2, half, rows - half))
    weight_sums(groups, lambda t, n: sums[0, t : t + n].reshape(n * columns, 256), taps, acc)
    groups = ((half + 2, 0, rows),)
    weight_sums(groups, lambda t, n: held[t : t + n].reshape(n * columns, 256), taps, acc_hidden)

    @pl.when(sample == pl.num_programs(0) - 1)
    def _():
        for k in range(9):
            at = 256 * (k % 3)
            out[k, 0] = acc[k // 3, :, at : at + 256].astype(BF)
            out[k, 1] = acc_hidden[k // 3, :, at : at + 256].astype(BF)


def field_spec(a):
    return pl.BlockSpec((1,) + a.shape[1:], lambda s: (s, 0, 0, 0))


def conv_call(
    body, name, place, fields, consts, height, out_specs, out_shape, scratch, cost=None
):
    return pl.pallas_call(
        functools.partial(body, height),
        grid=(fields[0][1].shape[0],),
        in_specs=[SMEM_SPEC] + [s for s, _ in fields] + [s for s, _ in consts],
        out_specs=out_specs,
        out_shape=out_shape,
        scratch_shapes=scratch,
        compiler_params=params(),
        cost_estimate=cost or SMALL_COST,
        name=name,
    )(place, *[a for _, a in fields], *[a for _, a in consts])


def whole(a):
    return field_spec(a), a


def conv_weight(place, grads, sums, hidden, height):
    _, rows, columns, width = sums.shape
    shape = (9, 2, width, width)
    acc = pltpu.VMEM((3, width, 3 * width), F32)
    return conv_call(
        conv_weight_body, "conv_weight", place, [whole(a) for a in (*grads, sums, hidden)], (),
        height, [const_spec(shape), const_spec((8, width))],
        [jax.ShapeDtypeStruct(shape, BF), jax.ShapeDtypeStruct((8, width), F32)],
        [
            pltpu.VMEM((rows + WIN, columns, 3 * width), BF),
            pltpu.VMEM((rows, columns, width), BF),
            acc,
            acc,
        ],
        pl.CostEstimate(flops=2 * 10**10, bytes_accessed=10**7, transcendentals=0),
    )


def conv_data_body(height, place, above, own, below, weight, out, taps, turned):
    sample = pl.program_id(0)
    columns = own.shape[2]
    column = iota((columns, 1), 0)

    @pl.when(sample == 0)
    def _():
        for k in range(9):
            at = 256 * (k % 3)
            turned[k // 3, :, at : at + 256] = weight[k, 0]

    own_taps(height, place, above, own, below, taps, 0)
    for r in range(0, own.shape[1], 4):
        total = 0.0
        for a in range(3):
            piece = taps[r + 2 - a : r + 6 - a].reshape(4 * columns, 768)
            total = total + dot_nt(piece, turned[a])
        for k in range(4):
            limit = row_limit(place, sample, place[0] + WIN // 2 + r + k)
            part = total[k * columns : (k + 1) * columns]
            out[0, r + k] = jnp.where(column < limit, part, 0.0)


def conv_data(place, grads, weight, height):
    own = grads[1]
    width = own.shape[-1]
    weight_spec = pl.BlockSpec((9, 1, width, width), lambda s: (0, 1, 0, 0))
    return conv_call(
        conv_data_body, "conv_data", place, [whole(a) for a in grads], ((weight_spec, weight),),
        height, field_spec(own), jax.ShapeDtypeStruct(own.shape, F32),
        [
            pltpu.VMEM((own.shape[1] + 2, own.shape[2], 3 * width), BF),
            pltpu.VMEM((3, width, 3 * width), BF),
        ],
        pl.CostEstimate(flops=10**10, bytes_accessed=10**7, transcendentals=0),
    )


def conv_forward_body(
    height, place, sums, sums_below, above, hidden, below, weight, bias, out, taps
):
    sample = pl.program_id(0)
    rows, columns = out.shape[1:3]
    column = iota((columns, 1), 0)
    half = WIN // 2
    start = place[0] + half
    not_first, not_last = start != 0, start + rows != height
    lanes = (1024, 512, 0)
    limit = row_limit(place, sample, start - 1, not_first)
    put_taps(sums[0, half - 1], limit, taps, 0, lanes)
    put_rows(sums, rows - half, half, sample, place, start, taps, 1, lanes)
    put_rows(sums_below, half, 0, sample, place, start + rows - half, taps, rows - half + 1, lanes)
    after = row_limit(place, sample, start + rows, not_last)
    put_taps(sums_below[0, half], after, taps, rows + 1, lanes)
    lanes = (1280, 768, 256)
    put_taps(above[0, ABOVE_HIDDEN], limit, taps, 0, lanes)
    put_rows(hidden, rows, 0, sample, place, start, taps, 1, lanes)
    put_taps(below[0, 1], after, taps, rows + 1, lanes)
    for r in range(0, rows, 4):
        total = bias[...]
        for a in range(3):
            piece = taps[r + a : r + a + 4].reshape(4 * columns, 1536)
            total = total + dot(piece, weight[a * 1536 : (a + 1) * 1536])
        for k in range(4):
            limit = row_limit(place, sample, start + r + k)
            part = total[k * columns : (k + 1) * columns]
            out[0, r + k] = jnp.where(column < limit, part, 0.0).astype(BF)


def conv_forward(place, sums, sums_below, hidden, weight, bias, height):
    samples, rows, columns, width = sums.shape
    fields = (sums, sums_below, *hidden)
    return pl.pallas_call(
        functools.partial(conv_forward_body, height),
        grid=(samples,),
        in_specs=[SMEM_SPEC]
        + [field_spec(a) for a in fields]
        + [const_spec(weight.shape), const_spec(bias.shape)],
        out_specs=field_spec(sums),
        out_shape=jax.ShapeDtypeStruct(sums.shape, BF),
        scratch_shapes=[pltpu.VMEM((rows + 2, columns, 6 * width), BF)],
        compiler_params=params(),
        cost_estimate=SMALL_COST,
        name="conv_forward",
    )(place, *fields, weight, bias)


def shards(
    layer_input,
    hidden_state,
    crop_rows,
    crop_cols,
    first_gain,
    first_shift,
    qkv_weight,
    bias_table,
    output_weight,
    output_bias,
    second_gain,
    second_shift,
    up_weight,
    up_bias,
    down_weight,
    down_bias,
    conv_weight_in,
    conv_bias,
    cotangent,
):
    samples, grid_rows, columns, width = layer_input.shape
    shape = layer_input.shape
    heads = bias_table.shape[1]
    scale = float((width // heads) ** (-0.5))
    half = WIN // 2
    devices = device_count()
    row_devices = lax.axis_size("rows")
    height = grid_rows * row_devices
    row_place = lax.axis_index("rows")
    row_start = row_place * grid_rows
    place = jnp.concatenate(
        [(row_start - half)[None].astype(jnp.int32), crop_rows, crop_cols]
    ).astype(jnp.int32)

    hidden_width = up_weight.shape[1]

    def vec(v):
        return v.reshape(1, -1)

    input_above = ring(layer_input[:, grid_rows - half :], 1)
    rows_out, rows_down = output_weight.shape[0], down_weight.shape[0]
    near = pack_near(qkv_weight, output_weight, up_weight, down_weight)
    held, order = gather_steps(near, input_above)
    late_cotangent, late_hidden = after((cotangent, hidden_state), held)
    halo_above = jnp.concatenate(
        [late_cotangent[:, grid_rows - half - 1 :], late_hidden[:, grid_rows - 1 :]], 1
    )
    halo_below = jnp.concatenate([late_cotangent[:, :1], late_hidden[:, :1]], 1)
    halo_above, halo_below = ring(halo_above, 1), ring(halo_below, -1)
    grads = (halo_above, cotangent, halo_below)
    conv_copies = after(make_copies(conv_weight_in, devices), held, input_above)
    conv_full = gather_copies(conv_copies).reshape(-1, width)

    qkv_full, output_full, up_full, down_full = unpack_near(
        order, held, (qkv_weight, output_weight, up_weight, down_weight)
    )
    offsets = bias_table.shape[0]
    table = jnp.pad(bias_table.T, ((0, 0), (0, 256 - offsets)))
    mask = jnp.asarray(head_mask(), BF)

    x, normed, xhat, rstd, qkv, prob, mix = attn_forward(
        place, input_above, layer_input, vec(first_gain), vec(first_shift), qkv_full, table,
        jnp.asarray(offset_places(False), BF), mask, height, scale,
    )
    normed_2, xhat_2, rstd_2, act, slope, sums, sums_first = ffn_forward(
        place, x, mix, output_full, vec(output_bias), vec(second_gain), vec(second_shift),
        up_full, vec(up_bias), down_full, vec(down_bias), height, shape,
    )
    conv_local, conv_bias_part = conv_weight(place, grads, sums, hidden_state, height)
    conv_local, exchange = scatter_pairs(conv_local.reshape(devices, -1, width))
    conv_all = exchange(conv_local)
    sums_below = ring(after(sums_first, conv_local), -1)
    conv_blocks = after(conv_full.reshape(9, 2, width, width), conv_local)
    first_grad, mixed, down_acc, up_acc, out_acc, vec_ffn = ffn_backward(
        place, halo_above, cotangent, act, slope, normed_2, xhat_2, rstd_2, mix, conv_blocks,
        output_full, vec(second_gain), up_full, down_full, height,
    )
    input_grad, input_up, qkv_acc, vec_attn = attn_backward(
        after(mixed, sums_below), qkv, prob, normed, xhat, rstd, first_grad, qkv_full,
        vec(first_gain), mask, conv_bias_part, jnp.asarray(offset_places(True), BF).T, scale, shape,
    )
    down_local = down_acc.reshape(devices, -1, rows_out, width).transpose(0, 2, 1, 3)
    parts = [
        down_local.reshape(devices, rows_out, -1),
        *(a.reshape(devices, rows_out, -1) for a in (out_acc, up_acc, qkv_acc)),
    ]
    last_local, exchange = scatter_pairs(
        with_vectors(parts, jnp.concatenate([vec_ffn, vec_attn], 1))
    )
    last_all = exchange(last_local)
    input_from_below = ring(after(input_up, last_local), -1)
    hidden_grad = conv_data(after(place, last_local), grads, conv_blocks, height)
    layer_output = conv_forward(
        after(place, hidden_grad), sums, sums_below, (halo_above, hidden_state, halo_below),
        conv_full, vec(conv_bias), height,
    )

    input_grad = lax.dynamic_update_slice(
        after(input_grad, layer_output), input_from_below.astype(F32), (0, grid_rows - half, 0, 0)
    )

    def total(parts):
        return jnp.sum(parts.astype(F32), 0)

    conv_weight_grad = total(conv_all)
    ends = np.cumsum([0, hidden_width, width, hidden_width, 3 * width])
    sums_all = total(last_all)
    parts = [sums_all[:, ends[k] : ends[k + 1]] for k in range(4)]
    down_weight_grad = parts[0].reshape(rows_out, -1, width).transpose(1, 0, 2)
    down_weight_grad = down_weight_grad.reshape(rows_down, width)
    output_weight_grad, up_weight_grad, qkv_weight_grad = parts[1:]
    vectors = sums_all[:, ends[4] :].reshape(8, 3, width)
    ffn_vec, table_grad, attn_vec = (vectors[:, k] for k in range(3))
    down_bias_grad, second_gain_grad, second_shift_grad, output_bias_grad = (
        ffn_vec[k] for k in range(4)
    )
    up_bias_grad = ffn_vec[4:].reshape(-1)
    bias_table_grad = table_grad[:, :offsets][:, ::-1].T
    first_gain_grad, first_shift_grad, conv_bias_grad = (attn_vec[k] for k in range(3))
    return (
        layer_output,
        input_grad,
        hidden_grad,
        first_gain_grad,
        first_shift_grad,
        qkv_weight_grad,
        bias_table_grad,
        output_weight_grad,
        output_bias_grad,
        second_gain_grad,
        second_shift_grad,
        up_weight_grad,
        up_bias_grad,
        down_weight_grad,
        down_bias_grad,
        conv_weight_grad,
        conv_bias_grad,
    )


def solution(mesh):
    field = P("batch", "rows", None, None)
    weight = P(AXES, None)
    in_specs = (
        field, field, P("batch"), P("batch"), P(), P(), weight, P(), weight, P(), P(), P(),
        weight, P(), weight, P(), weight, P(), field,
    )
    out_specs = (
        field, field, field, P(), P(), weight, P(), weight, P(), P(), P(), weight, P(), weight,
        P(), weight, P(),
    )
    return jax.shard_map(shards, mesh=mesh, in_specs=in_specs, out_specs=out_specs, check_vma=False)
```

profile of v0, /device:TPU:0, one launch (start us, length us, event | category | flops | bytes accessed | tf_op | source)
XLA Modules:
  0.0 202.7 jit_solution(4652847827567645519)
XLA Ops:
  0.7 1.4 pack_near.1
  2.1 5.0 %collective-permute-start.2 = (bf16[1,8,3072]{2,1,0:T(8,128)(2,1)}, bf16[1,8,3072]{2,1,0:T(8,128)(2,1)S(1)}, u32[]{:S(2)}, u32[]{:S(2)}) collective-permute-start(bf16[1,8,3072]{2,1,0:T(8,128)(2,1)} %bitcast.68), channel_id=1, source_target_pairs={{0,3},{1,2},{2,1},{3,0},{4,7},{5,6},{6,5},{7,4},{8,11},{9,10},{10,... | collective-permute-start | bytes 147464 | tf_op jit(solution)/shard_map/ppermute | solution.py:72
  7.1 0.6 collective-permute-start
  7.7 1.1 slice.78
  8.9 0.8 constant_dynamic-update-slice_fusion.6
  9.7 2.7 %collective-permute-done.1 = bf16[1,8,3072]{2,1,0:T(8,128)(2,1)S(1)} collective-permute-done((bf16[1,8,3072]{2,1,0:T(8,128)(2,1)}, bf16[1,8,3072]{2,1,0:T(8,128)(2,1)S(1)}, u32[]{:S(2)}, u32[]{:S(2)}) %collective-permute-start.1) | collective-permute-done | bytes 49184 | tf_op jit(solution)/shard_map/ppermute | solution.py:72
  12.3 0.8 pad_maximum_fusion.2
  13.2 2.5 %collective-permute-start.5 = (bf16[4,8,3072]{2,1,0:T(8,128)(2,1)S(1)}, bf16[4,8,3072]{2,1,0:T(8,128)(2,1)S(1)}, u32[]{:S(2)}, u32[]{:S(2)}) collective-permute-start(bf16[4,8,3072]{2,1,0:T(8,128)(2,1)S(1)} %pad_maximum_fusion.2), channel_id=1, source_target_pairs={{0,24},{1,25},{2,26},{3,27},{4,28},{5,29},{6,30},{7,31},{8,16},{9,... | collective-permute-start | bytes 589832 | tf_op jit(solution)/shard_map/ppermute | solution.py:72
  16.8 9.5 %collective-permute-done.3 = bf16[4,8,3072]{2,1,0:T(8,128)(2,1)S(1)} collective-permute-done((bf16[4,8,3072]{2,1,0:T(8,128)(2,1)S(1)}, bf16[4,8,3072]{2,1,0:T(8,128)(2,1)S(1)}, u32[]{:S(2)}, u32[]{:S(2)}) %collective-permute-start.3) | collective-permute-done | bytes 196640 | tf_op jit(solution)/shard_map/ppermute | solution.py:72
  27.1 2.5 %make_copies.1 = bf16[32,144,256]{2,1,0:T(8,128)(2,1)} custom-call(f32[144,256]{1,0:T(8,128)} %x.3), custom_call_target="tpu_custom_call" | custom-call | flops 1000000 | bytes 10000 | tf_op jit(solution)/shard_map/make_copies/pallas_call | solution.py:874
  29.5 0.9 constant_dynamic-update-slice_fusion.8
  30.5 0.9 constant_dynamic-update-slice_fusion.7.held
  31.4 5.1 %all-to-all-start = ((bf16[32,144,256]{2,1,0:T(8,128)(2,1)}), bf16[32,144,256]{2,1,0:T(8,128)(2,1)S(1)}, u32[]{:S(2)}, u32[]{:S(2)}) async-start(bf16[32,144,256]{2,1,0:T(8,128)(2,1)} %make_copies.1), calls=%async_computation | async-start | bytes 4718592 | tf_op jit(solution)/shard_map/all_to_all | solution.py:98
  36.6 1.1 fusion.3
  37.6 1.0 pad_maximum_fusion
  38.9 2.4 %collective-permute-start.9 = (bf16[2,2,128,256]{3,2,1,0:T(8,128)(2,1)S(1)}, bf16[2,2,128,256]{3,2,1,0:T(8,128)(2,1)S(1)}, u32[]{:S(2)}, u32[]{:S(2)}) collective-permute-start(bf16[2,2,128,256]{3,2,1,0:T(8,128)(2,1)S(1)} %pad_maximum_fusion.1), channel_id=1, source_target_pairs={{0,28},{4,0},{8,4},{12,8},{16,12},{20,16},{24,20},{28,24},{1,29},{... | collective-permute-start | bytes 786440 | tf_op jit(solution)/shard_map/ppermute | solution.py:110
  41.4 1.2 gather_fusion
  42.6 0.6 pad.4.table
  43.2 0.6 pad_add_fusion.place
  43.8 2.8 %unpack_near.1 = (bf16[256,768]{1,0:T(8,128)(2,1)}, bf16[256,256]{1,0:T(8,128)(2,1)}, bf16[256,1024]{1,0:T(8,128)(2,1)}, bf16[1024,256]{1,0:T(8,128)(2,1)}) custom-call(s32[32]{0:T(128)} %gather_fusion, bf16[32,8,3072]{2,1,0:T(8,128)(2,1)} %constant_dynamic-update-slice_fusion.7.held), custom_call_target="tpu_custom_call" | custom-call | flops 1000000 | bytes 10000 | tf_op jit(solution)/shard_map/unpack_near/pallas_call | solution.py:857
  46.6 13.5 %attn_forward.1 = (bf16[4096,256]{1,0:T(8,128)(2,1)}, bf16[4096,256]{1,0:T(8,128)(2,1)}, bf16[4096,256]{1,0:T(8,128)(2,1)}, f32[4096,128]{1,0:T(8,128)}, bf16[40...) custom-call(s32[5]{0:T(128)} %pad_add_fusion.place, ...), custom_call_target="tpu_custom_call" | custom-call | flops 1000000 | bytes 10000 | tf_op jit(solution)/shard_map/attn_forward/pallas_call | solution.py:318
  60.1 18.7 %ffn_forward.1 = (bf16[4096,256]{1,0:T(8,128)(2,1)}, bf16[4096,256]{1,0:T(8,128)(2,1)}, f32[4096,128]{1,0:T(8,128)}, bf16[4096,1024]{1,0:T(8,128)(2,1)}, bf16[40...) custom-call(s32[5]{0:T(128)} %pad_add_fusion.place, ...), custom_call_target="tpu_custom_call" | custom-call | flops 1000000 | bytes 10000 | tf_op jit(solution)/shard_map/ffn_forward/pallas_call | solution.py:443
  78.8 0.7 copy-done.3
  79.5 16.9 %conv_weight.1 = (bf16[9,2,256,256]{3,2,1,0:T(8,128)(2,1)}, f32[8,256]{1,0:T(8,128)}) custom-call(s32[5]{0:T(128)} %pad_add_fusion.place, bf16[2,6,128,256]{3,2,1,0:T(8,128)(2,1)} %collective-permute-done.8.above, bf16[2,16,128,256]{3,2,1,0:T(8,128)(2,1)} %own.5, bf16[2,2,128,256]{3,2,1,0:T(8,128)(2,1)} %copy-done.3, ...), custom_call_target="tpu_custom_call" | custom-call | flops 20000000000 | bytes 10000000 | tf_op jit(solution)/shard_map/conv_weight/pallas_call | solution.py:977
  96.4 1.3 dynamic-slice_bitcast_fusion
  97.9 3.0 %collective-permute-done.10 = bf16[4,4,144,256]{3,2,1,0:T(8,128)(2,1)} collective-permute-done((bf16[4,4,144,256]{3,2,1,0:T(8,128)(2,1)S(1)}, bf16[4,4,144,256]{3,2,1,0:T(8,128)(2,1)}, u32[]{:S(2)}, u32[]{:S(2)}) %collective-permute-start.10) | collective-permute-done | bytes 1179680 | tf_op jit(solution)/shard_map/ppermute | solution.py:87
  100.8 3.0 %fusion = bf16[4,4,144,256]{3,2,1,0:T(8,128)(2,1)} fusion(bf16[4,4,144,256]{3,2,1,0:T(8,128)(2,1)} %collective-permute-done.10, bf16[4,2,4,144,256]{4,3,2,1,0:T(8,128)(2,1)} %bitcast.65, s32[]{:T(128)S(6)} %select_n.31), kind=kLoop, calls=%fused_computation.2 | loop fusion | flops 2359296 | bytes 3538948 | tf_op jit(solution)/shard_map/convert_element_type | solution.py:88
  103.8 1.5 collective-permute-start.11
  105.3 5.6 %all-to-all-start.2 = ((bf16[16,144,256]{2,1,0:T(8,128)(2,1)}), bf16[16,144,256]{2,1,0:T(8,128)(2,1)S(1)}, u32[]{:S(2)}, u32[]{:S(2)}) async-start(bf16[16,144,256]{2,1,0:T(8,128)(2,1)} %bitcast.63), calls=%async_computation.2 | async-start | bytes 2359296 | tf_op jit(solution)/shard_map/all_to_all | solution.py:94
  111.0 26.0 %ffn_backward.1 = (f32[4096,256]{1,0:T(8,128)}, bf16[4096,256]{1,0:T(8,128)(2,1)}, bf16[1024,256]{1,0:T(8,128)(2,1)}, bf16[256,1024]{1,0:T(8,128)(2,1)}, bf16[25...) custom-call(s32[5]{0:T(128)} %pad_add_fusion.place, bf16[2,6,128,256]{3,2,1,0:T(8,128)(2,1)} %collective-permute-done.8.above, ...), custom_call_target="tpu_custom_call" | custom-call | flops 20000000000 | bytes 10000000 | tf_op jit(solution)/shard_map/ffn_backward/pallas_call | solution.py:592
  137.0 1.1 constant_dynamic-update-slice_fusion.12
  138.1 20.3 %attn_backward.1 = (f32[2,16,128,256]{3,2,1,0:T(8,128)}, bf16[2,4,128,256]{3,2,1,0:T(8,128)(2,1)}, bf16[256,768]{1,0:T(8,128)(2,1)}, bf16[8,512]{1,0:T(8,128)(2,1)}) custom-call(bf16[4096,256]{1,0:T(8,128)(2,1)} %get-tuple-element.82.mixed, bf16[4096,768]{1,0:T(8,128)(2,1)} %get-tuple-element.83.qkv, bf16[32,512,128]{2,1,0:T(8,128)(2,1)} %get-tuple-element.84.prob, ...), custom_call_target="tpu_custom_call" | custom-call | flops 1000000 | bytes 10000 | tf_op jit(solution)/shard_map/attn_backward/pallas_call | solution.py:771
  158.5 0.7 pad_maximum_fusion.3
  159.2 1.0 constant_dynamic-update-slice_fusion.9
  160.5 2.6 %collective-permute-done.12 = bf16[4,4,8,3840]{3,2,1,0:T(8,128)(2,1)S(1)} collective-permute-done((bf16[4,4,8,3840]{3,2,1,0:T(8,128)(2,1)S(1)}, bf16[4,4,8,3840]{3,2,1,0:T(8,128)(2,1)S(1)}, u32[]{:S(2)}, u32[]{:S(2)}) %collective-permute-start.12) | collective-permute-done | bytes 983072 | tf_op jit(solution)/shard_map/ppermute | solution.py:87
  163.0 1.2 fusion.1
  164.2 7.0 %all-to-all-start.1 = ((bf16[16,8,3840]{2,1,0:T(8,128)(2,1)}), bf16[16,8,3840]{2,1,0:T(8,128)(2,1)S(1)}, u32[]{:S(2)}, u32[]{:S(2)}) async-start(bf16[16,8,3840]{2,1,0:T(8,128)(2,1)} %bitcast.24), calls=%async_computation.1 | async-start | bytes 1966080 | tf_op jit(solution)/shard_map/all_to_all | solution.py:94
  171.3 0.8 convert_reduce_fusion
  172.1 2.0 collective-permute-start.13
  174.1 8.8 %conv_data.1 = f32[2,16,128,256]{3,2,1,0:T(8,128)} custom-call(s32[5]{0:T(128)} %pad_add_fusion.place, bf16[2,6,128,256]{3,2,1,0:T(8,128)(2,1)} %collective-permute-done.8.above, bf16[2,16,128,256]{3,2,1,0:T(8,128)(2,1)} %own.5, bf16[2,2,128,256]{3,2,1,0:T(8,128)(2,1)} %copy-done.3, bf16[9,2,256,256]{3,2,1,0:T(8,128)(2,1)} %bitcast.61), custom_call_target="tpu_custom_call" | custom-call | flops 10000000000 | bytes 10000000 | tf_op jit(solution)/shard_map/conv_data/pallas_call | solution.py:977
  182.9 14.7 %conv_forward.1 = bf16[2,16,128,256]{3,2,1,0:T(8,128)(2,1)} custom-call(s32[5]{0:T(128)} %pad_add_fusion.place, bf16[2,16,128,256]{3,2,1,0:T(8,128)(2,1)} %get-tuple-element.73.sums, bf16[2,5,128,256]{3,2,1,0:T(8,128)(2,1)} %collective-permute-done.11.sums_below, bf16[2,6,128,256]{3,2,1,0:T(8,128)(2,1)} %collective-permute-done.8.above, ...), custom_call_target="tpu_custom_call" | custom-call | flops 1000000 | bytes 10000 | tf_op jit(solution)/shard_map/conv_forward/pallas_call | solution.py:1084
  197.6 1.1 convert_dynamic-update-slice_fusion
  198.8 0.6 slice.106
  199.4 0.6 fusion.5
  200.0 0.6 fusion.4
  200.7 0.6 fusion.6
  201.3 0.6 copy.40
  202.0 0.7 slice_bitcast_fusion.2
  (61 shorter events, 2.8 us)
Async XLA Ops:
  2.1 7.6 %collective-permute-start.2 = (bf16[1,8,3072]{2,1,0:T(8,128)(2,1)}, bf16[1,8,3072]{2,1,0:T(8,128)(2,1)S(1)}, u32[]{:S(2)}, u32[]{:S(2)}) collective-permute-start(bf16[1,8,3072]{2,1,0:T(8,128)(2,1)} %bitcast.68), channel_id=1, source_target_pairs={{0,3},{1,2},{2,1},{3,0},{4,7},{5,6},{6,5},{7,4},{8,11},{9,10},{10,... | collective-permute-start | bytes 147464 | tf_op jit(solution)/shard_map/ppermute | solution.py:72
  7.1 5.2 %collective-permute-start.1 = (bf16[1,8,3072]{2,1,0:T(8,128)(2,1)}, bf16[1,8,3072]{2,1,0:T(8,128)(2,1)S(1)}, u32[]{:S(2)}, u32[]{:S(2)}) collective-permute-start(bf16[1,8,3072]{2,1,0:T(8,128)(2,1)} %bitcast.69), channel_id=1, source_target_pairs={{0,2},{1,3},{2,0},{3,1},{4,6},{5,7},{6,4},{7,5},{8,10},{9,11},{10,... | collective-permute-start | bytes 147464 | tf_op jit(solution)/shard_map/ppermute | solution.py:72
  7.1 5.2 %collective-permute-start = (bf16[1,8,3072]{2,1,0:T(8,128)(2,1)}, bf16[1,8,3072]{2,1,0:T(8,128)(2,1)S(1)}, u32[]{:S(2)}, u32[]{:S(2)}) collective-permute-start(bf16[1,8,3072]{2,1,0:T(8,128)(2,1)} %bitcast.70), channel_id=1, source_target_pairs={{0,1},{1,0},{2,3},{3,2},{4,5},{5,4},{6,7},{7,6},{8,9},{9,8},{10,11... | collective-permute-start | bytes 147464 | tf_op jit(solution)/shard_map/ppermute | solution.py:72
  8.8 18.0 %collective-permute-start.6 = (bf16[2,4,128,256]{3,2,1,0:T(8,128)(2,1)S(1)}, bf16[2,4,128,256]{3,2,1,0:T(8,128)(2,1)}, u32[]{:S(2)}, u32[]{:S(2)}) collective-permute-start(bf16[2,4,128,256]{3,2,1,0:T(8,128)(2,1)S(1)} %slice.78), channel_id=1, source_target_pairs={{0,4},{4,8},{8,12},{12,16},{16,20},{20,24},{24,28},{28,0},{1,5},{5... | collective-permute-start | bytes 1572872 | tf_op jit(solution)/shard_map/ppermute | solution.py:110
  13.2 13.6 %collective-permute-start.5 = (bf16[4,8,3072]{2,1,0:T(8,128)(2,1)S(1)}, bf16[4,8,3072]{2,1,0:T(8,128)(2,1)S(1)}, u32[]{:S(2)}, u32[]{:S(2)}) collective-permute-start(bf16[4,8,3072]{2,1,0:T(8,128)(2,1)S(1)} %pad_maximum_fusion.2), channel_id=1, source_target_pairs={{0,24},{1,25},{2,26},{3,27},{4,28},{5,29},{6,30},{7,31},{8,16},{9,... | collective-permute-start | bytes 589832 | tf_op jit(solution)/shard_map/ppermute | solution.py:72
  15.7 11.1 %collective-permute-start.4 = (bf16[4,8,3072]{2,1,0:T(8,128)(2,1)S(1)}, bf16[4,8,3072]{2,1,0:T(8,128)(2,1)S(1)}, u32[]{:S(2)}, u32[]{:S(2)}) collective-permute-start(bf16[4,8,3072]{2,1,0:T(8,128)(2,1)S(1)} %pad_maximum_fusion.2), channel_id=1, source_target_pairs={{0,16},{1,17},{2,18},{3,19},{4,20},{5,21},{6,22},{7,23},{8,24},{9,... | collective-permute-start | bytes 589832 | tf_op jit(solution)/shard_map/ppermute | solution.py:72
  16.2 10.1 %collective-permute-start.3 = (bf16[4,8,3072]{2,1,0:T(8,128)(2,1)S(1)}, bf16[4,8,3072]{2,1,0:T(8,128)(2,1)S(1)}, u32[]{:S(2)}, u32[]{:S(2)}) collective-permute-start(bf16[4,8,3072]{2,1,0:T(8,128)(2,1)S(1)} %pad_maximum_fusion.2), channel_id=1, source_target_pairs={{0,8},{1,9},{2,10},{3,11},{4,12},{5,13},{6,14},{7,15},{8,0},{9,1},... | collective-permute-start | bytes 589832 | tf_op jit(solution)/shard_map/ppermute | solution.py:72
  26.8 3.6 %collective-permute-start.7 = (bf16[16,8,3072]{2,1,0:T(8,128)(2,1)S(1)}, bf16[16,8,3072]{2,1,0:T(8,128)(2,1)S(1)}, u32[]{:S(2)}, u32[]{:S(2)}) collective-permute-start(bf16[16,8,3072]{2,1,0:T(8,128)(2,1)S(1)} %constant_dynamic-update-slice_fusion), channel_id=1, source_target_pairs={{0,4},{1,5},{2,6},{3,7},{4,0},{5,1},{6,2},{7,3},{8,12},{9,13},{10,... | collective-permute-start | bytes 2359304 | tf_op jit(solution)/shard_map/ppermute | solution.py:72
  31.4 6.2 %slice-start = ((bf16[2,16,128,256]{3,2,1,0:T(8,128)(2,1)}), bf16[2,5,128,256]{3,2,1,0:T(8,128)(2,1)S(1)}, s32[]{:S(2)}) async-start(bf16[2,16,128,256]{3,2,1,0:T(8,128)(2,1)} %own.5), calls=%async_computation.3 | async-start | bytes 1310720 | tf_op jit(solution)/shard_map/slice | solution.py:1145
  31.4 73.9 %all-to-all-start = ((bf16[32,144,256]{2,1,0:T(8,128)(2,1)}), bf16[32,144,256]{2,1,0:T(8,128)(2,1)S(1)}, u32[]{:S(2)}, u32[]{:S(2)}) async-start(bf16[32,144,256]{2,1,0:T(8,128)(2,1)} %make_copies.1), calls=%async_computation | async-start | bytes 4718592 | tf_op jit(solution)/shard_map/all_to_all | solution.py:98
  36.5 2.4 %slice-start.1 = ((bf16[2,16,128,256]{3,2,1,0:T(8,128)(2,1)}), bf16[2,1,128,256]{3,2,1,0:T(8,128)(2,1)S(1)}, s32[]{:S(2)}) async-start(bf16[2,16,128,256]{3,2,1,0:T(8,128)(2,1)} %own.5), calls=%async_computation.4 | async-start | bytes 262144 | tf_op jit(solution)/shard_map/slice | solution.py:1147
  36.5 4.9 %copy-start = (s32[32]{0:T(128)S(1)}, s32[32]{0:T(128)}, u32[]{:S(2)}) copy-start(s32[32]{0:T(128)} %constant.62.clone) | copy-start | bytes 388
  36.5 6.1 %copy-start.5 = (f32[225,8]{0,1:T(8,128)S(1)}, f32[225,8]{0,1:T(8,128)}, u32[]{:S(2)}) copy-start(f32[225,8]{0,1:T(8,128)} %param.30) | copy-start | bytes 21604
  36.5 6.7 %copy-start.7 = (s32[2]{0:T(128)S(1)}, s32[2]{0:T(128)}, u32[]{:S(2)}) copy-start(s32[2]{0:T(128)} %param.26) | copy-start | bytes 28
  36.6 6.6 %copy-start.8 = (s32[2]{0:T(128)S(1)}, s32[2]{0:T(128)}, u32[]{:S(2)}) copy-start(s32[2]{0:T(128)} %param.25) | copy-start | bytes 28
  38.6 40.2 %collective-permute-start.8 = (bf16[2,6,128,256]{3,2,1,0:T(8,128)(2,1)}, bf16[2,6,128,256]{3,2,1,0:T(8,128)(2,1)}, u32[]{:S(2)}, u32[]{:S(2)}) collective-permute-start(bf16[2,6,128,256]{3,2,1,0:T(8,128)(2,1)} %pad_maximum_fusion), channel_id=1, source_target_pairs={{0,4},{4,8},{8,12},{12,16},{16,20},{20,24},{24,28},{28,0},{1,5},{5... | collective-permute-start | bytes 2359304 | tf_op jit(solution)/shard_map/ppermute | solution.py:110
  38.9 39.9 %collective-permute-start.9 = (bf16[2,2,128,256]{3,2,1,0:T(8,128)(2,1)S(1)}, bf16[2,2,128,256]{3,2,1,0:T(8,128)(2,1)S(1)}, u32[]{:S(2)}, u32[]{:S(2)}) collective-permute-start(bf16[2,2,128,256]{3,2,1,0:T(8,128)(2,1)S(1)} %pad_maximum_fusion.1), channel_id=1, source_target_pairs={{0,28},{4,0},{8,4},{12,8},{16,12},{20,16},{24,20},{28,24},{1,29},{... | collective-permute-start | bytes 786440 | tf_op jit(solution)/shard_map/ppermute | solution.py:110
  78.8 0.7 copy-start.3
  97.8 3.0 %collective-permute-start.10 = (bf16[4,4,144,256]{3,2,1,0:T(8,128)(2,1)S(1)}, bf16[4,4,144,256]{3,2,1,0:T(8,128)(2,1)}, u32[]{:S(2)}, u32[]{:S(2)}) collective-permute-start(bf16[4,4,144,256]{3,2,1,0:T(8,128)(2,1)S(1)} %dynamic-slice_bitcast_fusion), channel_id=1, source_target_pairs={{0,4},{4,0},{8,12},{12,8},{16,20},{20,16},{24,28},{28,24},{1,5},{5... | collective-permute-start | bytes 3538952 | tf_op jit(solution)/shard_map/ppermute | solution.py:87
  103.8 33.2 %collective-permute-start.11 = (bf16[2,5,128,256]{3,2,1,0:T(8,128)(2,1)}, bf16[2,5,128,256]{3,2,1,0:T(8,128)(2,1)}, u32[]{:S(2)}, u32[]{:S(2)}) collective-permute-start(bf16[2,5,128,256]{3,2,1,0:T(8,128)(2,1)} %get-tuple-element.81), channel_id=1, source_target_pairs={{0,28},{4,0},{8,4},{12,8},{16,12},{20,16},{24,20},{28,24},{1,29},{... | collective-permute-start | bytes 1966088 | tf_op jit(solution)/shard_map/ppermute | solution.py:110
  105.3 5.6 %copy-start.1 = (bf16[32,144,256]{2,1,0:T(8,128)(2,1)}, bf16[32,144,256]{2,1,0:T(8,128)(2,1)S(1)}, u32[]{:S(2)}) copy-start(bf16[32,144,256]{2,1,0:T(8,128)(2,1)S(1)} %all-to-all-done) | copy-start | bytes 7077892
  105.3 58.9 %all-to-all-start.2 = ((bf16[16,144,256]{2,1,0:T(8,128)(2,1)}), bf16[16,144,256]{2,1,0:T(8,128)(2,1)S(1)}, u32[]{:S(2)}, u32[]{:S(2)}) async-start(bf16[16,144,256]{2,1,0:T(8,128)(2,1)} %bitcast.63), calls=%async_computation.2 | async-start | bytes 2359296 | tf_op jit(solution)/shard_map/all_to_all | solution.py:94
  138.1 20.4 %copy-start.6 = (bf16[8,256]{1,0:T(8,128)(2,1)S(1)}, bf16[8,256]{1,0:T(8,128)(2,1)}, u32[]{:S(2)}) copy-start(bf16[8,256]{1,0:T(8,128)(2,1)} %get-tuple-element.91) | copy-start | bytes 12292
  138.1 21.1 %copy-start.4 = (bf16[256,256]{1,0:T(8,128)(2,1)S(1)}, bf16[256,256]{1,0:T(8,128)(2,1)}, u32[]{:S(2)}) copy-start(bf16[256,256]{1,0:T(8,128)(2,1)} %get-tuple-element.77) | copy-start | bytes 393220
  138.1 21.1 %copy-start.2 = (bf16[256,1024]{1,0:T(8,128)(2,1)S(1)}, bf16[256,1024]{1,0:T(8,128)(2,1)}, u32[]{:S(2)}) copy-start(bf16[256,1024]{1,0:T(8,128)(2,1)} %get-tuple-element.78) | copy-start | bytes 1572868
  160.4 2.6 %collective-permute-start.12 = (bf16[4,4,8,3840]{3,2,1,0:T(8,128)(2,1)S(1)}, bf16[4,4,8,3840]{3,2,1,0:T(8,128)(2,1)S(1)}, u32[]{:S(2)}, u32[]{:S(2)}) collective-permute-start(bf16[4,4,8,3840]{3,2,1,0:T(8,128)(2,1)S(1)} %dynamic-slice_bitcast_fusion.1), channel_id=1, source_target_pairs={{0,4},{4,0},{8,12},{12,8},{16,20},{20,16},{24,28},{28,24},{1,5},{5... | collective-permute-start | bytes 2949128 | tf_op jit(solution)/shard_map/ppermute | solution.py:87
  164.2 7.9 %copy-start.9 = (bf16[2,4,128,256]{3,2,1,0:T(8,128)(2,1)S(1)}, bf16[2,4,128,256]{3,2,1,0:T(8,128)(2,1)}, u32[]{:S(2)}) copy-start(bf16[2,4,128,256]{3,2,1,0:T(8,128)(2,1)} %get-tuple-element.98) | copy-start | bytes 1572868
  164.2 34.5 %all-to-all-start.1 = ((bf16[16,8,3840]{2,1,0:T(8,128)(2,1)}), bf16[16,8,3840]{2,1,0:T(8,128)(2,1)S(1)}, u32[]{:S(2)}, u32[]{:S(2)}) async-start(bf16[16,8,3840]{2,1,0:T(8,128)(2,1)} %bitcast.24), calls=%async_computation.1 | async-start | bytes 1966080 | tf_op jit(solution)/shard_map/all_to_all | solution.py:94
  172.1 25.5 %collective-permute-start.13 = (bf16[2,4,128,256]{3,2,1,0:T(8,128)(2,1)S(1)}, bf16[2,4,128,256]{3,2,1,0:T(8,128)(2,1)S(1)}, u32[]{:S(2)}, u32[]{:S(2)}) collective-permute-start(bf16[2,4,128,256]{3,2,1,0:T(8,128)(2,1)S(1)} %copy-done.9), channel_id=1, source_target_pairs={{0,28},{4,0},{8,4},{12,8},{16,12},{20,16},{24,20},{28,24},{1,29},{... | collective-permute-start | bytes 1572872 | tf_op jit(solution)/shard_map/ppermute | solution.py:110
where the time goes:
time: 204 us; the launch traced here: 203 us
  Pallas kernels  126 us (62%)
  starting transfers between devices  33.6 us (16%)
  waiting for transfers between devices  18.2 us (9%)
  local copies, waits for them, and re-layouts  14.9 us (7%)
  other arithmetic  9.33 us (5%)
    pallas_call x1, Pallas kernels, ffn_backward(): pl.pallas_call(functools.partial(ffn_backward_body, height, step_of), gri...  26 us
    pallas_call x2, Pallas kernels, conv_call(): pl.pallas_call(functools.partial(body, height), grid=(fields[0][1].shape[...  25.8 us
    pallas_call x1, Pallas kernels, attn_backward(): pl.pallas_call(functools.partial(attn_backward_body, scale, step_of), gri...  20.3 us
    pallas_call x1, Pallas kernels, ffn_forward(): pl.pallas_call(functools.partial(ffn_forward_body, height, step_of), grid...  18.7 us
    pallas_call x1, Pallas kernels, conv_forward(): pl.pallas_call(functools.partial(conv_forward_body, height), grid=(sample...  14.7 us
    pallas_call x1, Pallas kernels, attn_forward(): pl.pallas_call(functools.partial(attn_forward_body, height, scale, step_o...  13.5 us
    ppermute x7, waiting for transfers between devices, gather_steps(): lax.ppermute(held, AXES, [(i, i ^ mask) for i in range(devices)])  12.7 us
    all_to_all x2, starting transfers between devices, scatter_pairs(): lax.all_to_all(a, AXES, 0, 0, axis_index_groups=groups, tiled=True)  12.7 us
  transfers between devices with their start and end apart: 17, of which 5 were waited for; matrix products, arithmetic and copies ran while one was open for 9% of the time, Pallas kernels for 61%

commit v1 on v0

--- a/solution.py
+++ b/solution.py
@@ -15,7 +15,7 @@
 AXES = ("rows", "batch")
 BF = jnp.bfloat16
 F32 = jnp.float32
-VMEM_LIMIT = 56 * 1024 * 1024
+MIB = 1024 * 1024
 LOG2E = 1.4426950408889634
 
 
@@ -57,16 +57,19 @@
     return groups + [row_bits[:1]]
 
 
-def gather_steps(x, other):
+def gather_steps(x, beside):
     devices = device_count()
     held = x[None]
     places = [0]
-    for group in bit_groups():
+    groups = bit_groups()
+    for k, group in enumerate(groups):
         masks = [0]
         for bit in group:
             masks = masks + [m | bit for m in masks]
-        if group == bit_groups()[-1]:
-            held = after(held, other)
+        if k == 1:
+            other = beside(held)
+        if k == len(groups) - 1:
+            held = after(held, *other)
         pieces = [held]
         for mask in masks[1:]:
             pieces.append(lax.ppermute(held, AXES, [(i, i ^ mask) for i in range(devices)]))
@@ -75,7 +78,7 @@
     order = np.zeros(devices, np.int32)
     for place, mask in enumerate(places):
         order[mask] = place
-    return held, jnp.asarray(order)[jnp.arange(devices) ^ device_index()]
+    return held, jnp.asarray(order)[jnp.arange(devices) ^ device_index()], other
 
 
 def scatter_pairs(x):
@@ -280,6 +283,10 @@
     lax.fori_loop(0, columns // 16, mix, 0, unroll=8)
 
 
+def near(*arrays):
+    return [pltpu.with_memory_space_constraint(a, pltpu.VMEM) for a in arrays]
+
+
 def const_spec(shape):
     return pl.BlockSpec(shape, lambda *_: (0,) * len(shape))
 
@@ -287,8 +294,12 @@
 SMALL_COST = pl.CostEstimate(flops=10**6, bytes_accessed=10**4, transcendentals=0)
 
 
-def params():
-    return pltpu.CompilerParams(vmem_limit_bytes=VMEM_LIMIT)
+def params(mib):
+    return pltpu.CompilerParams(vmem_limit_bytes=mib * MIB)
+
+
+def far(*arrays):
+    return [pltpu.with_memory_space_constraint(a, pltpu.HBM) for a in arrays]
 
 
 SMEM_SPEC = pl.BlockSpec(memory_space=pltpu.SMEM)
@@ -345,22 +356,22 @@
             pl.BlockSpec((tokens, width), row_block),
         ],
         out_shape=[
-            jax.ShapeDtypeStruct((total, width), BF),
-            jax.ShapeDtypeStruct((total, width), BF),
-            jax.ShapeDtypeStruct((total, width), BF),
-            jax.ShapeDtypeStruct((total, 128), F32),
-            jax.ShapeDtypeStruct((total, 3 * width), BF),
-            jax.ShapeDtypeStruct((total // 128, 512, 128), BF),
-            jax.ShapeDtypeStruct((total, width), BF),
+            pltpu.VMEM((total, width), BF),
+            pltpu.HBM((total, width), BF),
+            pltpu.HBM((total, width), BF),
+            pltpu.HBM((total, 128), F32),
+            pltpu.HBM((total, 3 * width), BF),
+            pltpu.HBM((total // 128, 512, 128), BF),
+            pltpu.VMEM((total, width), BF),
         ],
         scratch_shapes=[
             pltpu.VMEM((columns // WIN, WIN, WIN, width), F32),
             pltpu.VMEM((512, 128), F32),
         ],
-        compiler_params=params(),
+        compiler_params=params(24),
         cost_estimate=SMALL_COST,
         name="attn_forward",
-    )(place, above, own, own, gain, shift, weight, table, places, mask)
+    )(place, *far(above, own, own, gain, shift), *near(weight), *far(table, places, mask))
 
 
 def gelu_parts(x):
@@ -451,16 +462,19 @@
             pl.BlockSpec((1, WIN, columns, width), lambda s: (*step_of(s), 0, 0)),
             pl.BlockSpec((1, WIN // 2 + 1, columns, width), lambda s: (step_of(s)[0], 0, 0, 0)),
         ],
-        out_shape=[jax.ShapeDtypeStruct((total, n), t) for n, t in zip(rows, types)]
+        out_shape=[pltpu.HBM((total, n), t) for n, t in zip(rows, types)]
         + [
-            jax.ShapeDtypeStruct(shape, BF),
+            pltpu.VMEM(shape, BF),
             jax.ShapeDtypeStruct((samples, WIN // 2 + 1, columns, width), BF),
         ],
         scratch_shapes=[pltpu.VMEM((columns // WIN, WIN, WIN, width), F32)],
-        compiler_params=params(),
+        compiler_params=params(32),
         cost_estimate=SMALL_COST,
         name="ffn_forward",
-    )(place, x, mix, out_w, out_b, gain, shift, up_w, up_b, down_w, down_b)
+    )(
+        place, *near(x, mix, out_w), *far(out_b, gain, shift), *near(up_w), *far(up_b), *near(down_w),
+        *far(down_b),
+    )
 
 
 def column_sum(x):
@@ -490,23 +504,30 @@
     start = place[0] + half
     not_first = start != 0
     lanes = (0, 256, 512)
-
-    @pl.when(band == 0)
-    def _():
-        before = jnp.where(not_first, start, height) - half - 1
-        put_rows(above, half + 1, 0, sample, place, before, taps, 0, lanes)
-        put_taps(own[0, 0], row_limit(place, sample, start, not_first), taps, half + 1, lanes)
-        limit = row_limit(place, sample, start - 1, not_first)
-        put_taps(above[0, ABOVE_LAST], limit, taps, half + 2, lanes)
-        put_rows(own, half + 1, 0, sample, place, start, taps, half + 3, lanes)
-
-    @pl.when(band > 0)
-    def _():
-        for group in range(2):
-            first = band * WIN + (group - 1) * half - 1
-            put_rows(own, half + 2, first, sample, place, start + first, taps, group * (half + 2), lanes)
-
+    top = band == 0
+    before = jnp.where(top, jnp.where(not_first, start, height), start + band * WIN) - half - 1
+
+    def put_group(group):
+        for k in range(half + 2):
+            row = before + k if group == 0 else start + band * WIN + k - 1
+            at = band * WIN + (group - 1) * half - 1 + k
+            source = own[0, jnp.maximum(at, 0)]
+            allowed = True
+            if group == 0 and k <= half:
+                source = jnp.where(top, above[0, k], source)
+            elif group == 0:
+                row = start + band * WIN
+                allowed = ~top | not_first
+            elif k == 0:
+                source = jnp.where(top, above[0, ABOVE_LAST], source)
+                allowed = ~top | not_first
+            limit = row_limit(place, sample, row, allowed)
+            put_taps(source, limit, taps, group * (half + 2) + k, lanes)
+
+    put_group(0)
     for group in range(2):
+        if group == 0:
+            put_group(1)
         total = 0.0
         for a in range(3):
             at = group * (half + 2) + 2 - a
@@ -609,11 +630,11 @@
             const_spec((8, width)),
         ],
         out_shape=[
-            jax.ShapeDtypeStruct((total, width), F32),
-            jax.ShapeDtypeStruct((total, width), BF),
-            jax.ShapeDtypeStruct((hidden, width), BF),
-            jax.ShapeDtypeStruct((width, hidden), BF),
-            jax.ShapeDtypeStruct((width, width), BF),
+            pltpu.VMEM((total, width), F32),
+            pltpu.VMEM((total, width), BF),
+            pltpu.HBM((hidden, width), BF),
+            pltpu.HBM((width, hidden), BF),
+            pltpu.HBM((width, width), BF),
             jax.ShapeDtypeStruct((8, width), BF),
         ],
         scratch_shapes=[
@@ -628,12 +649,15 @@
             pltpu.VMEM((width, width), F32),
             pltpu.VMEM((8, width), F32),
         ],
-        compiler_params=params(),
+        compiler_params=params(44),
         cost_estimate=pl.CostEstimate(
             flops=2 * 10**10, bytes_accessed=10**7, transcendentals=0
         ),
         name="ffn_backward",
-    )(place, above, own, *rows, conv_w, out_w, gain, up_w, down_w)
+    )(
+        place, *far(above, own, *rows[:5]), *near(mix), *far(conv_w), *near(out_w), *far(gain),
+        *near(up_w, down_w),
+    )
 
 
 def attn_backward_body(
@@ -792,17 +816,19 @@
             pltpu.VMEM((columns // 16, 512, 128), BF),
             pltpu.VMEM((columns // WIN, WIN, WIN, width), F32),
         ],
-        compiler_params=params(),
+        compiler_params=params(32),
         cost_estimate=SMALL_COST,
         name="attn_backward",
-    )(*rows, *consts)
-
-
-def shifted(row, column, by):
+    )(*near(mixed), *far(*rows[1:6]), *near(first, weight), *far(*consts[1:]))
+
+
+def shifted(row, by):
     columns = row.shape[0]
     moved = pltpu.roll(row, by % columns, 0)
-    edge = 0 if by == 1 else columns - 1
-    return jnp.where(column == edge, 0.0, moved)
+    place = iota((8, 1), 0)
+    if by == 1:
+        return jnp.concatenate([jnp.where(place == 0, 0.0, moved[:8]), moved[8:]], 0)
+    return jnp.concatenate([moved[:-8], jnp.where(place == 7, 0.0, moved[-8:])], 0)
 
 
 def pack_near_body(qkv, out_w, up, down, near):
@@ -822,10 +848,10 @@
     return pl.pallas_call(
         pack_near_body,
         out_shape=jax.ShapeDtypeStruct((rows, lanes), BF),
-        compiler_params=params(),
+        compiler_params=params(16),
         cost_estimate=SMALL_COST,
         name="pack_near",
-    )(qkv, out_w, up, down)
+    )(*far(qkv, out_w, up, down))
 
 
 def unpack_near_body(order, held, qkv, out_w, up, down):
@@ -857,11 +883,36 @@
     return pl.pallas_call(
         unpack_near_body,
         in_specs=[SMEM_SPEC, pl.BlockSpec(memory_space=pltpu.VMEM)],
-        out_shape=[jax.ShapeDtypeStruct((devices * w.shape[0], w.shape[1]), BF) for w in weights],
-        compiler_params=params(),
+        out_shape=[pltpu.VMEM((devices * w.shape[0], w.shape[1]), BF) for w in weights],
+        compiler_params=params(24),
         cost_estimate=SMALL_COST,
         name="unpack_near",
     )(order, held)
+
+
+def last_sums_body(parts, down, out_w, up, qkv, vec):
+    count, rows, _ = parts.shape
+    total = parts[0].astype(F32)
+    for k in range(1, count):
+        total = total + parts[k].astype(F32)
+    width = down.shape[1]
+    for k in range(down.shape[0] // rows):
+        down[k * rows : (k + 1) * rows] = total[:, k * width : (k + 1) * width]
+    at = down.size // rows
+    for ref in (out_w, up, qkv, vec):
+        ref[...] = total[:, at : at + ref.shape[1]]
+        at += ref.shape[1]
+
+
+def last_sums(parts, down, rest):
+    shapes = (down, *rest)
+    return pl.pallas_call(
+        last_sums_body,
+        out_shape=[jax.ShapeDtypeStruct(a, F32) for a in shapes],
+        compiler_params=params(24),
+        cost_estimate=SMALL_COST,
+        name="last_sums",
+    )(parts)
 
 
 def copies_body(x, out):
@@ -874,10 +925,10 @@
     return pl.pallas_call(
         copies_body,
         out_shape=jax.ShapeDtypeStruct((count,) + x.shape, BF),
-        compiler_params=params(),
+        compiler_params=params(16),
         cost_estimate=SMALL_COST,
         name="make_copies",
-    )(x)
+    )(*far(x))
 
 
 def row_limit(place, sample, row, allowed=True):
@@ -887,17 +938,9 @@
 def put_taps(row, limit, target, at, lanes):
     column = iota((row.shape[0], 1), 0)
     wide = jnp.where(column < limit, row.astype(F32), 0.0)
-    target[at, :, lanes[0] : lanes[0] + 256] = shifted(wide, column, -1).astype(BF)
+    target[at, :, lanes[0] : lanes[0] + 256] = shifted(wide, -1).astype(BF)
     target[at, :, lanes[1] : lanes[1] + 256] = wide.astype(BF)
-    target[at, :, lanes[2] : lanes[2] + 256] = shifted(wide, column, 1).astype(BF)
-
-
-def put_rows(source, count, first, sample, place, row, target, at, lanes):
-    def one(r, _):
-        put_taps(source[0, first + r], row_limit(place, sample, row + r), target, at + r, lanes)
-        return 0
-
-    lax.fori_loop(0, count, one, 0, unroll=True)
+    target[at, :, lanes[2] : lanes[2] + 256] = shifted(wide, 1).astype(BF)
 
 
 ABOVE_LAST = WIN // 2
@@ -908,21 +951,19 @@
     sample = pl.program_id(0)
     rows = own.shape[1]
     start = place[0] + WIN // 2
-    lanes = (0, 256, 512)
-    limit = row_limit(place, sample, start - 1, start != 0)
-    put_taps(above[0, ABOVE_LAST], limit, taps, at, lanes)
-    put_rows(own, rows, 0, sample, place, start, taps, at + 1, lanes)
-    limit = row_limit(place, sample, start + rows, start + rows != height)
-    put_taps(below[0, 0], limit, taps, at + rows + 1, lanes)
-
-
-def weight_sums(groups, source, taps, acc):
-    columns = taps.shape[1]
-    for start, target, rows in groups:
-        turned = source(target, rows).T
-        for a in range(3):
-            piece = taps[start + 2 - a : start + 2 - a + rows].reshape(rows * columns, 768)
-            acc[a] += dot(turned, piece)
+
+    def put(r):
+        allowed = True
+        if r == 0:
+            source, allowed = above[0, ABOVE_LAST], start != 0
+        elif r <= rows:
+            source = own[0, r - 1]
+        else:
+            source, allowed = below[0, 0], start + rows != height
+        limit = row_limit(place, sample, start + r - 1, allowed)
+        put_taps(source, limit, taps, at + r, (0, 256, 512))
+
+    return put
 
 
 def conv_weight_body(
@@ -942,22 +983,33 @@
     not_first = start != 0
 
     before = jnp.where(not_first, start, height) - half - 1
-    put_rows(above, half + 1, 0, sample, place, before, taps, 0, (0, 256, 512))
+    put = own_taps(height, place, above, own, below, taps, half + 2)
+    for r in range(half + 1):
+        limit = row_limit(place, sample, before + r)
+        put_taps(above[0, r], limit, taps, r, (0, 256, 512))
     limit = row_limit(place, sample, start, not_first)
     put_taps(own[0, 0], limit, taps, half + 1, (0, 256, 512))
-    own_taps(height, place, above, own, below, taps, half + 2)
-
-    def one(r, _):
-        limit = row_limit(place, sample, start + r)
-        held[r] = jnp.where(column < limit, hidden[0, r].astype(F32), 0.0).astype(BF)
-        vec[0:1] += jnp.sum(taps[half + 3 + r, :, 256:512].astype(F32), 0, keepdims=True)
-        return 0
-
-    lax.fori_loop(0, rows, one, 0, unroll=4)
-    groups = ((0, 0, half), (half + 2, half, rows - half))
-    weight_sums(groups, lambda t, n: sums[0, t : t + n].reshape(n * columns, 256), taps, acc)
-    groups = ((half + 2, 0, rows),)
-    weight_sums(groups, lambda t, n: held[t : t + n].reshape(n * columns, 256), taps, acc_hidden)
+
+    def add(source, first, acc):
+        count = source.shape[0]
+        turned = source.reshape(count * columns, 256).T
+        for a in range(3):
+            piece = taps[first + 2 - a : first + 2 - a + count].reshape(count * columns, 768)
+            acc[a] += dot(turned, piece)
+
+    put(0)
+    put(1)
+    add(sums[0, :half], 0, acc)
+    step = 8
+    for r in range(0, rows, step):
+        for k in range(r, r + step):
+            put(k + 2)
+            limit = row_limit(place, sample, start + k)
+            held[k] = jnp.where(column < limit, hidden[0, k].astype(F32), 0.0).astype(BF)
+            vec[0:1] += jnp.sum(taps[half + 3 + k, :, 256:512].astype(F32), 0, keepdims=True)
+        add(held[r : r + step], half + 2 + r, acc_hidden)
+        last = min(r + step, rows - half)
+        add(sums[0, half + r : half + last], half + 2 + r, acc)
 
     @pl.when(sample == pl.num_programs(0) - 1)
     def _():
@@ -972,7 +1024,7 @@
 
 
 def conv_call(
-    body, name, place, fields, consts, height, out_specs, out_shape, scratch, cost=None
+    body, name, mib, place, fields, consts, height, out_specs, out_shape, scratch, cost=None
 ):
     return pl.pallas_call(
         functools.partial(body, height),
@@ -981,14 +1033,14 @@
         out_specs=out_specs,
         out_shape=out_shape,
         scratch_shapes=scratch,
-        compiler_params=params(),
+        compiler_params=params(mib),
         cost_estimate=cost or SMALL_COST,
         name=name,
-    )(place, *[a for _, a in fields], *[a for _, a in consts])
+    )(place, *[a for _, a in fields], *far(*[a for _, a in consts]))
 
 
 def whole(a):
-    return field_spec(a), a
+    return field_spec(a), far(a)[0]
 
 
 def conv_weight(place, grads, sums, hidden, height):
@@ -996,7 +1048,7 @@
     shape = (9, 2, width, width)
     acc = pltpu.VMEM((3, width, 3 * width), F32)
     return conv_call(
-        conv_weight_body, "conv_weight", place, [whole(a) for a in (*grads, sums, hidden)], (),
+        conv_weight_body, "conv_weight", 34, place, [*map(whole, grads), (field_spec(sums), near(sums)[0]), whole(hidden)], (),
         height, [const_spec(shape), const_spec((8, width))],
         [jax.ShapeDtypeStruct(shape, BF), jax.ShapeDtypeStruct((8, width), F32)],
         [
@@ -1020,8 +1072,12 @@
             at = 256 * (k % 3)
             turned[k // 3, :, at : at + 256] = weight[k, 0]
 
-    own_taps(height, place, above, own, below, taps, 0)
+    put = own_taps(height, place, above, own, below, taps, 0)
+    for r in range(2):
+        put(r)
     for r in range(0, own.shape[1], 4):
+        for k in range(r + 2, r + 6):
+            put(k)
         total = 0.0
         for a in range(3):
             piece = taps[r + 2 - a : r + 6 - a].reshape(4 * columns, 768)
@@ -1037,7 +1093,7 @@
     width = own.shape[-1]
     weight_spec = pl.BlockSpec((9, 1, width, width), lambda s: (0, 1, 0, 0))
     return conv_call(
-        conv_data_body, "conv_data", place, [whole(a) for a in grads], ((weight_spec, weight),),
+        conv_data_body, "conv_data", 28, place, [whole(a) for a in grads], ((weight_spec, weight),),
         height, field_spec(own), jax.ShapeDtypeStruct(own.shape, F32),
         [
             pltpu.VMEM((own.shape[1] + 2, own.shape[2], 3 * width), BF),
@@ -1056,18 +1112,28 @@
     half = WIN // 2
     start = place[0] + half
     not_first, not_last = start != 0, start + rows != height
-    lanes = (1024, 512, 0)
-    limit = row_limit(place, sample, start - 1, not_first)
-    put_taps(sums[0, half - 1], limit, taps, 0, lanes)
-    put_rows(sums, rows - half, half, sample, place, start, taps, 1, lanes)
-    put_rows(sums_below, half, 0, sample, place, start + rows - half, taps, rows - half + 1, lanes)
-    after = row_limit(place, sample, start + rows, not_last)
-    put_taps(sums_below[0, half], after, taps, rows + 1, lanes)
-    lanes = (1280, 768, 256)
-    put_taps(above[0, ABOVE_HIDDEN], limit, taps, 0, lanes)
-    put_rows(hidden, rows, 0, sample, place, start, taps, 1, lanes)
-    put_taps(below[0, 1], after, taps, rows + 1, lanes)
+
+    def put(r):
+        allowed = True
+        if r == 0:
+            first, second, allowed = sums[0, half - 1], above[0, ABOVE_HIDDEN], not_first
+        elif r <= rows:
+            first, second = None, hidden[0, r - 1]
+            if r <= rows - half:
+                first = sums[0, half + r - 1]
+            else:
+                first = sums_below[0, r - 1 - rows + half]
+        else:
+            first, second, allowed = sums_below[0, half], below[0, 1], not_last
+        limit = row_limit(place, sample, start + r - 1, allowed)
+        put_taps(first, limit, taps, r, (1024, 512, 0))
+        put_taps(second, limit, taps, r, (1280, 768, 256))
+
+    for r in range(2):
+        put(r)
     for r in range(0, rows, 4):
+        for k in range(r + 2, r + 6):
+            put(k)
         total = bias[...]
         for a in range(3):
             piece = taps[r + a : r + a + 4].reshape(4 * columns, 1536)
@@ -1080,7 +1146,7 @@
 
 def conv_forward(place, sums, sums_below, hidden, weight, bias, height):
     samples, rows, columns, width = sums.shape
-    fields = (sums, sums_below, *hidden)
+    fields = (*near(sums), *far(sums_below, *hidden))
     return pl.pallas_call(
         functools.partial(conv_forward_body, height),
         grid=(samples,),
@@ -1090,10 +1156,10 @@
         out_specs=field_spec(sums),
         out_shape=jax.ShapeDtypeStruct(sums.shape, BF),
         scratch_shapes=[pltpu.VMEM((rows + 2, columns, 6 * width), BF)],
-        compiler_params=params(),
+        compiler_params=params(32),
         cost_estimate=SMALL_COST,
         name="conv_forward",
-    )(place, *fields, weight, bias)
+    )(place, *fields, *far(weight, bias))
 
 
 def shards(
@@ -1138,23 +1204,27 @@
 
     input_above = ring(layer_input[:, grid_rows - half :], 1)
     rows_out, rows_down = output_weight.shape[0], down_weight.shape[0]
-    near = pack_near(qkv_weight, output_weight, up_weight, down_weight)
-    held, order = gather_steps(near, input_above)
-    late_cotangent, late_hidden = after((cotangent, hidden_state), held)
-    halo_above = jnp.concatenate(
-        [late_cotangent[:, grid_rows - half - 1 :], late_hidden[:, grid_rows - 1 :]], 1
-    )
-    halo_below = jnp.concatenate([late_cotangent[:, :1], late_hidden[:, :1]], 1)
+    weights = pack_near(qkv_weight, output_weight, up_weight, down_weight)
+    offsets = bias_table.shape[0]
+
+    def beside(held):
+        grad, hidden, weight, table = after(
+            (cotangent, hidden_state, conv_weight_in, bias_table), held
+        )
+        halo_above = jnp.concatenate([grad[:, grid_rows - half - 1 :], hidden[:, grid_rows - 1 :]], 1)
+        halo_below = jnp.concatenate([grad[:, :1], hidden[:, :1]], 1)
+        table = jnp.pad(table.T, ((0, 0), (0, 256 - offsets)))
+        return halo_above, halo_below, make_copies(weight, devices), table, input_above, place
+
+    held, order, (halo_above, halo_below, conv_copies, table, *_) = gather_steps(weights, beside)
+    halo_above, halo_below, conv_copies = after((halo_above, halo_below, conv_copies), held)
     halo_above, halo_below = ring(halo_above, 1), ring(halo_below, -1)
     grads = (halo_above, cotangent, halo_below)
-    conv_copies = after(make_copies(conv_weight_in, devices), held, input_above)
     conv_full = gather_copies(conv_copies).reshape(-1, width)
 
     qkv_full, output_full, up_full, down_full = unpack_near(
         order, held, (qkv_weight, output_weight, up_weight, down_weight)
     )
-    offsets = bias_table.shape[0]
-    table = jnp.pad(bias_table.T, ((0, 0), (0, 256 - offsets)))
     mask = jnp.asarray(head_mask(), BF)
 
     x, normed, xhat, rstd, qkv, prob, mix = attn_forward(
@@ -1178,6 +1248,7 @@
         after(mixed, sums_below), qkv, prob, normed, xhat, rstd, first_grad, qkv_full,
         vec(first_gain), mask, conv_bias_part, jnp.asarray(offset_places(True), BF).T, scale, shape,
     )
+    down_acc, up_acc, out_acc, vec_ffn = after((down_acc, up_acc, out_acc, vec_ffn), qkv_acc)
     down_local = down_acc.reshape(devices, -1, rows_out, width).transpose(0, 2, 1, 3)
     parts = [
         down_local.reshape(devices, rows_out, -1),
@@ -1202,13 +1273,15 @@
         return jnp.sum(parts.astype(F32), 0)
 
     conv_weight_grad = total(conv_all)
-    ends = np.cumsum([0, hidden_width, width, hidden_width, 3 * width])
-    sums_all = total(last_all)
-    parts = [sums_all[:, ends[k] : ends[k + 1]] for k in range(4)]
-    down_weight_grad = parts[0].reshape(rows_out, -1, width).transpose(1, 0, 2)
-    down_weight_grad = down_weight_grad.reshape(rows_down, width)
-    output_weight_grad, up_weight_grad, qkv_weight_grad = parts[1:]
-    vectors = sums_all[:, ends[4] :].reshape(8, 3, width)
+    down_weight_grad, output_weight_grad, up_weight_grad, qkv_weight_grad, vectors = last_sums(
+        last_all,
+        (rows_down, width),
+        [
+            (rows_out, width), (rows_out, hidden_width), (rows_out, 3 * width),
+            (rows_out, 24 * width // rows_out),
+        ],
+    )
+    vectors = vectors.reshape(8, 3, width)
     ffn_vec, table_grad, attn_vec = (vectors[:, k] for k in range(3))
     down_bias_grad, second_gain_grad, second_shift_grad, output_bias_grad = (
         ffn_vec[k] for k in range(4)

time: 204 us -> 187 us (0.917)
  Pallas kernels: 126 us -> 115 us
  local copies, waits for them, and re-layouts: 14.9 us -> 9.62 us
    pallas_call x2, Pallas kernels: 25.8 us -> 22.3 us  [conv_call(): pl.pallas_call(functools.partial(body, height), grid=(fields[0][1].shape[...]
    ppermute x7, waiting for transfers between devices: 12.7 us -> 9.78 us  [gather_steps(): lax.ppermute(held, AXES, [(i, i ^ mask) for i in range(devices)])]
    unnamed x34 -> x40, local copies, waits for them, and re-layouts: 5.4 us -> 3.02 us
    pallas_call x1, Pallas kernels: 26 us -> 23.8 us  [ffn_backward(): pl.pallas_call(functools.partial(ffn_backward_body, height, step_of), gri...]
    ppermute x5, waiting for transfers between devices: 0.01 us -> 2.14 us  [ring(): lax.ppermute(x, 'rows', [(i, (i + by) % devices) for i in range(devices)])]
  transfers between devices with their start and end apart: 17 -> 17, of which waited for: 5 -> 7; matrix products, arithmetic and copies ran while one was open for 9% -> 8% of each run, Pallas kernels for 61% -> 61%
where the time goes in v1:
time: 187 us; the launch traced here: 186 us
  Pallas kernels  115 us (61%)
  starting transfers between devices  33.3 us (18%)
  waiting for transfers between devices  17.7 us (9%)
  local copies, waits for them, and re-layouts  9.62 us (5%)
  other arithmetic  9.43 us (5%)
    pallas_call x1, Pallas kernels, ffn_backward(): pl.pallas_call(functools.partial(ffn_backward_body, height, step_of), gri...  23.8 us
    pallas_call x2, Pallas kernels, conv_call(): pl.pallas_call(functools.partial(body, height), grid=(fields[0][1].shape[...  22.3 us
    pallas_call x1, Pallas kernels, attn_backward(): pl.pallas_call(functools.partial(attn_backward_body, scale, step_of), gri...  19.2 us
    pallas_call x1, Pallas kernels, ffn_forward(): pl.pallas_call(functools.partial(ffn_forward_body, height, step_of), grid...  17.9 us
    pallas_call x1, Pallas kernels, conv_forward(): pl.pallas_call(functools.partial(conv_forward_body, height), grid=(sample...  13.9 us
    all_to_all x2, starting transfers between devices, scatter_pairs(): lax.all_to_all(a, AXES, 0, 0, axis_index_groups=groups, tiled=True)  13.7 us
    pallas_call x1, Pallas kernels, attn_forward(): pl.pallas_call(functools.partial(attn_forward_body, height, scale, step_o...  13.4 us
    ppermute x7, waiting for transfers between devices, gather_steps(): lax.ppermute(held, AXES, [(i, i ^ mask) for i in range(devices)])  9.78 us
  transfers between devices with their start and end apart: 17, of which 7 were waited for; matrix products, arithmetic and copies ran while one was open for 8% of the time, Pallas kernels for 61%

profile of v1, /device:TPU:0, one launch (start us, length us, event | category | flops | bytes accessed | tf_op | source)
XLA Modules:
  0.0 186.4 jit_solution(10206214972466117286)
XLA Ops:
  0.7 0.8 pack_near.1
  1.5 5.1 %collective-permute-start.2 = (bf16[1,8,3072]{2,1,0:T(8,128)(2,1)S(1)}, bf16[1,8,3072]{2,1,0:T(8,128)(2,1)S(1)}, u32[]{:S(2)}, u32[]{:S(2)}) collective-permute-start(bf16[1,8,3072]{2,1,0:T(8,128)(2,1)S(1)} %bitcast.56), channel_id=1, source_target_pairs={{0,3},{1,2},{2,1},{3,0},{4,7},{5,6},{6,5},{7,4},{8,11},{9,10},{10,... | collective-permute-start | bytes 147464 | tf_op jit(solution)/shard_map/ppermute | solution.py:75
  6.6 0.6 collective-permute-start
  7.2 1.1 slice.67
  8.4 0.7 pad_add_fusion.place
  9.1 2.4 %collective-permute-done.1 = bf16[1,8,3072]{2,1,0:T(8,128)(2,1)S(1)} collective-permute-done((bf16[1,8,3072]{2,1,0:T(8,128)(2,1)S(1)}, bf16[1,8,3072]{2,1,0:T(8,128)(2,1)S(1)}, u32[]{:S(2)}, u32[]{:S(2)}) %collective-permute-start.1) | collective-permute-done | bytes 49184 | tf_op jit(solution)/shard_map/ppermute | solution.py:75
  11.6 2.5 %collective-permute-start.5 = (bf16[4,8,3072]{2,1,0:T(8,128)(2,1)S(1)}, bf16[4,8,3072]{2,1,0:T(8,128)(2,1)S(1)}, u32[]{:S(2)}, u32[]{:S(2)}) collective-permute-start(bf16[4,8,3072]{2,1,0:T(8,128)(2,1)S(1)} %pad_maximum_fusion.2), channel_id=1, source_target_pairs={{0,24},{1,25},{2,26},{3,27},{4,28},{5,29},{6,30},{7,31},{8,16},{9,... | collective-permute-start | bytes 589832 | tf_op jit(solution)/shard_map/ppermute | solution.py:75
  14.1 0.5 collective-permute-start.4
  14.6 0.5 collective-permute-start.3
  15.2 1.1 fusion.3
  16.2 2.5 %make_copies.1 = bf16[32,144,256]{2,1,0:T(8,128)(2,1)} custom-call(f32[144,256]{1,0:T(8,128)} %x.2), custom_call_target="tpu_custom_call" | custom-call | flops 1000000 | bytes 10000 | tf_op jit(solution)/shard_map/make_copies/pallas_call | solution.py:925
  18.7 0.6 pad.4.table
  19.3 0.7 pad_maximum_fusion.1
  20.0 0.9 pad_maximum_fusion
  21.0 3.7 %collective-permute-done.3 = bf16[4,8,3072]{2,1,0:T(8,128)(2,1)S(1)} collective-permute-done((bf16[4,8,3072]{2,1,0:T(8,128)(2,1)S(1)}, bf16[4,8,3072]{2,1,0:T(8,128)(2,1)S(1)}, u32[]{:S(2)}, u32[]{:S(2)}) %collective-permute-start.3) | collective-permute-done | bytes 196640 | tf_op jit(solution)/shard_map/ppermute | solution.py:75
  24.7 1.5 collective-permute-done.4
  26.6 2.1 %collective-permute-done.7 = bf16[16,8,3072]{2,1,0:T(8,128)(2,1)S(1)} collective-permute-done((bf16[16,8,3072]{2,1,0:T(8,128)(2,1)S(1)}, bf16[16,8,3072]{2,1,0:T(8,128)(2,1)S(1)}, u32[]{:S(2)}, u32[]{:S(2)}) %collective-permute-start.7) | collective-permute-done | bytes 786464 | tf_op jit(solution)/shard_map/ppermute | solution.py:75
  28.8 5.2 %all-to-all-start = ((bf16[32,144,256]{2,1,0:T(8,128)(2,1)}), bf16[32,144,256]{2,1,0:T(8,128)(2,1)}, u32[]{:S(2)}, u32[]{:S(2)}) async-start(bf16[32,144,256]{2,1,0:T(8,128)(2,1)} %make_copies.1), calls=%async_computation | async-start | bytes 4718592 | tf_op jit(solution)/shard_map/all_to_all | solution.py:101
  34.0 0.2 collective-permute-start.8
  34.2 2.5 %collective-permute-start.9 = (bf16[2,2,128,256]{3,2,1,0:T(8,128)(2,1)}, bf16[2,2,128,256]{3,2,1,0:T(8,128)(2,1)}, u32[]{:S(2)}, u32[]{:S(2)}) collective-permute-start(bf16[2,2,128,256]{3,2,1,0:T(8,128)(2,1)} %pad_maximum_fusion.1), channel_id=1, source_target_pairs={{0,28},{4,0},{8,4},{12,8},{16,12},{20,16},{24,20},{28,24},{1,29},{... | collective-permute-start | bytes 786440 | tf_op jit(solution)/shard_map/ppermute | solution.py:113
  36.7 0.7 gather_fusion
  37.4 0.8 unpack_near.1
  38.2 13.4 %attn_forward.1 = (bf16[4096,256]{1,0:T(8,128)(2,1)S(1)}, bf16[4096,256]{1,0:T(8,128)(2,1)}, bf16[4096,256]{1,0:T(8,128)(2,1)}, f32[4096,128]{1,0:T(8,128)}, bf1...) custom-call(s32[5]{0:T(128)S(1)} %pad_add_fusion.place, ...), custom_call_target="tpu_custom_call" | custom-call | flops 1000000 | bytes 10000 | tf_op jit(solution)/shard_map/attn_forward/pallas_call | solution.py:329
  51.6 17.9 %ffn_forward.1 = (bf16[4096,256]{1,0:T(8,128)(2,1)}, bf16[4096,256]{1,0:T(8,128)(2,1)}, f32[4096,128]{1,0:T(8,128)}, bf16[4096,1024]{1,0:T(8,128)(2,1)}, bf16[40...) custom-call(s32[5]{0:T(128)S(1)} %pad_add_fusion.place, ...), custom_call_target="tpu_custom_call" | custom-call | flops 1000000 | bytes 10000 | tf_op jit(solution)/shard_map/ffn_forward/pallas_call | solution.py:454
  69.6 2.1 %collective-permute-done.8.above = bf16[2,6,128,256]{3,2,1,0:T(8,128)(2,1)} collective-permute-done((bf16[2,6,128,256]{3,2,1,0:T(8,128)(2,1)S(1)}, bf16[2,6,128,256]{3,2,1,0:T(8,128)(2,1)}, u32[]{:S(2)}, u32[]{:S(2)}) %collective-permute-start.8) | collective-permute-done | bytes 786464 | tf_op jit(solution)/shard_map/ppermute | solution.py:113
  71.7 13.4 %conv_weight.1 = (bf16[9,2,256,256]{3,2,1,0:T(8,128)(2,1)S(1)}, f32[8,256]{1,0:T(8,128)S(1)}) custom-call(s32[5]{0:T(128)S(1)} %pad_add_fusion.place, bf16[2,6,128,256]{3,2,1,0:T(8,128)(2,1)} %collective-permute-done.8.above, bf16[2,16,128,256]{3,2,1,0:T(8,128)(2,1)} %own.5, bf16[2,2,128,256]{3,2,1,0:T(8,128)(2,1)} %collective-permute-done.9.below, ...), custom_call_target="tpu_custom_call" | custom-call | flops 20000000000 | bytes 10000000 | tf_op jit(solution)/shard_map/conv_weight/pallas_call | solution.py:1029
  85.2 0.6 copy-done.6
  85.8 1.1 dynamic-slice_bitcast_fusion
  86.9 3.2 %collective-permute-done.10 = bf16[4,4,144,256]{3,2,1,0:T(8,128)(2,1)} collective-permute-done((bf16[4,4,144,256]{3,2,1,0:T(8,128)(2,1)}, bf16[4,4,144,256]{3,2,1,0:T(8,128)(2,1)}, u32[]{:S(2)}, u32[]{:S(2)}) %collective-permute-start.10) | collective-permute-done | bytes 1179680 | tf_op jit(solution)/shard_map/ppermute | solution.py:90
  90.1 2.6 %fusion = bf16[4,4,144,256]{3,2,1,0:T(8,128)(2,1)} fusion(bf16[4,4,144,256]{3,2,1,0:T(8,128)(2,1)} %collective-permute-done.10, bf16[4,2,4,144,256]{4,3,2,1,0:T(8,128)(2,1)S(1)} %bitcast.55, s32[]{:T(128)S(6)} %select_n.31), kind=kLoop, calls=%fused_computation.2 | loop fusion | flops 2359296 | bytes 3538948 | tf_op jit(solution)/shard_map/convert_element_type | solution.py:91
  92.8 6.8 %all-to-all-start.2 = ((bf16[16,144,256]{2,1,0:T(8,128)(2,1)}), bf16[16,144,256]{2,1,0:T(8,128)(2,1)}, u32[]{:S(2)}, u32[]{:S(2)}) async-start(bf16[16,144,256]{2,1,0:T(8,128)(2,1)} %bitcast.64), calls=%async_computation.2 | async-start | bytes 2359296 | tf_op jit(solution)/shard_map/all_to_all | solution.py:97
  99.6 1.0 copy-done.5
  100.7 23.8 %ffn_backward.1 = (f32[4096,256]{1,0:T(8,128)S(1)}, bf16[4096,256]{1,0:T(8,128)(2,1)S(1)}, bf16[1024,256]{1,0:T(8,128)(2,1)}, bf16[256,1024]{1,0:T(8,128)(2,1)},...) custom-call(s32[5]{0:T(128)S(1)} %pad_add_fusion.place, bf16[2,6,128,256]{3,2,1,0:T(8,128)(2,1)} %collective-permute-done.8.above, ...), custom_call_target="tpu_custom_call" | custom-call | flops 20000000000 | bytes 10000000 | tf_op jit(solution)/shard_map/ffn_backward/pallas_call | solution.py:613
  124.5 19.2 %attn_backward.1 = (f32[2,16,128,256]{3,2,1,0:T(8,128)}, bf16[2,4,128,256]{3,2,1,0:T(8,128)(2,1)S(1)}, bf16[256,768]{1,0:T(8,128)(2,1)S(1)}, bf16[8,512]{1,0:T(8,128)(2,1)S(1)}) custom-call(bf16[4096,256]{1,0:T(8,128)(2,1)S(1)} %get-tuple-element.100.mixed, bf16[4096,768]{1,0:T(8,128)(2,1)} %get-tuple-element.101.qkv, ...), custom_call_target="tpu_custom_call" | custom-call | flops 1000000 | bytes 10000 | tf_op jit(solution)/shard_map/attn_backward/pallas_call | solution.py:795
  143.7 0.2 copy.46
  144.0 0.4 concatenate.40
  145.1 2.6 %collective-permute-done.12 = bf16[4,4,8,3840]{3,2,1,0:T(8,128)(2,1)S(1)} collective-permute-done((bf16[4,4,8,3840]{3,2,1,0:T(8,128)(2,1)S(1)}, bf16[4,4,8,3840]{3,2,1,0:T(8,128)(2,1)S(1)}, u32[]{:S(2)}, u32[]{:S(2)}) %collective-permute-start.12) | collective-permute-done | bytes 983072 | tf_op jit(solution)/shard_map/ppermute | solution.py:90
  147.7 1.2 fusion.1
  148.8 6.9 %all-to-all-start.1 = ((bf16[16,8,3840]{2,1,0:T(8,128)(2,1)}), bf16[16,8,3840]{2,1,0:T(8,128)(2,1)S(1)}, u32[]{:S(2)}, u32[]{:S(2)}) async-start(bf16[16,8,3840]{2,1,0:T(8,128)(2,1)} %bitcast.23), calls=%async_computation.1 | async-start | bytes 1966080 | tf_op jit(solution)/shard_map/all_to_all | solution.py:97
  155.7 2.1 %convert_reduce_fusion = f32[144,256]{1,0:T(8,128)} fusion(bf16[16,144,256]{2,1,0:T(8,128)(2,1)} %all-to-all-done.2), kind=kLoop, calls=%fused_computation.3 | loop fusion | flops 1142784 | bytes 1327104 | tf_op jit(solution)/shard_map/reduce_sum | solution.py:1273
  157.8 2.0 %collective-permute-start.13 = (bf16[2,4,128,256]{3,2,1,0:T(8,128)(2,1)S(1)}, bf16[2,4,128,256]{3,2,1,0:T(8,128)(2,1)S(1)}, u32[]{:S(2)}, u32[]{:S(2)}) collective-permute-start(bf16[2,4,128,256]{3,2,1,0:T(8,128)(2,1)S(1)} %get-tuple-element.119), channel_id=1, source_target_pairs={{0,28},{4,0},{8,4},{12,8},{16,12},{20,16},{24,20},{28,24},{1,29},{... | collective-permute-start | bytes 1572872 | tf_op jit(solution)/shard_map/ppermute | solution.py:113
  159.8 8.8 %conv_data.1 = f32[2,16,128,256]{3,2,1,0:T(8,128)} custom-call(s32[5]{0:T(128)S(1)} %pad_add_fusion.place, bf16[2,6,128,256]{3,2,1,0:T(8,128)(2,1)} %collective-permute-done.8.above, bf16[2,16,128,256]{3,2,1,0:T(8,128)(2,1)} %own.5, bf16[2,2,128,256]{3,2,1,0:T(8,128)(2,1)} %collective-permute-done.9.below, bf16[9,2,256,256]{3,2,1,0:T(8,128)(2,1)} %bitcast.11.conv_w.weight), custom_call_target="tpu_custom_call" | custom-call | flops 10000000000 | bytes 10000000 | tf_op jit(solution)/shard_map/conv_data/pallas_call | solution.py:1029
  168.6 13.9 %conv_forward.1 = bf16[2,16,128,256]{3,2,1,0:T(8,128)(2,1)} custom-call(s32[5]{0:T(128)S(1)} %pad_add_fusion.place, bf16[2,16,128,256]{3,2,1,0:T(8,128)(2,1)S(1)} %copy-done.3, bf16[2,5,128,256]{3,2,1,0:T(8,128)(2,1)} %collective-permute-done.11.sums_below, bf16[2,6,128,256]{3,2,1,0:T(8,128)(2,1)} %collective-permute-done.8.above, ...), custom_call_target="tpu_custom_call" | custom-call | flops 1000000 | bytes 10000 | tf_op jit(solution)/shard_map/conv_forward/pallas_call | solution.py:1150
  182.6 1.1 convert_dynamic-update-slice_fusion
  183.7 0.7 last_sums.1
  184.4 0.6 fusion.4
  185.0 0.6 copy.44
  185.7 0.7 slice_bitcast_fusion.2
  (66 shorter events, 1.5 us)
Async XLA Ops:
  1.5 7.7 %collective-permute-start.2 = (bf16[1,8,3072]{2,1,0:T(8,128)(2,1)S(1)}, bf16[1,8,3072]{2,1,0:T(8,128)(2,1)S(1)}, u32[]{:S(2)}, u32[]{:S(2)}) collective-permute-start(bf16[1,8,3072]{2,1,0:T(8,128)(2,1)S(1)} %bitcast.56), channel_id=1, source_target_pairs={{0,3},{1,2},{2,1},{3,0},{4,7},{5,6},{6,5},{7,4},{8,11},{9,10},{10,... | collective-permute-start | bytes 147464 | tf_op jit(solution)/shard_map/ppermute | solution.py:75
  6.6 5.0 %collective-permute-start.1 = (bf16[1,8,3072]{2,1,0:T(8,128)(2,1)S(1)}, bf16[1,8,3072]{2,1,0:T(8,128)(2,1)S(1)}, u32[]{:S(2)}, u32[]{:S(2)}) collective-permute-start(bf16[1,8,3072]{2,1,0:T(8,128)(2,1)S(1)} %bitcast.57), channel_id=1, source_target_pairs={{0,2},{1,3},{2,0},{3,1},{4,6},{5,7},{6,4},{7,5},{8,10},{9,11},{10,... | collective-permute-start | bytes 147464 | tf_op jit(solution)/shard_map/ppermute | solution.py:75
  6.6 5.0 %collective-permute-start = (bf16[1,8,3072]{2,1,0:T(8,128)(2,1)S(1)}, bf16[1,8,3072]{2,1,0:T(8,128)(2,1)S(1)}, u32[]{:S(2)}, u32[]{:S(2)}) collective-permute-start(bf16[1,8,3072]{2,1,0:T(8,128)(2,1)S(1)} %bitcast.58), channel_id=1, source_target_pairs={{0,1},{1,0},{2,3},{3,2},{4,5},{5,4},{6,7},{7,6},{8,9},{9,8},{10,11... | collective-permute-start | bytes 147464 | tf_op jit(solution)/shard_map/ppermute | solution.py:75
  8.3 18.0 %collective-permute-start.6 = (bf16[2,4,128,256]{3,2,1,0:T(8,128)(2,1)S(1)}, bf16[2,4,128,256]{3,2,1,0:T(8,128)(2,1)}, u32[]{:S(2)}, u32[]{:S(2)}) collective-permute-start(bf16[2,4,128,256]{3,2,1,0:T(8,128)(2,1)S(1)} %slice.67), channel_id=1, source_target_pairs={{0,4},{4,8},{8,12},{12,16},{16,20},{20,24},{24,28},{28,0},{1,5},{5... | collective-permute-start | bytes 1572872 | tf_op jit(solution)/shard_map/ppermute | solution.py:113
  11.6 14.7 %collective-permute-start.5 = (bf16[4,8,3072]{2,1,0:T(8,128)(2,1)S(1)}, bf16[4,8,3072]{2,1,0:T(8,128)(2,1)S(1)}, u32[]{:S(2)}, u32[]{:S(2)}) collective-permute-start(bf16[4,8,3072]{2,1,0:T(8,128)(2,1)S(1)} %pad_maximum_fusion.2), channel_id=1, source_target_pairs={{0,24},{1,25},{2,26},{3,27},{4,28},{5,29},{6,30},{7,31},{8,16},{9,... | collective-permute-start | bytes 589832 | tf_op jit(solution)/shard_map/ppermute | solution.py:75
  14.1 12.2 %collective-permute-start.4 = (bf16[4,8,3072]{2,1,0:T(8,128)(2,1)S(1)}, bf16[4,8,3072]{2,1,0:T(8,128)(2,1)S(1)}, u32[]{:S(2)}, u32[]{:S(2)}) collective-permute-start(bf16[4,8,3072]{2,1,0:T(8,128)(2,1)S(1)} %pad_maximum_fusion.2), channel_id=1, source_target_pairs={{0,16},{1,17},{2,18},{3,19},{4,20},{5,21},{6,22},{7,23},{8,24},{9,... | collective-permute-start | bytes 589832 | tf_op jit(solution)/shard_map/ppermute | solution.py:75
  14.6 10.1 %collective-permute-start.3 = (bf16[4,8,3072]{2,1,0:T(8,128)(2,1)S(1)}, bf16[4,8,3072]{2,1,0:T(8,128)(2,1)S(1)}, u32[]{:S(2)}, u32[]{:S(2)}) collective-permute-start(bf16[4,8,3072]{2,1,0:T(8,128)(2,1)S(1)} %pad_maximum_fusion.2), channel_id=1, source_target_pairs={{0,8},{1,9},{2,10},{3,11},{4,12},{5,13},{6,14},{7,15},{8,0},{9,1},... | collective-permute-start | bytes 589832 | tf_op jit(solution)/shard_map/ppermute | solution.py:75
  15.2 3.5 %copy-start.12 = (f32[225,8]{0,1:T(8,128)S(1)}, f32[225,8]{0,1:T(8,128)}, u32[]{:S(2)}) copy-start(f32[225,8]{0,1:T(8,128)} %param.30) | copy-start | bytes 21604
  15.2 4.2 %slice-start = ((bf16[2,16,128,256]{3,2,1,0:T(8,128)(2,1)}), bf16[2,1,128,256]{3,2,1,0:T(8,128)(2,1)S(1)}, s32[]{:S(2)}) async-start(bf16[2,16,128,256]{3,2,1,0:T(8,128)(2,1)} %own.5), calls=%async_computation.3 | async-start | bytes 262144 | tf_op jit(solution)/shard_map/slice | solution.py:1215
  15.2 4.9 %slice-start.1 = ((bf16[2,16,128,256]{3,2,1,0:T(8,128)(2,1)}), bf16[2,5,128,256]{3,2,1,0:T(8,128)(2,1)S(1)}, s32[]{:S(2)}) async-start(bf16[2,16,128,256]{3,2,1,0:T(8,128)(2,1)} %own.5), calls=%async_computation.4 | async-start | bytes 1310720 | tf_op jit(solution)/shard_map/slice | solution.py:1214
  26.3 2.4 %collective-permute-start.7 = (bf16[16,8,3072]{2,1,0:T(8,128)(2,1)S(1)}, bf16[16,8,3072]{2,1,0:T(8,128)(2,1)S(1)}, u32[]{:S(2)}, u32[]{:S(2)}) collective-permute-start(bf16[16,8,3072]{2,1,0:T(8,128)(2,1)S(1)} %constant_dynamic-update-slice_fusion), channel_id=1, source_target_pairs={{0,4},{1,5},{2,6},{3,7},{4,0},{5,1},{6,2},{7,3},{8,12},{9,13},{10,... | collective-permute-start | bytes 2359304 | tf_op jit(solution)/shard_map/ppermute | solution.py:75
  28.7 5.2 %copy-start.8 = (bf16[2,6,128,256]{3,2,1,0:T(8,128)(2,1)S(1)}, bf16[2,6,128,256]{3,2,1,0:T(8,128)(2,1)}, u32[]{:S(2)}) copy-start(bf16[2,6,128,256]{3,2,1,0:T(8,128)(2,1)} %pad_maximum_fusion) | copy-start | bytes 2359300
  28.8 7.9 %copy-start.7 = (s32[32]{0:T(128)S(1)}, s32[32]{0:T(128)}, u32[]{:S(2)}) copy-start(s32[32]{0:T(128)} %constant.62.clone) | copy-start | bytes 388
  28.8 64.0 %all-to-all-start = ((bf16[32,144,256]{2,1,0:T(8,128)(2,1)}), bf16[32,144,256]{2,1,0:T(8,128)(2,1)}, u32[]{:S(2)}, u32[]{:S(2)}) async-start(bf16[32,144,256]{2,1,0:T(8,128)(2,1)} %make_copies.1), calls=%async_computation | async-start | bytes 4718592 | tf_op jit(solution)/shard_map/all_to_all | solution.py:101
  34.0 37.7 %collective-permute-start.8 = (bf16[2,6,128,256]{3,2,1,0:T(8,128)(2,1)S(1)}, bf16[2,6,128,256]{3,2,1,0:T(8,128)(2,1)}, u32[]{:S(2)}, u32[]{:S(2)}) collective-permute-start(bf16[2,6,128,256]{3,2,1,0:T(8,128)(2,1)S(1)} %copy-done.8), channel_id=1, source_target_pairs={{0,4},{4,8},{8,12},{12,16},{16,20},{20,24},{24,28},{28,0},{1,5},{5... | collective-permute-start | bytes 2359304 | tf_op jit(solution)/shard_map/ppermute | solution.py:113
  34.2 35.3 %collective-permute-start.9 = (bf16[2,2,128,256]{3,2,1,0:T(8,128)(2,1)}, bf16[2,2,128,256]{3,2,1,0:T(8,128)(2,1)}, u32[]{:S(2)}, u32[]{:S(2)}) collective-permute-start(bf16[2,2,128,256]{3,2,1,0:T(8,128)(2,1)} %pad_maximum_fusion.1), channel_id=1, source_target_pairs={{0,28},{4,0},{8,4},{12,8},{16,12},{20,16},{24,20},{28,24},{1,29},{... | collective-permute-start | bytes 786440 | tf_op jit(solution)/shard_map/ppermute | solution.py:113
  38.2 13.4 %copy-start.4 = (bf16[1024,256]{1,0:T(8,128)(2,1)}, bf16[1024,256]{1,0:T(8,128)(2,1)S(1)}, u32[]{:S(2)}) copy-start(bf16[1024,256]{1,0:T(8,128)(2,1)S(1)} %get-tuple-element.82.down_w) | copy-start | bytes 1572868
  51.6 17.9 %copy-start = (bf16[4096,256]{1,0:T(8,128)(2,1)}, bf16[4096,256]{1,0:T(8,128)(2,1)S(1)}, u32[]{:S(2)}) copy-start(bf16[4096,256]{1,0:T(8,128)(2,1)S(1)} %get-tuple-element.79.mix) | copy-start | bytes 6291460
  69.5 15.6 %copy-start.2 = (bf16[2,16,128,256]{3,2,1,0:T(8,128)(2,1)}, bf16[2,16,128,256]{3,2,1,0:T(8,128)(2,1)S(1)}, u32[]{:S(2)}) copy-start(bf16[2,16,128,256]{3,2,1,0:T(8,128)(2,1)S(1)} %get-tuple-element.90.sums) | copy-start | bytes 6291460
  85.2 0.6 copy-start.6
  86.9 3.2 %collective-permute-start.10 = (bf16[4,4,144,256]{3,2,1,0:T(8,128)(2,1)}, bf16[4,4,144,256]{3,2,1,0:T(8,128)(2,1)}, u32[]{:S(2)}, u32[]{:S(2)}) collective-permute-start(bf16[4,4,144,256]{3,2,1,0:T(8,128)(2,1)} %dynamic-slice_bitcast_fusion), channel_id=1, source_target_pairs={{0,4},{4,0},{8,12},{12,8},{16,20},{20,16},{24,28},{28,24},{1,5},{5... | collective-permute-start | bytes 3538952 | tf_op jit(solution)/shard_map/ppermute | solution.py:90
  92.7 6.9 %copy-start.1 = (bf16[4096,256]{1,0:T(8,128)(2,1)S(1)}, bf16[4096,256]{1,0:T(8,128)(2,1)}, u32[]{:S(2)}) copy-start(bf16[4096,256]{1,0:T(8,128)(2,1)} %copy-done) | copy-start | bytes 6291460
  92.7 31.8 %collective-permute-start.11 = (bf16[2,5,128,256]{3,2,1,0:T(8,128)(2,1)}, bf16[2,5,128,256]{3,2,1,0:T(8,128)(2,1)}, u32[]{:S(2)}, u32[]{:S(2)}) collective-permute-start(bf16[2,5,128,256]{3,2,1,0:T(8,128)(2,1)} %get-tuple-element.99), channel_id=1, source_target_pairs={{0,28},{4,0},{8,4},{12,8},{16,12},{20,16},{24,20},{28,24},{1,29},{... | collective-permute-start | bytes 1966088 | tf_op jit(solution)/shard_map/ppermute | solution.py:113
  92.8 56.0 %all-to-all-start.2 = ((bf16[16,144,256]{2,1,0:T(8,128)(2,1)}), bf16[16,144,256]{2,1,0:T(8,128)(2,1)}, u32[]{:S(2)}, u32[]{:S(2)}) async-start(bf16[16,144,256]{2,1,0:T(8,128)(2,1)} %bitcast.64), calls=%async_computation.2 | async-start | bytes 2359296 | tf_op jit(solution)/shard_map/all_to_all | solution.py:97
  99.6 1.0 copy-start.5
  124.5 19.3 %copy-start.10 = (bf16[1024,256]{1,0:T(8,128)(2,1)S(1)}, bf16[1024,256]{1,0:T(8,128)(2,1)}, u32[]{:S(2)}) copy-start(bf16[1024,256]{1,0:T(8,128)(2,1)} %get-tuple-element.109) | copy-start | bytes 1572868
  143.7 0.9 copy-start.11
  143.7 1.1 copy-start.9
  145.0 2.6 %collective-permute-start.12 = (bf16[4,4,8,3840]{3,2,1,0:T(8,128)(2,1)S(1)}, bf16[4,4,8,3840]{3,2,1,0:T(8,128)(2,1)S(1)}, u32[]{:S(2)}, u32[]{:S(2)}) collective-permute-start(bf16[4,4,8,3840]{3,2,1,0:T(8,128)(2,1)S(1)} %dynamic-slice_bitcast_fusion.1), channel_id=1, source_target_pairs={{0,4},{4,0},{8,12},{12,8},{16,20},{20,16},{24,28},{28,24},{1,5},{5... | collective-permute-start | bytes 2949128 | tf_op jit(solution)/shard_map/ppermute | solution.py:90
  148.8 34.8 %all-to-all-start.1 = ((bf16[16,8,3840]{2,1,0:T(8,128)(2,1)}), bf16[16,8,3840]{2,1,0:T(8,128)(2,1)S(1)}, u32[]{:S(2)}, u32[]{:S(2)}) async-start(bf16[16,8,3840]{2,1,0:T(8,128)(2,1)} %bitcast.23), calls=%async_computation.1 | async-start | bytes 1966080 | tf_op jit(solution)/shard_map/all_to_all | solution.py:97
  157.8 10.9 %copy-start.3 = (bf16[2,16,128,256]{3,2,1,0:T(8,128)(2,1)S(1)}, bf16[2,16,128,256]{3,2,1,0:T(8,128)(2,1)}, u32[]{:S(2)}) copy-start(bf16[2,16,128,256]{3,2,1,0:T(8,128)(2,1)} %copy-done.2) | copy-start | bytes 6291460
  157.8 24.8 %collective-permute-start.13 = (bf16[2,4,128,256]{3,2,1,0:T(8,128)(2,1)S(1)}, bf16[2,4,128,256]{3,2,1,0:T(8,128)(2,1)S(1)}, u32[]{:S(2)}, u32[]{:S(2)}) collective-permute-start(bf16[2,4,128,256]{3,2,1,0:T(8,128)(2,1)S(1)} %get-tuple-element.119), channel_id=1, source_target_pairs={{0,28},{4,0},{8,4},{12,8},{16,12},{20,16},{24,20},{28,24},{1,29},{... | collective-permute-start | bytes 1572872 | tf_op jit(solution)/shard_map/ppermute | solution.py:113

commit v2 on v1

--- a/solution.py
+++ b/solution.py
@@ -16,6 +16,7 @@
 BF = jnp.bfloat16
 F32 = jnp.float32
 MIB = 1024 * 1024
+BACK_MIB = 56
 LOG2E = 1.4426950408889634
 
 
@@ -87,9 +88,13 @@
     by_core = x.reshape((rows // 2, 2, batch) + x.shape[1:])
     mine = lax.dynamic_index_in_dim(by_core, core, 1, False)
     other = lax.dynamic_index_in_dim(by_core, 1 - core, 1, False)
+    return add_pairs(*(a.reshape((-1,) + x.shape[1:]) for a in (mine, other)))
+
+
+def add_pairs(mine, other):
+    rows, batch = lax.axis_size("rows"), lax.axis_size("batch")
     other = lax.ppermute(other, "rows", [(i, i ^ 1) for i in range(rows)])
     pairs = (mine.astype(F32) + other.astype(F32)).astype(BF)
-    pairs = pairs.reshape((rows // 2 * batch,) + x.shape[1:])
     groups = [
         [(2 * chip + k) * batch + b for chip in range(rows // 2) for b in range(batch)]
         for k in range(2)
@@ -464,7 +469,7 @@
         ],
         out_shape=[pltpu.HBM((total, n), t) for n, t in zip(rows, types)]
         + [
-            pltpu.VMEM(shape, BF),
+            pltpu.HBM(shape, BF),
             jax.ShapeDtypeStruct((samples, WIN // 2 + 1, columns, width), BF),
         ],
         scratch_shapes=[pltpu.VMEM((columns // WIN, WIN, WIN, width), F32)],
@@ -481,13 +486,11 @@
     return jnp.sum(x, 0, keepdims=True)
 
 
-def ffn_backward_body(
-    height, step_of, place, above, own, act, slope, normed, xhat_ref, rstd_ref, mix, conv_w,
-    out_w, gain, up_w, down_w, first_out, mixed_out, down_out, up_out, out_out, vec_out,
+def ffn_backward_step(
+    height, step, sample, band, place, above, own, act, slope, normed, xhat_ref, rstd_ref, mix, conv_w,
+    out_w, gain, up_w, down_w, first_out, mixed_out,
     taps, turned, branch, low, raised_s, attn, down_acc, up_acc, out_acc, vec,
 ):
-    step = pl.program_id(0)
-    sample, band = step_of(step)
     columns = own.shape[2]
     tokens = columns * WIN
     half = WIN // 2
@@ -580,92 +583,56 @@
         up_acc[:, wide] += dot(normed_t, raised_s[:, wide])
     out_acc[...] += dot(mix[...].T, attn[...])
 
-    @pl.when(step == pl.num_programs(0) - 1)
-    def _():
-        for f in range(0, 1024, 256):
-            wide = slice(f, f + 256)
-            down_out[wide] = down_acc[:, wide].T.astype(BF)
-            up_out[:, wide] = up_acc[:, wide].astype(BF)
-        out_out[...] = out_acc[...].astype(BF)
-        vec_out[...] = vec[...].astype(BF)
-
-
-def ffn_backward(
-    place, above, own, act, slope, normed, xhat, rstd, mix, conv_w, out_w, gain, up_w, down_w, height
-):
-    samples, grid_rows, columns, width = own.shape
-    bands = grid_rows // WIN
-    tokens = WIN * columns
-    steps = samples * bands
-    total = steps * tokens
-    hidden = up_w.shape[1]
-
-    def step_of(step):
-        return step // bands, step % bands
-
-    def row_block(step):
-        return (step, 0)
-
-    def sample_block(step):
-        return (step_of(step)[0], 0, 0, 0)
-
-    rows = (act, slope, normed, xhat, rstd, mix)
-    return pl.pallas_call(
-        functools.partial(ffn_backward_body, height, step_of),
-        grid=(steps,),
-        in_specs=[
-            SMEM_SPEC,
-            pl.BlockSpec((1,) + above.shape[1:], sample_block),
-            pl.BlockSpec((1,) + own.shape[1:], sample_block),
-        ]
-        + [pl.BlockSpec((tokens, a.shape[1]), row_block) for a in rows]
-        + [pl.BlockSpec((9, 1, width, width), lambda s: (0, 0, 0, 0))]
-        + [const_spec(a.shape) for a in (out_w, gain, up_w, down_w)],
-        out_specs=[
-            pl.BlockSpec((tokens, width), row_block),
-            pl.BlockSpec((tokens, width), row_block),
-            const_spec((hidden, width)),
-            const_spec((width, hidden)),
-            const_spec((width, width)),
-            const_spec((8, width)),
-        ],
-        out_shape=[
-            pltpu.VMEM((total, width), F32),
-            pltpu.VMEM((total, width), BF),
-            pltpu.HBM((hidden, width), BF),
-            pltpu.HBM((width, hidden), BF),
-            pltpu.HBM((width, width), BF),
-            jax.ShapeDtypeStruct((8, width), BF),
-        ],
-        scratch_shapes=[
-            pltpu.VMEM((WIN + 4, columns, 3 * width), BF),
-            pltpu.VMEM((3, width, 3 * width), BF),
-            pltpu.VMEM((columns // WIN, WIN, WIN, width), F32),
-            pltpu.VMEM((tokens, width), BF),
-            pltpu.VMEM((tokens, hidden), BF),
-            pltpu.VMEM((tokens, width), BF),
-            pltpu.VMEM((width, hidden), F32),
-            pltpu.VMEM((width, hidden), F32),
-            pltpu.VMEM((width, width), F32),
-            pltpu.VMEM((8, width), F32),
-        ],
-        compiler_params=params(44),
-        cost_estimate=pl.CostEstimate(
-            flops=2 * 10**10, bytes_accessed=10**7, transcendentals=0
-        ),
-        name="ffn_backward",
-    )(
-        place, *far(above, own, *rows[:5]), *near(mix), *far(conv_w), *near(out_w), *far(gain),
-        *near(up_w, down_w),
-    )
-
-
-def attn_backward_body(
-    scale, step_of, mixed, qkv, prob, normed, xhat_ref, rstd_ref, first, weight, gain, mask, conv_vec,
-    places, input_out, up_out, qkv_out, vec_out, qkv_acc, table_acc, vec_acc, grads, score_grads, sums,
-):
+
+def ffn_backward_end(down_out, up_out, out_out, vec_out, down_acc, up_acc, out_acc, vec):
+    for f in range(0, 1024, 256):
+        wide = slice(f, f + 256)
+        down_out[wide] = down_acc[:, wide].T.astype(BF)
+        up_out[:, wide] = up_acc[:, wide].astype(BF)
+    out_out[...] = out_acc[...].astype(BF)
+    vec_out[...] = vec[...].astype(BF)
+
+
+def send_rows(core, batch, mine, other, down_rows, down_acc, out_acc, up_acc, qkv_acc, vectors):
+    for f in range(0, 1024, 256):
+        turned = down_acc[:, f : f + 256].T.reshape(8, 4, 8, 256)
+        for k in range(4):
+            piece = turned[:, k].reshape(64, 256)
+            down_rows[f // 4 : f // 4 + 64, 256 * k : 256 * k + 256] = piece.astype(BF)
+    count = 8 * batch
+    wide_vectors = jnp.concatenate([vectors] * batch, 0).astype(BF)
+
+    def put(target, k):
+        for chip in range(256 // (2 * count)):
+            rows = slice((2 * chip + k) * count, (2 * chip + k + 1) * count)
+            to = slice(chip * count, (chip + 1) * count)
+            at = 0
+            for ref in (down_rows, out_acc, up_acc, qkv_acc):
+                target[to, at : at + ref.shape[1]] = ref[rows].astype(BF)
+                at += ref.shape[1]
+            target[to, at:] = wide_vectors
+
+    for k in range(2):
+
+        @pl.when(core == k)
+        def _():
+            put(mine, k)
+            put(other, 1 - k)
+
+
+def backward_body(height, scale, step_of, batch, *refs):
+    place, above, own, *refs = refs
+    ffn_rows, refs = refs[:6], refs[6:]
+    attn_rows, refs = refs[:5], refs[5:]
+    ffn_consts, refs = refs[:5], refs[5:]
+    (weight, gain, mask, conv_vec, places), refs = refs[:5], refs[5:]
+    input_out, up_out, *refs = refs
+    outs, refs = (refs[:2], refs[2:]) if batch else (refs[:6], refs[6:])
+    ffn_scratch, (first, mixed, qkv_acc, table_acc, vec_acc, grads, score_grads, sums, down_rows) = (
+        refs[:10], refs[10:],
+    )
     step = pl.program_id(0)
-    _, band = step_of(step)
+    sample, band = step_of(step)
     columns = input_out.shape[2]
     half = WIN // 2
 
@@ -674,6 +641,11 @@
         for ref in (qkv_acc, table_acc, vec_acc):
             ref[...] = jnp.zeros_like(ref)
 
+    ffn_backward_step(
+        height, step, sample, band, place, above, own, *ffn_rows, *ffn_consts, first, mixed,
+        *ffn_scratch,
+    )
+    qkv, prob, normed, xhat_ref, rstd_ref = attn_rows
     attn_backward_step(
         scale, mixed, qkv, prob, normed, xhat_ref, rstd_ref, first, weight, gain, mask,
         qkv_acc, table_acc, vec_acc, grads, score_grads, sums,
@@ -695,11 +667,22 @@
 
     @pl.when(step == pl.num_programs(0) - 1)
     def _():
+        table = collect_bias(table_acc[...], places[...])
+        rest = jnp.concatenate([vec_acc[0:2], conv_vec[0:1], jnp.zeros((5, 256), F32)], 0)
+        vectors = jnp.concatenate([table, rest], 1)
+        down_acc, up_acc, out_acc, vec = ffn_scratch[6:]
+        if batch:
+            vectors = jnp.concatenate([vec[...], vectors], 1)
+            send_rows(
+                place[place.shape[0] - 1], batch, *outs, down_rows, down_acc, out_acc, up_acc, qkv_acc,
+                vectors,
+            )
+            return
+        *ffn_outs, qkv_out, vec_out = outs
+        ffn_backward_end(*ffn_outs, down_acc, up_acc, out_acc, vec)
         for f in range(0, 768, 256):
             qkv_out[:, f : f + 256] = qkv_acc[:, f : f + 256].astype(BF)
-        table = collect_bias(table_acc[...], places[...])
-        rest = jnp.concatenate([vec_acc[0:2], conv_vec[0:1], jnp.zeros((5, 256), F32)], 0)
-        vec_out[...] = jnp.concatenate([table, rest], 1).astype(BF)
+        vec_out[...] = vectors.astype(BF)
 
 
 def attn_backward_step(
@@ -770,12 +753,12 @@
     lax.fori_loop(0, tokens // 256, part, 0, unroll=True)
 
 
-def attn_backward(
-    mixed, qkv, prob, normed, xhat, rstd, first, weight, gain, mask, conv_vec, places, scale, shape
-):
-    samples, grid_rows, columns, width = shape
+def backward(place, above, own, ffn_rows, attn_rows, ffn_consts, attn_consts, height, scale, batch):
+    samples, grid_rows, columns, width = own.shape
     bands = grid_rows // WIN
     tokens = WIN * columns
+    steps = samples * bands
+    hidden = ffn_rows[0].shape[1]
     half = WIN // 2
 
     def step_of(step):
@@ -787,39 +770,61 @@
     def sample_block(step):
         return (step_of(step)[0], 0, 0, 0)
 
-    rows = (mixed, qkv, prob, normed, xhat, rstd, first)
-    consts = (weight, gain, mask, conv_vec, places)
-    in_specs = [pl.BlockSpec((tokens, a.shape[1]), row_block) for a in rows]
-    in_specs[2] = pl.BlockSpec((columns // 16, 512, 128), lambda s: (s, 0, 0))
-    in_specs += [const_spec(a.shape) for a in consts]
+    in_specs = [
+        SMEM_SPEC,
+        pl.BlockSpec((1,) + above.shape[1:], sample_block),
+        pl.BlockSpec((1,) + own.shape[1:], sample_block),
+    ]
+    in_specs += [pl.BlockSpec((tokens, a.shape[1]), row_block) for a in (*ffn_rows, *attn_rows)]
+    in_specs[10] = pl.BlockSpec((columns // 16, 512, 128), lambda s: (s, 0, 0))
+    in_specs += [pl.BlockSpec((9, 1, width, width), lambda s: (0, 0, 0, 0))]
+    in_specs += [const_spec(a.shape) for a in (*ffn_consts[1:], *attn_consts)]
+    outs = [(own.shape, F32), ((samples, half, columns, width), BF)]
+    if batch:
+        outs += [((width // 2, 2 * hidden + 7 * width), BF)] * 2
+    else:
+        outs += [
+            ((hidden, width), BF), ((width, hidden), BF), ((width, width), BF), ((8, width), BF),
+            ((width, 3 * width), BF), ((8, 2 * width), BF),
+        ]
+    out_specs = [const_spec(a) for a, _ in outs]
+    out_specs[0] = pl.BlockSpec((1,) + own.shape[1:], sample_block)
+    out_specs[1] = pl.BlockSpec((1, half, columns, width), sample_block)
     return pl.pallas_call(
-        functools.partial(attn_backward_body, scale, step_of),
-        grid=(samples * bands,),
+        functools.partial(backward_body, height, scale, step_of, batch),
+        grid=(steps,),
         in_specs=in_specs,
-        out_specs=[
-            pl.BlockSpec((1,) + shape[1:], sample_block),
-            pl.BlockSpec((1, half, columns, width), sample_block),
-            const_spec((width, 3 * width)),
-            const_spec((8, 2 * width)),
-        ],
-        out_shape=[
-            jax.ShapeDtypeStruct(shape, F32),
-            jax.ShapeDtypeStruct((samples, half, columns, width), BF),
-            jax.ShapeDtypeStruct((width, 3 * width), BF),
-            jax.ShapeDtypeStruct((8, 2 * width), BF),
-        ],
+        out_specs=out_specs,
+        out_shape=[pltpu.HBM(a, t) for a, t in outs],
         scratch_shapes=[
+            pltpu.VMEM((WIN + 4, columns, 3 * width), BF),
+            pltpu.VMEM((3, width, 3 * width), BF),
+            pltpu.VMEM((columns // WIN, WIN, WIN, width), F32),
+            pltpu.VMEM((tokens, width), BF),
+            pltpu.VMEM((tokens, hidden), BF),
+            pltpu.VMEM((tokens, width), BF),
+            pltpu.VMEM((width, hidden), F32),
+            pltpu.VMEM((width, hidden), F32),
+            pltpu.VMEM((width, width), F32),
+            pltpu.VMEM((8, width), F32),
+            pltpu.VMEM((tokens, width), F32),
+            pltpu.VMEM((tokens, width), BF),
             pltpu.VMEM((width, 3 * width), F32),
             pltpu.VMEM((512, 128), F32),
             pltpu.VMEM((8, width), F32),
             pltpu.VMEM((tokens, 3 * width), BF),
             pltpu.VMEM((columns // 16, 512, 128), BF),
             pltpu.VMEM((columns // WIN, WIN, WIN, width), F32),
+            pltpu.VMEM((width, hidden), BF),
         ],
-        compiler_params=params(32),
-        cost_estimate=SMALL_COST,
-        name="attn_backward",
-    )(*near(mixed), *far(*rows[1:6]), *near(first, weight), *far(*consts[1:]))
+        compiler_params=params(BACK_MIB),
+        cost_estimate=pl.CostEstimate(
+            flops=4 * 10**10, bytes_accessed=10**7, transcendentals=0
+        ),
+        name="backward",
+    )(
+        place, *far(above, own, *ffn_rows, *attn_rows, *ffn_consts, *attn_consts),
+    )
 
 
 def shifted(row, by):
@@ -890,8 +895,8 @@
     )(order, held)
 
 
-def last_sums_body(parts, down, out_w, up, qkv, vec):
-    count, rows, _ = parts.shape
+def last_sums_body(parts, down, out_w, up, qkv, *vectors):
+    count, rows, lanes = parts.shape
     total = parts[0].astype(F32)
     for k in range(1, count):
         total = total + parts[k].astype(F32)
@@ -899,19 +904,52 @@
     for k in range(down.shape[0] // rows):
         down[k * rows : (k + 1) * rows] = total[:, k * width : (k + 1) * width]
     at = down.size // rows
-    for ref in (out_w, up, qkv, vec):
+    for ref in (out_w, up, qkv):
         ref[...] = total[:, at : at + ref.shape[1]]
         at += ref.shape[1]
 
+    def vector(row, group):
+        row, lane = divmod((row * 3 + group) * width, lanes - at)
+        return total[row : row + 1, at + lane : at + lane + width]
+
+    singles, (up_bias, table), more = vectors[:4], vectors[4:6], vectors[6:]
+    for k, ref in enumerate(singles):
+        ref[...] = vector(k, 0)
+    for k in range(4):
+        up_bias[:, k * width : (k + 1) * width] = vector(4 + k, 0)
+    for k in range(8):
+        table[k : k + 1] = vector(k, 1)
+    for k, ref in enumerate(more):
+        ref[...] = vector(k, 2)
+
 
 def last_sums(parts, down, rest):
-    shapes = (down, *rest)
+    width = down[1]
+    vectors = [(1, width)] * 4 + [(1, 4 * width), (8, width)] + [(1, width)] * 3
+    shapes = (down, *rest, *vectors)
     return pl.pallas_call(
         last_sums_body,
         out_shape=[jax.ShapeDtypeStruct(a, F32) for a in shapes],
         compiler_params=params(24),
         cost_estimate=SMALL_COST,
         name="last_sums",
+    )(parts)
+
+
+def sum_body(parts, out):
+    total = parts[0].astype(F32)
+    for k in range(1, parts.shape[0]):
+        total = total + parts[k].astype(F32)
+    out[...] = total
+
+
+def sum_parts(parts):
+    return pl.pallas_call(
+        sum_body,
+        out_shape=jax.ShapeDtypeStruct(parts.shape[1:], F32),
+        compiler_params=params(16),
+        cost_estimate=SMALL_COST,
+        name="sum_parts",
     )(parts)
 
 
@@ -1048,7 +1086,7 @@
     shape = (9, 2, width, width)
     acc = pltpu.VMEM((3, width, 3 * width), F32)
     return conv_call(
-        conv_weight_body, "conv_weight", 34, place, [*map(whole, grads), (field_spec(sums), near(sums)[0]), whole(hidden)], (),
+        conv_weight_body, "conv_weight", 34, place, [*map(whole, grads), whole(sums), whole(hidden)], (),
         height, [const_spec(shape), const_spec((8, width))],
         [jax.ShapeDtypeStruct(shape, BF), jax.ShapeDtypeStruct((8, width), F32)],
         [
@@ -1146,7 +1184,7 @@
 
 def conv_forward(place, sums, sums_below, hidden, weight, bias, height):
     samples, rows, columns, width = sums.shape
-    fields = (*near(sums), *far(sums_below, *hidden))
+    fields = far(sums, sums_below, *hidden)
     return pl.pallas_call(
         functools.partial(conv_forward_body, height),
         grid=(samples,),
@@ -1194,7 +1232,7 @@
     row_place = lax.axis_index("rows")
     row_start = row_place * grid_rows
     place = jnp.concatenate(
-        [(row_start - half)[None].astype(jnp.int32), crop_rows, crop_cols]
+        [(row_start - half)[None].astype(jnp.int32), crop_rows, crop_cols, (row_place % 2)[None]]
     ).astype(jnp.int32)
 
     hidden_width = up_weight.shape[1]
@@ -1240,23 +1278,30 @@
     conv_all = exchange(conv_local)
     sums_below = ring(after(sums_first, conv_local), -1)
     conv_blocks = after(conv_full.reshape(9, 2, width, width), conv_local)
-    first_grad, mixed, down_acc, up_acc, out_acc, vec_ffn = ffn_backward(
-        place, halo_above, cotangent, act, slope, normed_2, xhat_2, rstd_2, mix, conv_blocks,
-        output_full, vec(second_gain), up_full, down_full, height,
-    )
-    input_grad, input_up, qkv_acc, vec_attn = attn_backward(
-        after(mixed, sums_below), qkv, prob, normed, xhat, rstd, first_grad, qkv_full,
-        vec(first_gain), mask, conv_bias_part, jnp.asarray(offset_places(True), BF).T, scale, shape,
-    )
-    down_acc, up_acc, out_acc, vec_ffn = after((down_acc, up_acc, out_acc, vec_ffn), qkv_acc)
-    down_local = down_acc.reshape(devices, -1, rows_out, width).transpose(0, 2, 1, 3)
-    parts = [
-        down_local.reshape(devices, rows_out, -1),
-        *(a.reshape(devices, rows_out, -1) for a in (out_acc, up_acc, qkv_acc)),
-    ]
-    last_local, exchange = scatter_pairs(
-        with_vectors(parts, jnp.concatenate([vec_ffn, vec_attn], 1))
-    )
+    input_grad, input_up, *last_parts = backward(
+        place, halo_above, cotangent,
+        (act, slope, normed_2, xhat_2, rstd_2, mix),
+        (qkv, prob, normed, xhat, rstd),
+        (conv_blocks, output_full, vec(second_gain), up_full, down_full),
+        (
+            qkv_full, vec(first_gain), mask, conv_bias_part,
+            jnp.asarray(offset_places(True), BF).T,
+        ),
+        height, scale, lax.axis_size("batch") if rows_out == 8 else 0,
+    )
+    last_parts = after(tuple(last_parts), sums_below)
+    if rows_out == 8:
+        last_local, exchange = add_pairs(*(a.reshape(-1, rows_out, a.shape[1]) for a in last_parts))
+    else:
+        down_acc, up_acc, out_acc, vec_ffn, qkv_acc, vec_attn = last_parts
+        down_local = down_acc.reshape(devices, -1, rows_out, width).transpose(0, 2, 1, 3)
+        parts = [
+            down_local.reshape(devices, rows_out, -1),
+            *(a.reshape(devices, rows_out, -1) for a in (out_acc, up_acc, qkv_acc)),
+        ]
+        last_local, exchange = scatter_pairs(
+            with_vectors(parts, jnp.concatenate([vec_ffn, vec_attn], 1))
+        )
     last_all = exchange(last_local)
     input_from_below = ring(after(input_up, last_local), -1)
     hidden_grad = conv_data(after(place, last_local), grads, conv_blocks, height)
@@ -1269,26 +1314,17 @@
         after(input_grad, layer_output), input_from_below.astype(F32), (0, grid_rows - half, 0, 0)
     )
 
-    def total(parts):
-        return jnp.sum(parts.astype(F32), 0)
-
-    conv_weight_grad = total(conv_all)
-    down_weight_grad, output_weight_grad, up_weight_grad, qkv_weight_grad, vectors = last_sums(
+    conv_weight_grad = sum_parts(conv_all)
+    down_weight_grad, output_weight_grad, up_weight_grad, qkv_weight_grad, *vectors = last_sums(
         last_all,
         (rows_down, width),
-        [
-            (rows_out, width), (rows_out, hidden_width), (rows_out, 3 * width),
-            (rows_out, 24 * width // rows_out),
-        ],
-    )
-    vectors = vectors.reshape(8, 3, width)
-    ffn_vec, table_grad, attn_vec = (vectors[:, k] for k in range(3))
-    down_bias_grad, second_gain_grad, second_shift_grad, output_bias_grad = (
-        ffn_vec[k] for k in range(4)
-    )
-    up_bias_grad = ffn_vec[4:].reshape(-1)
-    bias_table_grad = table_grad[:, :offsets][:, ::-1].T
-    first_gain_grad, first_shift_grad, conv_bias_grad = (attn_vec[k] for k in range(3))
+        [(rows_out, width), (rows_out, hidden_width), (rows_out, 3 * width)],
+    )
+    bias_table_grad = vectors.pop(5)[:, :offsets][:, ::-1].T
+    (
+        down_bias_grad, second_gain_grad, second_shift_grad, output_bias_grad, up_bias_grad,
+        first_gain_grad, first_shift_grad, conv_bias_grad,
+    ) = (v.reshape(-1) for v in vectors)
     return (
         layer_output,
         input_grad,

time: 187 us -> 180 us (0.963)
  local copies, waits for them, and re-layouts: 9.62 us -> 5.08 us
  other arithmetic: 9.43 us -> 7.45 us
    unnamed x40 -> x32, local copies, waits for them, and re-layouts: 3.02 us -> 0.73 us
    reduce_sum x1 -> x0, other arithmetic: 2.1 us -> none  [total(): return jnp.sum(parts.astype(F32), 0)]
    pallas_call x2, Pallas kernels: 43 us -> 41 us  [the longest x1 40.2 us: backward(): pl.pallas_call(functools.partial(backward_body, height, scale, step_of, b...]
  transfers between devices with their start and end apart: 17 -> 17, of which waited for: 7 -> 7; matrix products, arithmetic and copies ran while one was open for 8% -> 6% of each run, Pallas kernels for 61% -> 63%
where the time goes in v2:
time: 180 us; the launch traced here: 179 us
  Pallas kernels  115 us (64%)
  starting transfers between devices  33.4 us (19%)
  waiting for transfers between devices  17 us (9%)
  other arithmetic  7.45 us (4%)
  local copies, waits for them, and re-layouts  5.08 us (3%)
    pallas_call x1, Pallas kernels, backward(): pl.pallas_call(functools.partial(backward_body, height, scale, step_of, b...  40.2 us
    pallas_call x2, Pallas kernels, conv_call(): pl.pallas_call(functools.partial(body, height), grid=(fields[0][1].shape[...  22.6 us
    pallas_call x1, Pallas kernels, ffn_forward(): pl.pallas_call(functools.partial(ffn_forward_body, height, step_of), grid...  18 us
    pallas_call x1, Pallas kernels, conv_forward(): pl.pallas_call(functools.partial(conv_forward_body, height), grid=(sample...  14.8 us
    all_to_all x2, starting transfers between devices, add_pairs(): lax.all_to_all(a, AXES, 0, 0, axis_index_groups=groups, tiled=True)  13.9 us
    pallas_call x1, Pallas kernels, attn_forward(): pl.pallas_call(functools.partial(attn_forward_body, height, scale, step_o...  13.7 us
    ppermute x7, waiting for transfers between devices, gather_steps(): lax.ppermute(held, AXES, [(i, i ^ mask) for i in range(devices)])  9.73 us
    ppermute x7, starting transfers between devices, gather_steps(): lax.ppermute(held, AXES, [(i, i ^ mask) for i in range(devices)])  9.51 us
  transfers between devices with their start and end apart: 17, of which 7 were waited for; matrix products, arithmetic and copies ran while one was open for 6% of the time, Pallas kernels for 63%

profile of v2, /device:TPU:0, one launch (start us, length us, event | category | flops | bytes accessed | tf_op | source)
XLA Modules:
  0.0 179.0 jit_solution(7788352734221588562)
XLA Ops:
  0.7 0.8 pack_near.1
  1.5 5.1 %collective-permute-start.2 = (bf16[1,8,3072]{2,1,0:T(8,128)(2,1)S(1)}, bf16[1,8,3072]{2,1,0:T(8,128)(2,1)S(1)}, u32[]{:S(2)}, u32[]{:S(2)}) collective-permute-start(bf16[1,8,3072]{2,1,0:T(8,128)(2,1)S(1)} %bitcast.43), channel_id=1, source_target_pairs={{0,3},{1,2},{2,1},{3,0},{4,7},{5,6},{6,5},{7,4},{8,11},{9,10},{10,... | collective-permute-start | bytes 147464 | tf_op jit(solution)/shard_map/ppermute | solution.py:76
  6.6 0.6 collective-permute-start
  7.2 1.1 slice.22
  8.3 0.1 collective-permute-start.6
  8.4 0.8 pad_add_fusion.place.refs_0_
  9.2 2.4 %collective-permute-done.1 = bf16[1,8,3072]{2,1,0:T(8,128)(2,1)S(1)} collective-permute-done((bf16[1,8,3072]{2,1,0:T(8,128)(2,1)S(1)}, bf16[1,8,3072]{2,1,0:T(8,128)(2,1)S(1)}, u32[]{:S(2)}, u32[]{:S(2)}) %collective-permute-start.1) | collective-permute-done | bytes 49184 | tf_op jit(solution)/shard_map/ppermute | solution.py:76
  11.6 2.5 %collective-permute-start.5 = (bf16[4,8,3072]{2,1,0:T(8,128)(2,1)S(1)}, bf16[4,8,3072]{2,1,0:T(8,128)(2,1)S(1)}, u32[]{:S(2)}, u32[]{:S(2)}) collective-permute-start(bf16[4,8,3072]{2,1,0:T(8,128)(2,1)S(1)} %pad_maximum_fusion.2), channel_id=1, source_target_pairs={{0,24},{1,25},{2,26},{3,27},{4,28},{5,29},{6,30},{7,31},{8,16},{9,... | collective-permute-start | bytes 589832 | tf_op jit(solution)/shard_map/ppermute | solution.py:76
  14.1 0.5 collective-permute-start.4
  14.6 0.5 collective-permute-start.3
  15.2 1.1 fusion.3
  16.2 2.5 %make_copies.1 = bf16[32,144,256]{2,1,0:T(8,128)(2,1)} custom-call(f32[144,256]{1,0:T(8,128)} %x.2), custom_call_target="tpu_custom_call" | custom-call | flops 1000000 | bytes 10000 | tf_op jit(solution)/shard_map/make_copies/pallas_call | solution.py:963
  18.7 0.6 pad.4.table
  19.3 0.7 pad_maximum_fusion.1
  20.1 1.0 pad_maximum_fusion
  21.0 3.7 %collective-permute-done.3 = bf16[4,8,3072]{2,1,0:T(8,128)(2,1)S(1)} collective-permute-done((bf16[4,8,3072]{2,1,0:T(8,128)(2,1)S(1)}, bf16[4,8,3072]{2,1,0:T(8,128)(2,1)S(1)}, u32[]{:S(2)}, u32[]{:S(2)}) %collective-permute-start.3) | collective-permute-done | bytes 196640 | tf_op jit(solution)/shard_map/ppermute | solution.py:76
  24.7 1.5 collective-permute-done.4
  26.3 0.2 collective-permute-start.7
  26.6 0.1 constant_dynamic-update-slice_fusion.8
  26.6 2.1 %collective-permute-done.7 = bf16[16,8,3072]{2,1,0:T(8,128)(2,1)S(1)} collective-permute-done((bf16[16,8,3072]{2,1,0:T(8,128)(2,1)S(1)}, bf16[16,8,3072]{2,1,0:T(8,128)(2,1)S(1)}, u32[]{:S(2)}, u32[]{:S(2)}) %collective-permute-start.7) | collective-permute-done | bytes 786464 | tf_op jit(solution)/shard_map/ppermute | solution.py:76
  28.7 0.1 constant_dynamic-update-slice_fusion.7.held
  28.8 5.2 %all-to-all-start = ((bf16[32,144,256]{2,1,0:T(8,128)(2,1)}), bf16[32,144,256]{2,1,0:T(8,128)(2,1)}, u32[]{:S(2)}, u32[]{:S(2)}) async-start(bf16[32,144,256]{2,1,0:T(8,128)(2,1)} %make_copies.1), calls=%async_computation | async-start | bytes 4718592 | tf_op jit(solution)/shard_map/all_to_all | solution.py:106
  34.0 0.2 collective-permute-start.8
  34.2 2.5 %collective-permute-start.9 = (bf16[2,2,128,256]{3,2,1,0:T(8,128)(2,1)}, bf16[2,2,128,256]{3,2,1,0:T(8,128)(2,1)}, u32[]{:S(2)}, u32[]{:S(2)}) collective-permute-start(bf16[2,2,128,256]{3,2,1,0:T(8,128)(2,1)} %pad_maximum_fusion.1), channel_id=1, source_target_pairs={{0,28},{4,0},{8,4},{12,8},{16,12},{20,16},{24,20},{28,24},{1,29},{... | collective-permute-start | bytes 786440 | tf_op jit(solution)/shard_map/ppermute | solution.py:118
  36.7 0.7 gather_fusion
  37.4 0.8 unpack_near.1
  38.2 13.7 %attn_forward.1 = (bf16[4096,256]{1,0:T(8,128)(2,1)S(1)}, bf16[4096,256]{1,0:T(8,128)(2,1)}, bf16[4096,256]{1,0:T(8,128)(2,1)}, f32[4096,128]{1,0:T(8,128)}, bf1...) custom-call(s32[6]{0:T(128)S(1)} %pad_add_fusion.place.refs_0_, ...), custom_call_target="tpu_custom_call" | custom-call | flops 1000000 | bytes 10000 | tf_op jit(solution)/shard_map/attn_forward/pallas_call | solution.py:334
  52.0 18.0 %ffn_forward.1 = (bf16[4096,256]{1,0:T(8,128)(2,1)}, bf16[4096,256]{1,0:T(8,128)(2,1)}, f32[4096,128]{1,0:T(8,128)}, bf16[4096,1024]{1,0:T(8,128)(2,1)}, bf16[40...) custom-call(s32[6]{0:T(128)S(1)} %pad_add_fusion.place.refs_0_, ...), custom_call_target="tpu_custom_call" | custom-call | flops 1000000 | bytes 10000 | tf_op jit(solution)/shard_map/ffn_forward/pallas_call | solution.py:459
  70.1 1.6 collective-permute-done.8.above.refs_1_
  71.7 13.8 %conv_weight.1 = (bf16[9,2,256,256]{3,2,1,0:T(8,128)(2,1)S(1)}, f32[8,256]{1,0:T(8,128)S(1)}) custom-call(s32[6]{0:T(128)S(1)} %pad_add_fusion.place.refs_0_, bf16[2,6,128,256]{3,2,1,0:T(8,128)(2,1)} %collective-permute-done.8.above.refs_1_, bf16[2,16,128,256]{3,2,1,0:T(8,128)(2,1)} %own.3, bf16[2,2,128,256]{3,2,1,0:T(8,128)(2,1)} %collective-permute-done.9.below, ...), custom_call_target="tpu_custom_call" | custom-call | flops 20000000000 | bytes 10000000 | tf_op jit(solution)/shard_map/conv_weight/pallas_call | solution.py:1067
  85.5 0.2 constant_dynamic-slice_fusion.1
  85.6 0.4 copy-done.7
  86.1 2.8 %collective-permute-done.10 = bf16[16,144,256]{2,1,0:T(8,128)(2,1)S(1)} collective-permute-done((bf16[16,144,256]{2,1,0:T(8,128)(2,1)S(1)}, bf16[16,144,256]{2,1,0:T(8,128)(2,1)S(1)}, u32[]{:S(2)}, u32[]{:S(2)}) %collective-permute-start.10) | collective-permute-done | bytes 1179680 | tf_op jit(solution)/shard_map/ppermute | solution.py:96
  88.9 1.5 fusion
  90.4 6.9 %all-to-all-start.2 = ((bf16[16,144,256]{2,1,0:T(8,128)(2,1)}), bf16[16,144,256]{2,1,0:T(8,128)(2,1)S(1)}, u32[]{:S(2)}, u32[]{:S(2)}) async-start(bf16[16,144,256]{2,1,0:T(8,128)(2,1)} %fusion), calls=%async_computation.2 | async-start | bytes 2359296 | tf_op jit(solution)/shard_map/all_to_all | solution.py:102
  97.2 40.2 %backward.1 = (f32[2,16,128,256]{3,2,1,0:T(8,128)}, bf16[2,4,128,256]{3,2,1,0:T(8,128)(2,1)}, bf16[128,3840]{1,0:T(8,128)(2,1)}, bf16[128,3840]{1,0:T(8,128)(2,1)}) custom-call(s32[6]{0:T(128)} %copy-done.5, bf16[2,6,128,256]{3,2,1,0:T(8,128)(2,1)} %collective-permute-done.8.above.refs_1_, bf16[2,16,128,256]{3,2,1,0:T(8,128)(2,1)} %own.3, ...), custom_call_target="tpu_custom_call" | custom-call | flops 40000000000 | bytes 10000000 | tf_op jit(solution)/shard_map/backward/pallas_call | solution.py:793
  137.4 0.1 collective-permute-start.12
  137.5 2.8 %collective-permute-done.12 = bf16[16,8,3840]{2,1,0:T(8,128)(2,1)S(1)} collective-permute-done((bf16[16,8,3840]{2,1,0:T(8,128)(2,1)}, bf16[16,8,3840]{2,1,0:T(8,128)(2,1)S(1)}, u32[]{:S(2)}, u32[]{:S(2)}) %collective-permute-start.12) | collective-permute-done | bytes 983072 | tf_op jit(solution)/shard_map/ppermute | solution.py:96
  140.3 2.4 %fusion.1 = bf16[16,8,3840]{2,1,0:T(8,128)(2,1)} fusion(bf16[16,8,3840]{2,1,0:T(8,128)(2,1)S(1)} %collective-permute-done.12, bf16[128,3840]{1,0:T(8,128)(2,1)} %get-tuple-element.102), kind=kLoop, calls=%fused_computation.4 | loop fusion | flops 1966080 | bytes 2949120 | tf_op jit(solution)/shard_map/convert_element_type | solution.py:97
  142.7 7.0 %all-to-all-start.1 = ((bf16[16,8,3840]{2,1,0:T(8,128)(2,1)}), bf16[16,8,3840]{2,1,0:T(8,128)(2,1)S(1)}, u32[]{:S(2)}, u32[]{:S(2)}) async-start(bf16[16,8,3840]{2,1,0:T(8,128)(2,1)} %fusion.1), calls=%async_computation.1 | async-start | bytes 1966080 | tf_op jit(solution)/shard_map/all_to_all | solution.py:102
  149.8 0.8 sum_parts.1
  150.6 2.0 %collective-permute-start.13 = (bf16[2,4,128,256]{3,2,1,0:T(8,128)(2,1)S(1)}, bf16[2,4,128,256]{3,2,1,0:T(8,128)(2,1)S(1)}, u32[]{:S(2)}, u32[]{:S(2)}) collective-permute-start(bf16[2,4,128,256]{3,2,1,0:T(8,128)(2,1)S(1)} %copy-done.11), channel_id=1, source_target_pairs={{0,28},{4,0},{8,4},{12,8},{16,12},{20,16},{24,20},{28,24},{1,29},{... | collective-permute-start | bytes 1572872 | tf_op jit(solution)/shard_map/ppermute | solution.py:118
  152.6 8.9 %conv_data.1 = f32[2,16,128,256]{3,2,1,0:T(8,128)} custom-call(s32[6]{0:T(128)S(1)} %copy-done.6, bf16[2,6,128,256]{3,2,1,0:T(8,128)(2,1)} %collective-permute-done.8.above.refs_1_, bf16[2,16,128,256]{3,2,1,0:T(8,128)(2,1)} %own.3, bf16[2,2,128,256]{3,2,1,0:T(8,128)(2,1)} %collective-permute-done.9.below, bf16[9,2,256,256]{3,2,1,0:T(8,128)(2,1)} %bitcast.12.refs_14_.weight), custom_call_target="tpu_custom_call" | custom-call | flops 10000000000 | bytes 10000000 | tf_op jit(solution)/shard_map/conv_data/pallas_call | solution.py:1067
  161.5 14.8 %conv_forward.1 = bf16[2,16,128,256]{3,2,1,0:T(8,128)(2,1)} custom-call(s32[6]{0:T(128)S(1)} %copy-done.6, bf16[2,16,128,256]{3,2,1,0:T(8,128)(2,1)} %get-tuple-element.94.sums, bf16[2,5,128,256]{3,2,1,0:T(8,128)(2,1)} %copy-done.9, bf16[2,6,128,256]{3,2,1,0:T(8,128)(2,1)} %collective-permute-done.8.above.refs_1_, bf16[2,16,128,256]{3,2,1,0:T(8,128)(2,1)} %hidden.3, ...), custom_call_target="tpu_custom_call" | custom-call | flops 1000000 | bytes 10000 | tf_op jit(solution)/shard_map/conv_forward/pallas_call | solution.py:1188
  176.3 1.1 convert_dynamic-update-slice_fusion
  177.4 0.8 last_sums.1
  178.2 0.2 reverse
  178.3 0.7 slice_bitcast_fusion
  (50 shorter events, 0.2 us)
Async XLA Ops:
  1.5 7.7 %collective-permute-start.2 = (bf16[1,8,3072]{2,1,0:T(8,128)(2,1)S(1)}, bf16[1,8,3072]{2,1,0:T(8,128)(2,1)S(1)}, u32[]{:S(2)}, u32[]{:S(2)}) collective-permute-start(bf16[1,8,3072]{2,1,0:T(8,128)(2,1)S(1)} %bitcast.43), channel_id=1, source_target_pairs={{0,3},{1,2},{2,1},{3,0},{4,7},{5,6},{6,5},{7,4},{8,11},{9,10},{10,... | collective-permute-start | bytes 147464 | tf_op jit(solution)/shard_map/ppermute | solution.py:76
  6.6 5.0 %collective-permute-start.1 = (bf16[1,8,3072]{2,1,0:T(8,128)(2,1)S(1)}, bf16[1,8,3072]{2,1,0:T(8,128)(2,1)S(1)}, u32[]{:S(2)}, u32[]{:S(2)}) collective-permute-start(bf16[1,8,3072]{2,1,0:T(8,128)(2,1)S(1)} %bitcast.44), channel_id=1, source_target_pairs={{0,2},{1,3},{2,0},{3,1},{4,6},{5,7},{6,4},{7,5},{8,10},{9,11},{10,... | collective-permute-start | bytes 147464 | tf_op jit(solution)/shard_map/ppermute | solution.py:76
  6.6 5.0 %collective-permute-start = (bf16[1,8,3072]{2,1,0:T(8,128)(2,1)S(1)}, bf16[1,8,3072]{2,1,0:T(8,128)(2,1)S(1)}, u32[]{:S(2)}, u32[]{:S(2)}) collective-permute-start(bf16[1,8,3072]{2,1,0:T(8,128)(2,1)S(1)} %bitcast.45), channel_id=1, source_target_pairs={{0,1},{1,0},{2,3},{3,2},{4,5},{5,4},{6,7},{7,6},{8,9},{9,8},{10,11... | collective-permute-start | bytes 147464 | tf_op jit(solution)/shard_map/ppermute | solution.py:76
  8.3 18.0 %collective-permute-start.6 = (bf16[2,4,128,256]{3,2,1,0:T(8,128)(2,1)S(1)}, bf16[2,4,128,256]{3,2,1,0:T(8,128)(2,1)}, u32[]{:S(2)}, u32[]{:S(2)}) collective-permute-start(bf16[2,4,128,256]{3,2,1,0:T(8,128)(2,1)S(1)} %slice.22), channel_id=1, source_target_pairs={{0,4},{4,8},{8,12},{12,16},{16,20},{20,24},{24,28},{28,0},{1,5},{5... | collective-permute-start | bytes 1572872 | tf_op jit(solution)/shard_map/ppermute | solution.py:118
  9.2 62.5 %copy-start.5 = (s32[6]{0:T(128)}, s32[6]{0:T(128)S(1)}, u32[]{:S(2)}) copy-start(s32[6]{0:T(128)S(1)} %pad_add_fusion.place.refs_0_) | copy-start | bytes 76
  11.6 14.7 %collective-permute-start.5 = (bf16[4,8,3072]{2,1,0:T(8,128)(2,1)S(1)}, bf16[4,8,3072]{2,1,0:T(8,128)(2,1)S(1)}, u32[]{:S(2)}, u32[]{:S(2)}) collective-permute-start(bf16[4,8,3072]{2,1,0:T(8,128)(2,1)S(1)} %pad_maximum_fusion.2), channel_id=1, source_target_pairs={{0,24},{1,25},{2,26},{3,27},{4,28},{5,29},{6,30},{7,31},{8,16},{9,... | collective-permute-start | bytes 589832 | tf_op jit(solution)/shard_map/ppermute | solution.py:76
  14.1 12.2 %collective-permute-start.4 = (bf16[4,8,3072]{2,1,0:T(8,128)(2,1)S(1)}, bf16[4,8,3072]{2,1,0:T(8,128)(2,1)S(1)}, u32[]{:S(2)}, u32[]{:S(2)}) collective-permute-start(bf16[4,8,3072]{2,1,0:T(8,128)(2,1)S(1)} %pad_maximum_fusion.2), channel_id=1, source_target_pairs={{0,16},{1,17},{2,18},{3,19},{4,20},{5,21},{6,22},{7,23},{8,24},{9,... | collective-permute-start | bytes 589832 | tf_op jit(solution)/shard_map/ppermute | solution.py:76
  14.6 10.1 %collective-permute-start.3 = (bf16[4,8,3072]{2,1,0:T(8,128)(2,1)S(1)}, bf16[4,8,3072]{2,1,0:T(8,128)(2,1)S(1)}, u32[]{:S(2)}, u32[]{:S(2)}) collective-permute-start(bf16[4,8,3072]{2,1,0:T(8,128)(2,1)S(1)} %pad_maximum_fusion.2), channel_id=1, source_target_pairs={{0,8},{1,9},{2,10},{3,11},{4,12},{5,13},{6,14},{7,15},{8,0},{9,1},... | collective-permute-start | bytes 589832 | tf_op jit(solution)/shard_map/ppermute | solution.py:76
  15.2 3.5 %copy-start.10 = (f32[225,8]{0,1:T(8,128)S(1)}, f32[225,8]{0,1:T(8,128)}, u32[]{:S(2)}) copy-start(f32[225,8]{0,1:T(8,128)} %param.30) | copy-start | bytes 21604
  15.2 4.2 %slice-start = ((bf16[2,16,128,256]{3,2,1,0:T(8,128)(2,1)}), bf16[2,1,128,256]{3,2,1,0:T(8,128)(2,1)S(1)}, s32[]{:S(2)}) async-start(bf16[2,16,128,256]{3,2,1,0:T(8,128)(2,1)} %own.3), calls=%async_computation.3 | async-start | bytes 262144 | tf_op jit(solution)/shard_map/slice | solution.py:1253
  15.2 4.9 %slice-start.1 = ((bf16[2,16,128,256]{3,2,1,0:T(8,128)(2,1)}), bf16[2,5,128,256]{3,2,1,0:T(8,128)(2,1)S(1)}, s32[]{:S(2)}) async-start(bf16[2,16,128,256]{3,2,1,0:T(8,128)(2,1)} %own.3), calls=%async_computation.4 | async-start | bytes 1310720 | tf_op jit(solution)/shard_map/slice | solution.py:1252
  26.3 2.4 %collective-permute-start.7 = (bf16[16,8,3072]{2,1,0:T(8,128)(2,1)S(1)}, bf16[16,8,3072]{2,1,0:T(8,128)(2,1)S(1)}, u32[]{:S(2)}, u32[]{:S(2)}) collective-permute-start(bf16[16,8,3072]{2,1,0:T(8,128)(2,1)S(1)} %constant_dynamic-update-slice_fusion), channel_id=1, source_target_pairs={{0,4},{1,5},{2,6},{3,7},{4,0},{5,1},{6,2},{7,3},{8,12},{9,13},{10,... | collective-permute-start | bytes 2359304 | tf_op jit(solution)/shard_map/ppermute | solution.py:76
  28.7 7.9 %copy-start.8 = (s32[32]{0:T(128)S(1)}, s32[32]{0:T(128)}, u32[]{:S(2)}) copy-start(s32[32]{0:T(128)} %constant.55.clone) | copy-start | bytes 388
  28.8 61.6 %all-to-all-start = ((bf16[32,144,256]{2,1,0:T(8,128)(2,1)}), bf16[32,144,256]{2,1,0:T(8,128)(2,1)}, u32[]{:S(2)}, u32[]{:S(2)}) async-start(bf16[32,144,256]{2,1,0:T(8,128)(2,1)} %make_copies.1), calls=%async_computation | async-start | bytes 4718592 | tf_op jit(solution)/shard_map/all_to_all | solution.py:106
  34.0 37.7 %collective-permute-start.8 = (bf16[2,6,128,256]{3,2,1,0:T(8,128)(2,1)}, bf16[2,6,128,256]{3,2,1,0:T(8,128)(2,1)}, u32[]{:S(2)}, u32[]{:S(2)}) collective-permute-start(bf16[2,6,128,256]{3,2,1,0:T(8,128)(2,1)} %pad_maximum_fusion), channel_id=1, source_target_pairs={{0,4},{4,8},{8,12},{12,16},{16,20},{20,24},{24,28},{28,0},{1,5},{5... | collective-permute-start | bytes 2359304 | tf_op jit(solution)/shard_map/ppermute | solution.py:118
  34.2 35.9 %collective-permute-start.9 = (bf16[2,2,128,256]{3,2,1,0:T(8,128)(2,1)}, bf16[2,2,128,256]{3,2,1,0:T(8,128)(2,1)}, u32[]{:S(2)}, u32[]{:S(2)}) collective-permute-start(bf16[2,2,128,256]{3,2,1,0:T(8,128)(2,1)} %pad_maximum_fusion.1), channel_id=1, source_target_pairs={{0,28},{4,0},{8,4},{12,8},{16,12},{20,16},{24,20},{28,24},{1,29},{... | collective-permute-start | bytes 786440 | tf_op jit(solution)/shard_map/ppermute | solution.py:118
  38.2 13.8 %copy-start.3 = (bf16[256,768]{1,0:T(8,128)(2,1)}, bf16[256,768]{1,0:T(8,128)(2,1)S(1)}, u32[]{:S(2)}) copy-start(bf16[256,768]{1,0:T(8,128)(2,1)S(1)} %get-tuple-element.76.weight.refs_19_) | copy-start | bytes 1179652
  38.2 13.8 %copy-start.1 = (bf16[256,1024]{1,0:T(8,128)(2,1)}, bf16[256,1024]{1,0:T(8,128)(2,1)S(1)}, u32[]{:S(2)}) copy-start(bf16[256,1024]{1,0:T(8,128)(2,1)S(1)} %get-tuple-element.80.up_w.refs_17_) | copy-start | bytes 1572868
  38.2 13.8 %copy-start.2 = (bf16[1024,256]{1,0:T(8,128)(2,1)}, bf16[1024,256]{1,0:T(8,128)(2,1)S(1)}, u32[]{:S(2)}) copy-start(bf16[1024,256]{1,0:T(8,128)(2,1)S(1)} %get-tuple-element.81.down_w.refs_18_) | copy-start | bytes 1572868
  38.2 13.8 %copy-start.4 = (bf16[256,256]{1,0:T(8,128)(2,1)}, bf16[256,256]{1,0:T(8,128)(2,1)S(1)}, u32[]{:S(2)}) copy-start(bf16[256,256]{1,0:T(8,128)(2,1)S(1)} %get-tuple-element.79.out_w.refs_15_) | copy-start | bytes 393220
  52.0 18.1 %copy-start = (bf16[4096,256]{1,0:T(8,128)(2,1)}, bf16[4096,256]{1,0:T(8,128)(2,1)S(1)}, u32[]{:S(2)}) copy-start(bf16[4096,256]{1,0:T(8,128)(2,1)S(1)} %get-tuple-element.78.mix.refs_8_) | copy-start | bytes 6291460
  85.5 0.6 copy-start.7
  86.1 2.8 %collective-permute-start.10 = (bf16[16,144,256]{2,1,0:T(8,128)(2,1)S(1)}, bf16[16,144,256]{2,1,0:T(8,128)(2,1)S(1)}, u32[]{:S(2)}, u32[]{:S(2)}) collective-permute-start(bf16[16,144,256]{2,1,0:T(8,128)(2,1)S(1)} %bitcast.47), channel_id=1, source_target_pairs={{0,4},{4,0},{8,12},{12,8},{16,20},{20,16},{24,28},{28,24},{1,5},{5... | collective-permute-start | bytes 3538952 | tf_op jit(solution)/shard_map/ppermute | solution.py:96
  90.4 47.1 %collective-permute-start.11 = (bf16[2,5,128,256]{3,2,1,0:T(8,128)(2,1)}, bf16[2,5,128,256]{3,2,1,0:T(8,128)(2,1)S(1)}, u32[]{:S(2)}, u32[]{:S(2)}) collective-permute-start(bf16[2,5,128,256]{3,2,1,0:T(8,128)(2,1)} %get-tuple-element.101), channel_id=1, source_target_pairs={{0,28},{4,0},{8,4},{12,8},{16,12},{20,16},{24,20},{28,24},{1,29},{... | collective-permute-start | bytes 1966088 | tf_op jit(solution)/shard_map/ppermute | solution.py:118
  90.4 52.4 %all-to-all-start.2 = ((bf16[16,144,256]{2,1,0:T(8,128)(2,1)}), bf16[16,144,256]{2,1,0:T(8,128)(2,1)S(1)}, u32[]{:S(2)}, u32[]{:S(2)}) async-start(bf16[16,144,256]{2,1,0:T(8,128)(2,1)} %fusion), calls=%async_computation.2 | async-start | bytes 2359296 | tf_op jit(solution)/shard_map/all_to_all | solution.py:102
  137.4 5.3 %copy-start.9 = (bf16[2,5,128,256]{3,2,1,0:T(8,128)(2,1)}, bf16[2,5,128,256]{3,2,1,0:T(8,128)(2,1)S(1)}, u32[]{:S(2)}) copy-start(bf16[2,5,128,256]{3,2,1,0:T(8,128)(2,1)S(1)} %collective-permute-done.11.sums_below) | copy-start | bytes 1966084
  137.4 2.8 %collective-permute-start.12 = (bf16[16,8,3840]{2,1,0:T(8,128)(2,1)}, bf16[16,8,3840]{2,1,0:T(8,128)(2,1)S(1)}, u32[]{:S(2)}, u32[]{:S(2)}) collective-permute-start(bf16[16,8,3840]{2,1,0:T(8,128)(2,1)} %bitcast.59), channel_id=1, source_target_pairs={{0,4},{4,0},{8,12},{12,8},{16,20},{20,16},{24,28},{28,24},{1,5},{5... | collective-permute-start | bytes 2949128 | tf_op jit(solution)/shard_map/ppermute | solution.py:96
  142.7 7.9 %copy-start.11 = (bf16[2,4,128,256]{3,2,1,0:T(8,128)(2,1)S(1)}, bf16[2,4,128,256]{3,2,1,0:T(8,128)(2,1)}, u32[]{:S(2)}) copy-start(bf16[2,4,128,256]{3,2,1,0:T(8,128)(2,1)} %get-tuple-element.109) | copy-start | bytes 1572868
  142.7 9.9 %copy-start.6 = (s32[6]{0:T(128)S(1)}, s32[6]{0:T(128)}, u32[]{:S(2)}) copy-start(s32[6]{0:T(128)} %copy-done.5) | copy-start | bytes 76
  142.7 34.6 %all-to-all-start.1 = ((bf16[16,8,3840]{2,1,0:T(8,128)(2,1)}), bf16[16,8,3840]{2,1,0:T(8,128)(2,1)S(1)}, u32[]{:S(2)}, u32[]{:S(2)}) async-start(bf16[16,8,3840]{2,1,0:T(8,128)(2,1)} %fusion.1), calls=%async_computation.1 | async-start | bytes 1966080 | tf_op jit(solution)/shard_map/all_to_all | solution.py:102
  150.6 25.7 %collective-permute-start.13 = (bf16[2,4,128,256]{3,2,1,0:T(8,128)(2,1)S(1)}, bf16[2,4,128,256]{3,2,1,0:T(8,128)(2,1)S(1)}, u32[]{:S(2)}, u32[]{:S(2)}) collective-permute-start(bf16[2,4,128,256]{3,2,1,0:T(8,128)(2,1)S(1)} %copy-done.11), channel_id=1, source_target_pairs={{0,28},{4,0},{8,4},{12,8},{16,12},{20,16},{24,20},{28,24},{1,29},{... | collective-permute-start | bytes 1572872 | tf_op jit(solution)/shard_map/ppermute | solution.py:118

commit v3 on v2

--- a/solution.py
+++ b/solution.py
@@ -16,7 +16,7 @@
 BF = jnp.bfloat16
 F32 = jnp.float32
 MIB = 1024 * 1024
-BACK_MIB = 56
+BACK_MIB = 54
 LOG2E = 1.4426950408889634
 
 
@@ -795,7 +795,8 @@
         grid=(steps,),
         in_specs=in_specs,
         out_specs=out_specs,
-        out_shape=[pltpu.HBM(a, t) for a, t in outs],
+        out_shape=[pltpu.HBM(a, t) for a, t in outs[:2]]
+        + [jax.ShapeDtypeStruct(a, t) for a, t in outs[2:]],
         scratch_shapes=[
             pltpu.VMEM((WIN + 4, columns, 3 * width), BF),
             pltpu.VMEM((3, width, 3 * width), BF),
@@ -1184,7 +1185,7 @@
 
 def conv_forward(place, sums, sums_below, hidden, weight, bias, height):
     samples, rows, columns, width = sums.shape
-    fields = far(sums, sums_below, *hidden)
+    fields = (*near(sums), *far(sums_below, *hidden))
     return pl.pallas_call(
         functools.partial(conv_forward_body, height),
         grid=(samples,),

time: 180 us -> 179 us (level)
  no operation moved by 1% of the time
where the time goes in v3:
time: 179 us; the launch traced here: 178 us
  Pallas kernels  114 us (64%)
  starting transfers between devices  33.4 us (19%)
  waiting for transfers between devices  17 us (9%)
  other arithmetic  7.48 us (4%)
  local copies, waits for them, and re-layouts  5.09 us (3%)
    pallas_call x1, Pallas kernels, backward(): pl.pallas_call(functools.partial(backward_body, height, scale, step_of, b...  40.2 us
    pallas_call x2, Pallas kernels, conv_call(): pl.pallas_call(functools.partial(body, height), grid=(fields[0][1].shape[...  22.6 us
    pallas_call x1, Pallas kernels, ffn_forward(): pl.pallas_call(functools.partial(ffn_forward_body, height, step_of), grid...  18 us
    pallas_call x1, Pallas kernels, conv_forward(): pl.pallas_call(functools.partial(conv_forward_body, height), grid=(sample...  14 us
    all_to_all x2, starting transfers between devices, add_pairs(): lax.all_to_all(a, AXES, 0, 0, axis_index_groups=groups, tiled=True)  13.9 us
    pallas_call x1, Pallas kernels, attn_forward(): pl.pallas_call(functools.partial(attn_forward_body, height, scale, step_o...  13.7 us
    ppermute x7, waiting for transfers between devices, gather_steps(): lax.ppermute(held, AXES, [(i, i ^ mask) for i in range(devices)])  9.72 us
    ppermute x7, starting transfers between devices, gather_steps(): lax.ppermute(held, AXES, [(i, i ^ mask) for i in range(devices)])  9.51 us
  transfers between devices with their start and end apart: 17, of which 7 were waited for; matrix products, arithmetic and copies ran while one was open for 6% of the time, Pallas kernels for 63%

profile of v3, /device:TPU:0, one launch (start us, length us, event | category | flops | bytes accessed | tf_op | source)
XLA Modules:
  0.0 178.1 jit_solution(3400482713609234546)
XLA Ops:
  0.7 0.8 pack_near.1
  1.5 5.1 %collective-permute-start.2 = (bf16[1,8,3072]{2,1,0:T(8,128)(2,1)S(1)}, bf16[1,8,3072]{2,1,0:T(8,128)(2,1)S(1)}, u32[]{:S(2)}, u32[]{:S(2)}) collective-permute-start(bf16[1,8,3072]{2,1,0:T(8,128)(2,1)S(1)} %bitcast.43), channel_id=1, source_target_pairs={{0,3},{1,2},{2,1},{3,0},{4,7},{5,6},{6,5},{7,4},{8,11},{9,10},{10,... | collective-permute-start | bytes 147464 | tf_op jit(solution)/shard_map/ppermute | solution.py:76
  6.6 0.6 collective-permute-start
  7.2 1.1 slice.22
  8.3 0.1 collective-permute-start.6
  8.4 0.8 pad_add_fusion.place.refs_0_
  9.2 2.4 %collective-permute-done.1 = bf16[1,8,3072]{2,1,0:T(8,128)(2,1)S(1)} collective-permute-done((bf16[1,8,3072]{2,1,0:T(8,128)(2,1)S(1)}, bf16[1,8,3072]{2,1,0:T(8,128)(2,1)S(1)}, u32[]{:S(2)}, u32[]{:S(2)}) %collective-permute-start.1) | collective-permute-done | bytes 49184 | tf_op jit(solution)/shard_map/ppermute | solution.py:76
  11.6 2.5 %collective-permute-start.5 = (bf16[4,8,3072]{2,1,0:T(8,128)(2,1)S(1)}, bf16[4,8,3072]{2,1,0:T(8,128)(2,1)S(1)}, u32[]{:S(2)}, u32[]{:S(2)}) collective-permute-start(bf16[4,8,3072]{2,1,0:T(8,128)(2,1)S(1)} %pad_maximum_fusion.2), channel_id=1, source_target_pairs={{0,24},{1,25},{2,26},{3,27},{4,28},{5,29},{6,30},{7,31},{8,16},{9,... | collective-permute-start | bytes 589832 | tf_op jit(solution)/shard_map/ppermute | solution.py:76
  14.1 0.5 collective-permute-start.4
  14.6 0.5 collective-permute-start.3
  15.2 1.1 fusion.3
  16.2 2.5 %make_copies.1 = bf16[32,144,256]{2,1,0:T(8,128)(2,1)} custom-call(f32[144,256]{1,0:T(8,128)} %x.2), custom_call_target="tpu_custom_call" | custom-call | flops 1000000 | bytes 10000 | tf_op jit(solution)/shard_map/make_copies/pallas_call | solution.py:964
  18.7 0.6 pad.4.table
  19.3 0.7 pad_maximum_fusion.1
  20.1 1.0 pad_maximum_fusion
  21.0 3.7 %collective-permute-done.3 = bf16[4,8,3072]{2,1,0:T(8,128)(2,1)S(1)} collective-permute-done((bf16[4,8,3072]{2,1,0:T(8,128)(2,1)S(1)}, bf16[4,8,3072]{2,1,0:T(8,128)(2,1)S(1)}, u32[]{:S(2)}, u32[]{:S(2)}) %collective-permute-start.3) | collective-permute-done | bytes 196640 | tf_op jit(solution)/shard_map/ppermute | solution.py:76
  24.7 1.5 collective-permute-done.4
  26.3 0.2 collective-permute-start.7
  26.6 0.1 constant_dynamic-update-slice_fusion.8
  26.6 2.1 %collective-permute-done.7 = bf16[16,8,3072]{2,1,0:T(8,128)(2,1)S(1)} collective-permute-done((bf16[16,8,3072]{2,1,0:T(8,128)(2,1)S(1)}, bf16[16,8,3072]{2,1,0:T(8,128)(2,1)S(1)}, u32[]{:S(2)}, u32[]{:S(2)}) %collective-permute-start.7) | collective-permute-done | bytes 786464 | tf_op jit(solution)/shard_map/ppermute | solution.py:76
  28.7 0.1 constant_dynamic-update-slice_fusion.7.held
  28.8 5.2 %all-to-all-start = ((bf16[32,144,256]{2,1,0:T(8,128)(2,1)}), bf16[32,144,256]{2,1,0:T(8,128)(2,1)}, u32[]{:S(2)}, u32[]{:S(2)}) async-start(bf16[32,144,256]{2,1,0:T(8,128)(2,1)} %make_copies.1), calls=%async_computation | async-start | bytes 4718592 | tf_op jit(solution)/shard_map/all_to_all | solution.py:106
  34.0 0.2 collective-permute-start.8
  34.2 2.5 %collective-permute-start.9 = (bf16[2,2,128,256]{3,2,1,0:T(8,128)(2,1)}, bf16[2,2,128,256]{3,2,1,0:T(8,128)(2,1)}, u32[]{:S(2)}, u32[]{:S(2)}) collective-permute-start(bf16[2,2,128,256]{3,2,1,0:T(8,128)(2,1)} %pad_maximum_fusion.1), channel_id=1, source_target_pairs={{0,28},{4,0},{8,4},{12,8},{16,12},{20,16},{24,20},{28,24},{1,29},{... | collective-permute-start | bytes 786440 | tf_op jit(solution)/shard_map/ppermute | solution.py:118
  36.7 0.7 gather_fusion
  37.4 0.8 unpack_near.1
  38.2 13.7 %attn_forward.1 = (bf16[4096,256]{1,0:T(8,128)(2,1)S(1)}, bf16[4096,256]{1,0:T(8,128)(2,1)}, bf16[4096,256]{1,0:T(8,128)(2,1)}, f32[4096,128]{1,0:T(8,128)}, bf1...) custom-call(s32[6]{0:T(128)S(1)} %pad_add_fusion.place.refs_0_, ...), custom_call_target="tpu_custom_call" | custom-call | flops 1000000 | bytes 10000 | tf_op jit(solution)/shard_map/attn_forward/pallas_call | solution.py:334
  52.0 18.0 %ffn_forward.1 = (bf16[4096,256]{1,0:T(8,128)(2,1)}, bf16[4096,256]{1,0:T(8,128)(2,1)}, f32[4096,128]{1,0:T(8,128)}, bf16[4096,1024]{1,0:T(8,128)(2,1)}, bf16[40...) custom-call(s32[6]{0:T(128)S(1)} %pad_add_fusion.place.refs_0_, ...), custom_call_target="tpu_custom_call" | custom-call | flops 1000000 | bytes 10000 | tf_op jit(solution)/shard_map/ffn_forward/pallas_call | solution.py:459
  70.0 1.6 collective-permute-done.8.above.refs_1_
  71.7 13.8 %conv_weight.1 = (bf16[9,2,256,256]{3,2,1,0:T(8,128)(2,1)S(1)}, f32[8,256]{1,0:T(8,128)S(1)}) custom-call(s32[6]{0:T(128)S(1)} %pad_add_fusion.place.refs_0_, bf16[2,6,128,256]{3,2,1,0:T(8,128)(2,1)} %collective-permute-done.8.above.refs_1_, bf16[2,16,128,256]{3,2,1,0:T(8,128)(2,1)} %own.3, bf16[2,2,128,256]{3,2,1,0:T(8,128)(2,1)} %collective-permute-done.9.below, ...), custom_call_target="tpu_custom_call" | custom-call | flops 20000000000 | bytes 10000000 | tf_op jit(solution)/shard_map/conv_weight/pallas_call | solution.py:1068
  85.5 0.2 constant_dynamic-slice_fusion.1
  85.6 0.4 copy-done.8
  86.1 2.8 %collective-permute-done.10 = bf16[16,144,256]{2,1,0:T(8,128)(2,1)S(1)} collective-permute-done((bf16[16,144,256]{2,1,0:T(8,128)(2,1)S(1)}, bf16[16,144,256]{2,1,0:T(8,128)(2,1)S(1)}, u32[]{:S(2)}, u32[]{:S(2)}) %collective-permute-start.10) | collective-permute-done | bytes 1179680 | tf_op jit(solution)/shard_map/ppermute | solution.py:96
  88.9 1.5 fusion
  90.4 6.9 %all-to-all-start.2 = ((bf16[16,144,256]{2,1,0:T(8,128)(2,1)}), bf16[16,144,256]{2,1,0:T(8,128)(2,1)S(1)}, u32[]{:S(2)}, u32[]{:S(2)}) async-start(bf16[16,144,256]{2,1,0:T(8,128)(2,1)} %fusion), calls=%async_computation.2 | async-start | bytes 2359296 | tf_op jit(solution)/shard_map/all_to_all | solution.py:102
  97.2 40.2 %backward.1 = (f32[2,16,128,256]{3,2,1,0:T(8,128)}, bf16[2,4,128,256]{3,2,1,0:T(8,128)(2,1)}, bf16[128,3840]{1,0:T(8,128)(2,1)}, bf16[128,3840]{1,0:T(8,128)(2,1)}) custom-call(s32[6]{0:T(128)} %copy-done.6, bf16[2,6,128,256]{3,2,1,0:T(8,128)(2,1)} %collective-permute-done.8.above.refs_1_, bf16[2,16,128,256]{3,2,1,0:T(8,128)(2,1)} %own.3, ...), custom_call_target="tpu_custom_call" | custom-call | flops 40000000000 | bytes 10000000 | tf_op jit(solution)/shard_map/backward/pallas_call | solution.py:793
  137.4 0.1 collective-permute-start.12
  137.5 2.8 %collective-permute-done.12 = bf16[16,8,3840]{2,1,0:T(8,128)(2,1)S(1)} collective-permute-done((bf16[16,8,3840]{2,1,0:T(8,128)(2,1)}, bf16[16,8,3840]{2,1,0:T(8,128)(2,1)S(1)}, u32[]{:S(2)}, u32[]{:S(2)}) %collective-permute-start.12) | collective-permute-done | bytes 983072 | tf_op jit(solution)/shard_map/ppermute | solution.py:96
  140.3 2.5 %fusion.1 = bf16[16,8,3840]{2,1,0:T(8,128)(2,1)} fusion(bf16[16,8,3840]{2,1,0:T(8,128)(2,1)S(1)} %collective-permute-done.12, bf16[128,3840]{1,0:T(8,128)(2,1)} %get-tuple-element.102), kind=kLoop, calls=%fused_computation.4 | loop fusion | flops 1966080 | bytes 2949120 | tf_op jit(solution)/shard_map/convert_element_type | solution.py:97
  142.7 7.0 %all-to-all-start.1 = ((bf16[16,8,3840]{2,1,0:T(8,128)(2,1)}), bf16[16,8,3840]{2,1,0:T(8,128)(2,1)S(1)}, u32[]{:S(2)}, u32[]{:S(2)}) async-start(bf16[16,8,3840]{2,1,0:T(8,128)(2,1)} %fusion.1), calls=%async_computation.1 | async-start | bytes 1966080 | tf_op jit(solution)/shard_map/all_to_all | solution.py:102
  149.8 0.8 sum_parts.1
  150.6 2.0 %collective-permute-start.13 = (bf16[2,4,128,256]{3,2,1,0:T(8,128)(2,1)S(1)}, bf16[2,4,128,256]{3,2,1,0:T(8,128)(2,1)S(1)}, u32[]{:S(2)}, u32[]{:S(2)}) collective-permute-start(bf16[2,4,128,256]{3,2,1,0:T(8,128)(2,1)S(1)} %copy-done.12), channel_id=1, source_target_pairs={{0,28},{4,0},{8,4},{12,8},{16,12},{20,16},{24,20},{28,24},{1,29},{... | collective-permute-start | bytes 1572872 | tf_op jit(solution)/shard_map/ppermute | solution.py:118
  152.6 8.9 %conv_data.1 = f32[2,16,128,256]{3,2,1,0:T(8,128)} custom-call(s32[6]{0:T(128)S(1)} %copy-done.7, bf16[2,6,128,256]{3,2,1,0:T(8,128)(2,1)} %collective-permute-done.8.above.refs_1_, bf16[2,16,128,256]{3,2,1,0:T(8,128)(2,1)} %own.3, bf16[2,2,128,256]{3,2,1,0:T(8,128)(2,1)} %collective-permute-done.9.below, bf16[9,2,256,256]{3,2,1,0:T(8,128)(2,1)} %bitcast.12.refs_14_.weight), custom_call_target="tpu_custom_call" | custom-call | flops 10000000000 | bytes 10000000 | tf_op jit(solution)/shard_map/conv_data/pallas_call | solution.py:1068
  161.5 14.0 %conv_forward.1 = bf16[2,16,128,256]{3,2,1,0:T(8,128)(2,1)} custom-call(s32[6]{0:T(128)S(1)} %copy-done.7, bf16[2,16,128,256]{3,2,1,0:T(8,128)(2,1)S(1)} %copy-done.1, bf16[2,5,128,256]{3,2,1,0:T(8,128)(2,1)} %copy-done.10, bf16[2,6,128,256]{3,2,1,0:T(8,128)(2,1)} %collective-permute-done.8.above.refs_1_, bf16[2,16,128,256]{3,2,1,0:T(8,128)(2,1)} %hidden.3, ...), custom_call_target="tpu_custom_call" | custom-call | flops 1000000 | bytes 10000 | tf_op jit(solution)/shard_map/conv_forward/pallas_call | solution.py:1189
  175.4 1.1 convert_dynamic-update-slice_fusion
  176.5 0.8 last_sums.1
  177.3 0.2 reverse
  177.4 0.7 slice_bitcast_fusion
  (52 shorter events, 0.2 us)
Async XLA Ops:
  1.5 7.7 %collective-permute-start.2 = (bf16[1,8,3072]{2,1,0:T(8,128)(2,1)S(1)}, bf16[1,8,3072]{2,1,0:T(8,128)(2,1)S(1)}, u32[]{:S(2)}, u32[]{:S(2)}) collective-permute-start(bf16[1,8,3072]{2,1,0:T(8,128)(2,1)S(1)} %bitcast.43), channel_id=1, source_target_pairs={{0,3},{1,2},{2,1},{3,0},{4,7},{5,6},{6,5},{7,4},{8,11},{9,10},{10,... | collective-permute-start | bytes 147464 | tf_op jit(solution)/shard_map/ppermute | solution.py:76
  6.6 5.0 %collective-permute-start.1 = (bf16[1,8,3072]{2,1,0:T(8,128)(2,1)S(1)}, bf16[1,8,3072]{2,1,0:T(8,128)(2,1)S(1)}, u32[]{:S(2)}, u32[]{:S(2)}) collective-permute-start(bf16[1,8,3072]{2,1,0:T(8,128)(2,1)S(1)} %bitcast.44), channel_id=1, source_target_pairs={{0,2},{1,3},{2,0},{3,1},{4,6},{5,7},{6,4},{7,5},{8,10},{9,11},{10,... | collective-permute-start | bytes 147464 | tf_op jit(solution)/shard_map/ppermute | solution.py:76
  6.6 5.0 %collective-permute-start = (bf16[1,8,3072]{2,1,0:T(8,128)(2,1)S(1)}, bf16[1,8,3072]{2,1,0:T(8,128)(2,1)S(1)}, u32[]{:S(2)}, u32[]{:S(2)}) collective-permute-start(bf16[1,8,3072]{2,1,0:T(8,128)(2,1)S(1)} %bitcast.45), channel_id=1, source_target_pairs={{0,1},{1,0},{2,3},{3,2},{4,5},{5,4},{6,7},{7,6},{8,9},{9,8},{10,11... | collective-permute-start | bytes 147464 | tf_op jit(solution)/shard_map/ppermute | solution.py:76
  8.3 18.0 %collective-permute-start.6 = (bf16[2,4,128,256]{3,2,1,0:T(8,128)(2,1)S(1)}, bf16[2,4,128,256]{3,2,1,0:T(8,128)(2,1)}, u32[]{:S(2)}, u32[]{:S(2)}) collective-permute-start(bf16[2,4,128,256]{3,2,1,0:T(8,128)(2,1)S(1)} %slice.22), channel_id=1, source_target_pairs={{0,4},{4,8},{8,12},{12,16},{16,20},{20,24},{24,28},{28,0},{1,5},{5... | collective-permute-start | bytes 1572872 | tf_op jit(solution)/shard_map/ppermute | solution.py:118
  9.2 62.5 %copy-start.6 = (s32[6]{0:T(128)}, s32[6]{0:T(128)S(1)}, u32[]{:S(2)}) copy-start(s32[6]{0:T(128)S(1)} %pad_add_fusion.place.refs_0_) | copy-start | bytes 76
  11.6 14.7 %collective-permute-start.5 = (bf16[4,8,3072]{2,1,0:T(8,128)(2,1)S(1)}, bf16[4,8,3072]{2,1,0:T(8,128)(2,1)S(1)}, u32[]{:S(2)}, u32[]{:S(2)}) collective-permute-start(bf16[4,8,3072]{2,1,0:T(8,128)(2,1)S(1)} %pad_maximum_fusion.2), channel_id=1, source_target_pairs={{0,24},{1,25},{2,26},{3,27},{4,28},{5,29},{6,30},{7,31},{8,16},{9,... | collective-permute-start | bytes 589832 | tf_op jit(solution)/shard_map/ppermute | solution.py:76
  14.1 12.2 %collective-permute-start.4 = (bf16[4,8,3072]{2,1,0:T(8,128)(2,1)S(1)}, bf16[4,8,3072]{2,1,0:T(8,128)(2,1)S(1)}, u32[]{:S(2)}, u32[]{:S(2)}) collective-permute-start(bf16[4,8,3072]{2,1,0:T(8,128)(2,1)S(1)} %pad_maximum_fusion.2), channel_id=1, source_target_pairs={{0,16},{1,17},{2,18},{3,19},{4,20},{5,21},{6,22},{7,23},{8,24},{9,... | collective-permute-start | bytes 589832 | tf_op jit(solution)/shard_map/ppermute | solution.py:76
  14.6 10.1 %collective-permute-start.3 = (bf16[4,8,3072]{2,1,0:T(8,128)(2,1)S(1)}, bf16[4,8,3072]{2,1,0:T(8,128)(2,1)S(1)}, u32[]{:S(2)}, u32[]{:S(2)}) collective-permute-start(bf16[4,8,3072]{2,1,0:T(8,128)(2,1)S(1)} %pad_maximum_fusion.2), channel_id=1, source_target_pairs={{0,8},{1,9},{2,10},{3,11},{4,12},{5,13},{6,14},{7,15},{8,0},{9,1},... | collective-permute-start | bytes 589832 | tf_op jit(solution)/shard_map/ppermute | solution.py:76
  15.2 3.5 %copy-start.11 = (f32[225,8]{0,1:T(8,128)S(1)}, f32[225,8]{0,1:T(8,128)}, u32[]{:S(2)}) copy-start(f32[225,8]{0,1:T(8,128)} %param.30) | copy-start | bytes 21604
  15.2 4.2 %slice-start = ((bf16[2,16,128,256]{3,2,1,0:T(8,128)(2,1)}), bf16[2,1,128,256]{3,2,1,0:T(8,128)(2,1)S(1)}, s32[]{:S(2)}) async-start(bf16[2,16,128,256]{3,2,1,0:T(8,128)(2,1)} %own.3), calls=%async_computation.3 | async-start | bytes 262144 | tf_op jit(solution)/shard_map/slice | solution.py:1254
  15.2 4.9 %slice-start.1 = ((bf16[2,16,128,256]{3,2,1,0:T(8,128)(2,1)}), bf16[2,5,128,256]{3,2,1,0:T(8,128)(2,1)S(1)}, s32[]{:S(2)}) async-start(bf16[2,16,128,256]{3,2,1,0:T(8,128)(2,1)} %own.3), calls=%async_computation.4 | async-start | bytes 1310720 | tf_op jit(solution)/shard_map/slice | solution.py:1253
  26.3 2.4 %collective-permute-start.7 = (bf16[16,8,3072]{2,1,0:T(8,128)(2,1)S(1)}, bf16[16,8,3072]{2,1,0:T(8,128)(2,1)S(1)}, u32[]{:S(2)}, u32[]{:S(2)}) collective-permute-start(bf16[16,8,3072]{2,1,0:T(8,128)(2,1)S(1)} %constant_dynamic-update-slice_fusion), channel_id=1, source_target_pairs={{0,4},{1,5},{2,6},{3,7},{4,0},{5,1},{6,2},{7,3},{8,12},{9,13},{10,... | collective-permute-start | bytes 2359304 | tf_op jit(solution)/shard_map/ppermute | solution.py:76
  28.7 7.9 %copy-start.9 = (s32[32]{0:T(128)S(1)}, s32[32]{0:T(128)}, u32[]{:S(2)}) copy-start(s32[32]{0:T(128)} %constant.55.clone) | copy-start | bytes 388
  28.8 61.6 %all-to-all-start = ((bf16[32,144,256]{2,1,0:T(8,128)(2,1)}), bf16[32,144,256]{2,1,0:T(8,128)(2,1)}, u32[]{:S(2)}, u32[]{:S(2)}) async-start(bf16[32,144,256]{2,1,0:T(8,128)(2,1)} %make_copies.1), calls=%async_computation | async-start | bytes 4718592 | tf_op jit(solution)/shard_map/all_to_all | solution.py:106
  34.0 37.7 %collective-permute-start.8 = (bf16[2,6,128,256]{3,2,1,0:T(8,128)(2,1)}, bf16[2,6,128,256]{3,2,1,0:T(8,128)(2,1)}, u32[]{:S(2)}, u32[]{:S(2)}) collective-permute-start(bf16[2,6,128,256]{3,2,1,0:T(8,128)(2,1)} %pad_maximum_fusion), channel_id=1, source_target_pairs={{0,4},{4,8},{8,12},{12,16},{16,20},{20,24},{24,28},{28,0},{1,5},{5... | collective-permute-start | bytes 2359304 | tf_op jit(solution)/shard_map/ppermute | solution.py:118
  34.2 35.8 %collective-permute-start.9 = (bf16[2,2,128,256]{3,2,1,0:T(8,128)(2,1)}, bf16[2,2,128,256]{3,2,1,0:T(8,128)(2,1)}, u32[]{:S(2)}, u32[]{:S(2)}) collective-permute-start(bf16[2,2,128,256]{3,2,1,0:T(8,128)(2,1)} %pad_maximum_fusion.1), channel_id=1, source_target_pairs={{0,28},{4,0},{8,4},{12,8},{16,12},{20,16},{24,20},{28,24},{1,29},{... | collective-permute-start | bytes 786440 | tf_op jit(solution)/shard_map/ppermute | solution.py:118
  38.2 13.8 %copy-start.4 = (bf16[256,768]{1,0:T(8,128)(2,1)}, bf16[256,768]{1,0:T(8,128)(2,1)S(1)}, u32[]{:S(2)}) copy-start(bf16[256,768]{1,0:T(8,128)(2,1)S(1)} %get-tuple-element.76.weight.refs_19_) | copy-start | bytes 1179652
  38.2 13.8 %copy-start.2 = (bf16[256,1024]{1,0:T(8,128)(2,1)}, bf16[256,1024]{1,0:T(8,128)(2,1)S(1)}, u32[]{:S(2)}) copy-start(bf16[256,1024]{1,0:T(8,128)(2,1)S(1)} %get-tuple-element.80.up_w.refs_17_) | copy-start | bytes 1572868
  38.2 13.8 %copy-start.3 = (bf16[1024,256]{1,0:T(8,128)(2,1)}, bf16[1024,256]{1,0:T(8,128)(2,1)S(1)}, u32[]{:S(2)}) copy-start(bf16[1024,256]{1,0:T(8,128)(2,1)S(1)} %get-tuple-element.81.down_w.refs_18_) | copy-start | bytes 1572868
  38.2 13.8 %copy-start.5 = (bf16[256,256]{1,0:T(8,128)(2,1)}, bf16[256,256]{1,0:T(8,128)(2,1)S(1)}, u32[]{:S(2)}) copy-start(bf16[256,256]{1,0:T(8,128)(2,1)S(1)} %get-tuple-element.79.out_w.refs_15_) | copy-start | bytes 393220
  52.0 18.1 %copy-start = (bf16[4096,256]{1,0:T(8,128)(2,1)}, bf16[4096,256]{1,0:T(8,128)(2,1)S(1)}, u32[]{:S(2)}) copy-start(bf16[4096,256]{1,0:T(8,128)(2,1)S(1)} %get-tuple-element.78.mix.refs_8_) | copy-start | bytes 6291460
  85.5 0.6 copy-start.8
  86.1 2.8 %collective-permute-start.10 = (bf16[16,144,256]{2,1,0:T(8,128)(2,1)S(1)}, bf16[16,144,256]{2,1,0:T(8,128)(2,1)S(1)}, u32[]{:S(2)}, u32[]{:S(2)}) collective-permute-start(bf16[16,144,256]{2,1,0:T(8,128)(2,1)S(1)} %bitcast.47), channel_id=1, source_target_pairs={{0,4},{4,0},{8,12},{12,8},{16,20},{20,16},{24,28},{28,24},{1,5},{5... | collective-permute-start | bytes 3538952 | tf_op jit(solution)/shard_map/ppermute | solution.py:96
  90.4 47.0 %collective-permute-start.11 = (bf16[2,5,128,256]{3,2,1,0:T(8,128)(2,1)}, bf16[2,5,128,256]{3,2,1,0:T(8,128)(2,1)S(1)}, u32[]{:S(2)}, u32[]{:S(2)}) collective-permute-start(bf16[2,5,128,256]{3,2,1,0:T(8,128)(2,1)} %get-tuple-element.101), channel_id=1, source_target_pairs={{0,28},{4,0},{8,4},{12,8},{16,12},{20,16},{24,20},{28,24},{1,29},{... | collective-permute-start | bytes 1966088 | tf_op jit(solution)/shard_map/ppermute | solution.py:118
  90.4 52.4 %all-to-all-start.2 = ((bf16[16,144,256]{2,1,0:T(8,128)(2,1)}), bf16[16,144,256]{2,1,0:T(8,128)(2,1)S(1)}, u32[]{:S(2)}, u32[]{:S(2)}) async-start(bf16[16,144,256]{2,1,0:T(8,128)(2,1)} %fusion), calls=%async_computation.2 | async-start | bytes 2359296 | tf_op jit(solution)/shard_map/all_to_all | solution.py:102
  137.4 5.3 %copy-start.10 = (bf16[2,5,128,256]{3,2,1,0:T(8,128)(2,1)}, bf16[2,5,128,256]{3,2,1,0:T(8,128)(2,1)S(1)}, u32[]{:S(2)}) copy-start(bf16[2,5,128,256]{3,2,1,0:T(8,128)(2,1)S(1)} %collective-permute-done.11.sums_below) | copy-start | bytes 1966084
  137.4 2.8 %collective-permute-start.12 = (bf16[16,8,3840]{2,1,0:T(8,128)(2,1)}, bf16[16,8,3840]{2,1,0:T(8,128)(2,1)S(1)}, u32[]{:S(2)}, u32[]{:S(2)}) collective-permute-start(bf16[16,8,3840]{2,1,0:T(8,128)(2,1)} %bitcast.59), channel_id=1, source_target_pairs={{0,4},{4,0},{8,12},{12,8},{16,20},{20,16},{24,28},{28,24},{1,5},{5... | collective-permute-start | bytes 2949128 | tf_op jit(solution)/shard_map/ppermute | solution.py:96
  142.7 7.9 %copy-start.12 = (bf16[2,4,128,256]{3,2,1,0:T(8,128)(2,1)S(1)}, bf16[2,4,128,256]{3,2,1,0:T(8,128)(2,1)}, u32[]{:S(2)}) copy-start(bf16[2,4,128,256]{3,2,1,0:T(8,128)(2,1)} %get-tuple-element.109) | copy-start | bytes 1572868
  142.7 9.9 %copy-start.7 = (s32[6]{0:T(128)S(1)}, s32[6]{0:T(128)}, u32[]{:S(2)}) copy-start(s32[6]{0:T(128)} %copy-done.6) | copy-start | bytes 76
  142.7 33.8 %all-to-all-start.1 = ((bf16[16,8,3840]{2,1,0:T(8,128)(2,1)}), bf16[16,8,3840]{2,1,0:T(8,128)(2,1)S(1)}, u32[]{:S(2)}, u32[]{:S(2)}) async-start(bf16[16,8,3840]{2,1,0:T(8,128)(2,1)} %fusion.1), calls=%async_computation.1 | async-start | bytes 1966080 | tf_op jit(solution)/shard_map/all_to_all | solution.py:102
  150.6 10.9 %copy-start.1 = (bf16[2,16,128,256]{3,2,1,0:T(8,128)(2,1)S(1)}, bf16[2,16,128,256]{3,2,1,0:T(8,128)(2,1)}, u32[]{:S(2)}) copy-start(bf16[2,16,128,256]{3,2,1,0:T(8,128)(2,1)} %get-tuple-element.94.sums) | copy-start | bytes 6291460
  150.6 24.8 %collective-permute-start.13 = (bf16[2,4,128,256]{3,2,1,0:T(8,128)(2,1)S(1)}, bf16[2,4,128,256]{3,2,1,0:T(8,128)(2,1)S(1)}, u32[]{:S(2)}, u32[]{:S(2)}) collective-permute-start(bf16[2,4,128,256]{3,2,1,0:T(8,128)(2,1)S(1)} %copy-done.12), channel_id=1, source_target_pairs={{0,28},{4,0},{8,4},{12,8},{16,12},{20,16},{24,20},{28,24},{1,29},{... | collective-permute-start | bytes 1572872 | tf_op jit(solution)/shard_map/ppermute | solution.py:118

commit v4 on v3

--- a/solution.py
+++ b/solution.py
@@ -79,7 +79,7 @@
     order = np.zeros(devices, np.int32)
     for place, mask in enumerate(places):
         order[mask] = place
-    return held, jnp.asarray(order)[jnp.arange(devices) ^ device_index()], other
+    return held, jnp.asarray(order), other
 
 
 def scatter_pairs(x):
@@ -860,12 +860,13 @@
     )(*far(qkv, out_w, up, down))
 
 
-def unpack_near_body(order, held, qkv, out_w, up, down):
+def unpack_near_body(place_ref, order, held, qkv, out_w, up, down):
     devices, rows, _ = held.shape
+    me = place_ref[place_ref.shape[0] - 2]
     count = max(16 // rows, 1)
 
     def some(k, _):
-        pieces = [held[order[k * count + n]] for n in range(count)]
+        pieces = [held[order[(k * count + n) ^ me]] for n in range(count)]
         at = 0
         place = pl.ds(pl.multiple_of(k * count * rows, count * rows), count * rows)
         for ref in (qkv, out_w, up):
@@ -884,16 +885,16 @@
     lax.fori_loop(0, devices // count, some, 0, unroll=4)
 
 
-def unpack_near(order, held, weights):
+def unpack_near(place, order, held, weights):
     devices = held.shape[0]
     return pl.pallas_call(
         unpack_near_body,
-        in_specs=[SMEM_SPEC, pl.BlockSpec(memory_space=pltpu.VMEM)],
+        in_specs=[SMEM_SPEC, SMEM_SPEC, pl.BlockSpec(memory_space=pltpu.VMEM)],
         out_shape=[pltpu.VMEM((devices * w.shape[0], w.shape[1]), BF) for w in weights],
         compiler_params=params(24),
         cost_estimate=SMALL_COST,
         name="unpack_near",
-    )(order, held)
+    )(place, order, held)
 
 
 def last_sums_body(parts, down, out_w, up, qkv, *vectors):
@@ -1233,7 +1234,9 @@
     row_place = lax.axis_index("rows")
     row_start = row_place * grid_rows
     place = jnp.concatenate(
-        [(row_start - half)[None].astype(jnp.int32), crop_rows, crop_cols, (row_place % 2)[None]]
+        [
+            (row_start - half)[None], crop_rows, crop_cols, device_index()[None], (row_place % 2)[None],
+        ]
     ).astype(jnp.int32)
 
     hidden_width = up_weight.shape[1]
@@ -1262,7 +1265,7 @@
     conv_full = gather_copies(conv_copies).reshape(-1, width)
 
     qkv_full, output_full, up_full, down_full = unpack_near(
-        order, held, (qkv_weight, output_weight, up_weight, down_weight)
+        place, order, held, (qkv_weight, output_weight, up_weight, down_weight)
     )
     mask = jnp.asarray(head_mask(), BF)
 

time: 179 us -> 179 us (level)
  no operation moved by 1% of the time
where the time goes in v4:
time: 179 us; the launch traced here: 178 us
  Pallas kernels  114 us (64%)
  starting transfers between devices  33.4 us (19%)
  waiting for transfers between devices  17.5 us (10%)
  other arithmetic  6.71 us (4%)
  local copies, waits for them, and re-layouts  5.14 us (3%)
    pallas_call x1, Pallas kernels, backward(): pl.pallas_call(functools.partial(backward_body, height, scale, step_of, b...  40.2 us
    pallas_call x2, Pallas kernels, conv_call(): pl.pallas_call(functools.partial(body, height), grid=(fields[0][1].shape[...  22.6 us
    pallas_call x1, Pallas kernels, ffn_forward(): pl.pallas_call(functools.partial(ffn_forward_body, height, step_of), grid...  18.2 us
    pallas_call x1, Pallas kernels, conv_forward(): pl.pallas_call(functools.partial(conv_forward_body, height), grid=(sample...  14 us
    all_to_all x2, starting transfers between devices, add_pairs(): lax.all_to_all(a, AXES, 0, 0, axis_index_groups=groups, tiled=True)  13.9 us
    pallas_call x1, Pallas kernels, attn_forward(): pl.pallas_call(functools.partial(attn_forward_body, height, scale, step_o...  13.8 us
    ppermute x7, waiting for transfers between devices, gather_steps(): lax.ppermute(held, AXES, [(i, i ^ mask) for i in range(devices)])  9.73 us
    ppermute x7, starting transfers between devices, gather_steps(): lax.ppermute(held, AXES, [(i, i ^ mask) for i in range(devices)])  9.51 us
  transfers between devices with their start and end apart: 17, of which 7 were waited for; matrix products, arithmetic and copies ran while one was open for 6% of the time, Pallas kernels for 63%

profile of v4, /device:TPU:0, one launch (start us, length us, event | category | flops | bytes accessed | tf_op | source)
XLA Modules:
  0.0 178.1 jit_solution(389417522183527937)
XLA Ops:
  0.7 0.8 pack_near.1
  1.5 5.1 %collective-permute-start.2 = (bf16[1,8,3072]{2,1,0:T(8,128)(2,1)S(1)}, bf16[1,8,3072]{2,1,0:T(8,128)(2,1)S(1)}, u32[]{:S(2)}, u32[]{:S(2)}) collective-permute-start(bf16[1,8,3072]{2,1,0:T(8,128)(2,1)S(1)} %bitcast.42), channel_id=1, source_target_pairs={{0,3},{1,2},{2,1},{3,0},{4,7},{5,6},{6,5},{7,4},{8,11},{9,10},{10,... | collective-permute-start | bytes 147464 | tf_op jit(solution)/shard_map/ppermute | solution.py:76
  6.6 0.6 collective-permute-start
  7.2 1.1 slice.22
  8.3 0.1 collective-permute-start.6
  8.4 0.8 concatenate.19.place_ref.place.refs_0_
  9.1 2.4 %collective-permute-done.1 = bf16[1,8,3072]{2,1,0:T(8,128)(2,1)S(1)} collective-permute-done((bf16[1,8,3072]{2,1,0:T(8,128)(2,1)S(1)}, bf16[1,8,3072]{2,1,0:T(8,128)(2,1)S(1)}, u32[]{:S(2)}, u32[]{:S(2)}) %collective-permute-start.1) | collective-permute-done | bytes 49184 | tf_op jit(solution)/shard_map/ppermute | solution.py:76
  11.6 2.5 %collective-permute-start.5 = (bf16[4,8,3072]{2,1,0:T(8,128)(2,1)S(1)}, bf16[4,8,3072]{2,1,0:T(8,128)(2,1)S(1)}, u32[]{:S(2)}, u32[]{:S(2)}) collective-permute-start(bf16[4,8,3072]{2,1,0:T(8,128)(2,1)S(1)} %pad_maximum_fusion.2), channel_id=1, source_target_pairs={{0,24},{1,25},{2,26},{3,27},{4,28},{5,29},{6,30},{7,31},{8,16},{9,... | collective-permute-start | bytes 589832 | tf_op jit(solution)/shard_map/ppermute | solution.py:76
  14.1 0.5 collective-permute-start.4
  14.6 0.5 collective-permute-start.3
  15.2 1.1 fusion.2
  16.2 2.5 %make_copies.1 = bf16[32,144,256]{2,1,0:T(8,128)(2,1)} custom-call(f32[144,256]{1,0:T(8,128)} %x.2), custom_call_target="tpu_custom_call" | custom-call | flops 1000000 | bytes 10000 | tf_op jit(solution)/shard_map/make_copies/pallas_call | solution.py:965
  18.7 0.6 pad.4.table
  19.3 0.7 pad_maximum_fusion.1
  20.1 1.0 pad_maximum_fusion
  21.0 3.7 %collective-permute-done.3 = bf16[4,8,3072]{2,1,0:T(8,128)(2,1)S(1)} collective-permute-done((bf16[4,8,3072]{2,1,0:T(8,128)(2,1)S(1)}, bf16[4,8,3072]{2,1,0:T(8,128)(2,1)S(1)}, u32[]{:S(2)}, u32[]{:S(2)}) %collective-permute-start.3) | collective-permute-done | bytes 196640 | tf_op jit(solution)/shard_map/ppermute | solution.py:76
  24.7 1.5 collective-permute-done.4
  26.3 0.2 collective-permute-start.7
  26.6 0.1 constant_dynamic-update-slice_fusion.8
  26.6 2.1 %collective-permute-done.7 = bf16[16,8,3072]{2,1,0:T(8,128)(2,1)S(1)} collective-permute-done((bf16[16,8,3072]{2,1,0:T(8,128)(2,1)S(1)}, bf16[16,8,3072]{2,1,0:T(8,128)(2,1)S(1)}, u32[]{:S(2)}, u32[]{:S(2)}) %collective-permute-start.7) | collective-permute-done | bytes 786464 | tf_op jit(solution)/shard_map/ppermute | solution.py:76
  28.7 0.1 constant_dynamic-update-slice_fusion.7.held
  28.8 0.0 copy-start.8
  28.8 5.2 %all-to-all-start = ((bf16[32,144,256]{2,1,0:T(8,128)(2,1)}), bf16[32,144,256]{2,1,0:T(8,128)(2,1)}, u32[]{:S(2)}, u32[]{:S(2)}) async-start(bf16[32,144,256]{2,1,0:T(8,128)(2,1)} %make_copies.1), calls=%async_computation | async-start | bytes 4718592 | tf_op jit(solution)/shard_map/all_to_all | solution.py:106
  34.0 0.2 collective-permute-start.8
  34.2 2.5 %collective-permute-start.9 = (bf16[2,2,128,256]{3,2,1,0:T(8,128)(2,1)}, bf16[2,2,128,256]{3,2,1,0:T(8,128)(2,1)}, u32[]{:S(2)}, u32[]{:S(2)}) collective-permute-start(bf16[2,2,128,256]{3,2,1,0:T(8,128)(2,1)} %pad_maximum_fusion.1), channel_id=1, source_target_pairs={{0,28},{4,0},{8,4},{12,8},{16,12},{20,16},{24,20},{28,24},{1,29},{... | collective-permute-start | bytes 786440 | tf_op jit(solution)/shard_map/ppermute | solution.py:118
  36.7 0.8 unpack_near.1
  37.5 13.8 %attn_forward.1 = (bf16[4096,256]{1,0:T(8,128)(2,1)S(1)}, bf16[4096,256]{1,0:T(8,128)(2,1)}, bf16[4096,256]{1,0:T(8,128)(2,1)}, f32[4096,128]{1,0:T(8,128)}, bf1...) custom-call(s32[7]{0:T(128)S(1)} %concatenate.19.place_ref.place.refs_0_, ...), custom_call_target="tpu_custom_call" | custom-call | flops 1000000 | bytes 10000 | tf_op jit(solution)/shard_map/attn_forward/pallas_call | solution.py:334
  51.4 18.2 %ffn_forward.1 = (bf16[4096,256]{1,0:T(8,128)(2,1)}, bf16[4096,256]{1,0:T(8,128)(2,1)}, f32[4096,128]{1,0:T(8,128)}, bf16[4096,1024]{1,0:T(8,128)(2,1)}, bf16[40...) custom-call(s32[7]{0:T(128)S(1)} %concatenate.19.place_ref.place.refs_0_, ...), custom_call_target="tpu_custom_call" | custom-call | flops 1000000 | bytes 10000 | tf_op jit(solution)/shard_map/ffn_forward/pallas_call | solution.py:459
  69.6 2.1 %collective-permute-done.8.above.refs_1_ = bf16[2,6,128,256]{3,2,1,0:T(8,128)(2,1)} collective-permute-done((bf16[2,6,128,256]{3,2,1,0:T(8,128)(2,1)}, bf16[2,6,128,256]{3,2,1,0:T(8,128)(2,1)}, u32[]{:S(2)}, u32[]{:S(2)}) %collective-permute-start.8) | collective-permute-done | bytes 786464 | tf_op jit(solution)/shard_map/ppermute | solution.py:118
  71.7 13.8 %conv_weight.1 = (bf16[9,2,256,256]{3,2,1,0:T(8,128)(2,1)S(1)}, f32[8,256]{1,0:T(8,128)S(1)}) custom-call(s32[7]{0:T(128)S(1)} %concatenate.19.place_ref.place.refs_0_, bf16[2,6,128,256]{3,2,1,0:T(8,128)(2,1)} %collective-permute-done.8.above.refs_1_, bf16[2,16,128,256]{3,2,1,0:T(8,128)(2,1)} %own.3, bf16[2,2,128,256]{3,2,1,0:T(8,128)(2,1)} %collective-permute-done.9.below, ...), custom_call_target="tpu_custom_call" | custom-call | flops 20000000000 | bytes 10000000 | tf_op jit(solution)/shard_map/conv_weight/pallas_call | solution.py:1069
  85.5 0.2 constant_dynamic-slice_fusion.1
  85.6 0.4 copy-done.9
  86.1 2.8 %collective-permute-done.10 = bf16[16,144,256]{2,1,0:T(8,128)(2,1)S(1)} collective-permute-done((bf16[16,144,256]{2,1,0:T(8,128)(2,1)S(1)}, bf16[16,144,256]{2,1,0:T(8,128)(2,1)S(1)}, u32[]{:S(2)}, u32[]{:S(2)}) %collective-permute-start.10) | collective-permute-done | bytes 1179680 | tf_op jit(solution)/shard_map/ppermute | solution.py:96
  88.9 1.5 fusion
  90.4 6.9 %all-to-all-start.2 = ((bf16[16,144,256]{2,1,0:T(8,128)(2,1)}), bf16[16,144,256]{2,1,0:T(8,128)(2,1)S(1)}, u32[]{:S(2)}, u32[]{:S(2)}) async-start(bf16[16,144,256]{2,1,0:T(8,128)(2,1)} %fusion), calls=%async_computation.2 | async-start | bytes 2359296 | tf_op jit(solution)/shard_map/all_to_all | solution.py:102
  97.2 40.2 %backward.1 = (f32[2,16,128,256]{3,2,1,0:T(8,128)}, bf16[2,4,128,256]{3,2,1,0:T(8,128)(2,1)}, bf16[128,3840]{1,0:T(8,128)(2,1)}, bf16[128,3840]{1,0:T(8,128)(2,1)}) custom-call(s32[7]{0:T(128)} %copy-done.6, bf16[2,6,128,256]{3,2,1,0:T(8,128)(2,1)} %collective-permute-done.8.above.refs_1_, bf16[2,16,128,256]{3,2,1,0:T(8,128)(2,1)} %own.3, ...), custom_call_target="tpu_custom_call" | custom-call | flops 40000000000 | bytes 10000000 | tf_op jit(solution)/shard_map/backward/pallas_call | solution.py:793
  137.4 0.1 collective-permute-start.12
  137.5 2.8 %collective-permute-done.12 = bf16[16,8,3840]{2,1,0:T(8,128)(2,1)S(1)} collective-permute-done((bf16[16,8,3840]{2,1,0:T(8,128)(2,1)}, bf16[16,8,3840]{2,1,0:T(8,128)(2,1)S(1)}, u32[]{:S(2)}, u32[]{:S(2)}) %collective-permute-start.12) | collective-permute-done | bytes 983072 | tf_op jit(solution)/shard_map/ppermute | solution.py:96
  140.3 2.5 %fusion.1 = bf16[16,8,3840]{2,1,0:T(8,128)(2,1)} fusion(bf16[16,8,3840]{2,1,0:T(8,128)(2,1)S(1)} %collective-permute-done.12, bf16[128,3840]{1,0:T(8,128)(2,1)} %get-tuple-element.102), kind=kLoop, calls=%fused_computation.3 | loop fusion | flops 1966080 | bytes 2949120 | tf_op jit(solution)/shard_map/convert_element_type | solution.py:97
  142.7 7.0 %all-to-all-start.1 = ((bf16[16,8,3840]{2,1,0:T(8,128)(2,1)}), bf16[16,8,3840]{2,1,0:T(8,128)(2,1)S(1)}, u32[]{:S(2)}, u32[]{:S(2)}) async-start(bf16[16,8,3840]{2,1,0:T(8,128)(2,1)} %fusion.1), calls=%async_computation.1 | async-start | bytes 1966080 | tf_op jit(solution)/shard_map/all_to_all | solution.py:102
  149.8 0.8 sum_parts.1
  150.6 2.0 %collective-permute-start.13 = (bf16[2,4,128,256]{3,2,1,0:T(8,128)(2,1)S(1)}, bf16[2,4,128,256]{3,2,1,0:T(8,128)(2,1)S(1)}, u32[]{:S(2)}, u32[]{:S(2)}) collective-permute-start(bf16[2,4,128,256]{3,2,1,0:T(8,128)(2,1)S(1)} %copy-done.12), channel_id=1, source_target_pairs={{0,28},{4,0},{8,4},{12,8},{16,12},{20,16},{24,20},{28,24},{1,29},{... | collective-permute-start | bytes 1572872 | tf_op jit(solution)/shard_map/ppermute | solution.py:118
  152.6 8.9 %conv_data.1 = f32[2,16,128,256]{3,2,1,0:T(8,128)} custom-call(s32[7]{0:T(128)S(1)} %copy-done.7, bf16[2,6,128,256]{3,2,1,0:T(8,128)(2,1)} %collective-permute-done.8.above.refs_1_, bf16[2,16,128,256]{3,2,1,0:T(8,128)(2,1)} %own.3, bf16[2,2,128,256]{3,2,1,0:T(8,128)(2,1)} %collective-permute-done.9.below, bf16[9,2,256,256]{3,2,1,0:T(8,128)(2,1)} %bitcast.12.refs_14_.weight), custom_call_target="tpu_custom_call" | custom-call | flops 10000000000 | bytes 10000000 | tf_op jit(solution)/shard_map/conv_data/pallas_call | solution.py:1069
  161.5 14.0 %conv_forward.1 = bf16[2,16,128,256]{3,2,1,0:T(8,128)(2,1)} custom-call(s32[7]{0:T(128)S(1)} %copy-done.7, bf16[2,16,128,256]{3,2,1,0:T(8,128)(2,1)S(1)} %copy-done.1, bf16[2,5,128,256]{3,2,1,0:T(8,128)(2,1)} %copy-done.10, bf16[2,6,128,256]{3,2,1,0:T(8,128)(2,1)} %collective-permute-done.8.above.refs_1_, bf16[2,16,128,256]{3,2,1,0:T(8,128)(2,1)} %hidden.3, ...), custom_call_target="tpu_custom_call" | custom-call | flops 1000000 | bytes 10000 | tf_op jit(solution)/shard_map/conv_forward/pallas_call | solution.py:1190
  175.4 1.1 convert_dynamic-update-slice_fusion
  176.5 0.8 last_sums.1
  177.3 0.2 reverse
  177.4 0.7 slice_bitcast_fusion
  (49 shorter events, 0.2 us)
Async XLA Ops:
  1.5 7.7 %collective-permute-start.2 = (bf16[1,8,3072]{2,1,0:T(8,128)(2,1)S(1)}, bf16[1,8,3072]{2,1,0:T(8,128)(2,1)S(1)}, u32[]{:S(2)}, u32[]{:S(2)}) collective-permute-start(bf16[1,8,3072]{2,1,0:T(8,128)(2,1)S(1)} %bitcast.42), channel_id=1, source_target_pairs={{0,3},{1,2},{2,1},{3,0},{4,7},{5,6},{6,5},{7,4},{8,11},{9,10},{10,... | collective-permute-start | bytes 147464 | tf_op jit(solution)/shard_map/ppermute | solution.py:76
  6.6 5.0 %collective-permute-start.1 = (bf16[1,8,3072]{2,1,0:T(8,128)(2,1)S(1)}, bf16[1,8,3072]{2,1,0:T(8,128)(2,1)S(1)}, u32[]{:S(2)}, u32[]{:S(2)}) collective-permute-start(bf16[1,8,3072]{2,1,0:T(8,128)(2,1)S(1)} %bitcast.43), channel_id=1, source_target_pairs={{0,2},{1,3},{2,0},{3,1},{4,6},{5,7},{6,4},{7,5},{8,10},{9,11},{10,... | collective-permute-start | bytes 147464 | tf_op jit(solution)/shard_map/ppermute | solution.py:76
  6.6 5.0 %collective-permute-start = (bf16[1,8,3072]{2,1,0:T(8,128)(2,1)S(1)}, bf16[1,8,3072]{2,1,0:T(8,128)(2,1)S(1)}, u32[]{:S(2)}, u32[]{:S(2)}) collective-permute-start(bf16[1,8,3072]{2,1,0:T(8,128)(2,1)S(1)} %bitcast.44), channel_id=1, source_target_pairs={{0,1},{1,0},{2,3},{3,2},{4,5},{5,4},{6,7},{7,6},{8,9},{9,8},{10,11... | collective-permute-start | bytes 147464 | tf_op jit(solution)/shard_map/ppermute | solution.py:76
  8.3 18.0 %collective-permute-start.6 = (bf16[2,4,128,256]{3,2,1,0:T(8,128)(2,1)S(1)}, bf16[2,4,128,256]{3,2,1,0:T(8,128)(2,1)}, u32[]{:S(2)}, u32[]{:S(2)}) collective-permute-start(bf16[2,4,128,256]{3,2,1,0:T(8,128)(2,1)S(1)} %slice.22), channel_id=1, source_target_pairs={{0,4},{4,8},{8,12},{12,16},{16,20},{20,24},{24,28},{28,0},{1,5},{5... | collective-permute-start | bytes 1572872 | tf_op jit(solution)/shard_map/ppermute | solution.py:118
  9.1 62.5 %copy-start.6 = (s32[7]{0:T(128)}, s32[7]{0:T(128)S(1)}, u32[]{:S(2)}) copy-start(s32[7]{0:T(128)S(1)} %concatenate.19.place_ref.place.refs_0_) | copy-start | bytes 88
  11.6 14.7 %collective-permute-start.5 = (bf16[4,8,3072]{2,1,0:T(8,128)(2,1)S(1)}, bf16[4,8,3072]{2,1,0:T(8,128)(2,1)S(1)}, u32[]{:S(2)}, u32[]{:S(2)}) collective-permute-start(bf16[4,8,3072]{2,1,0:T(8,128)(2,1)S(1)} %pad_maximum_fusion.2), channel_id=1, source_target_pairs={{0,24},{1,25},{2,26},{3,27},{4,28},{5,29},{6,30},{7,31},{8,16},{9,... | collective-permute-start | bytes 589832 | tf_op jit(solution)/shard_map/ppermute | solution.py:76
  14.1 12.2 %collective-permute-start.4 = (bf16[4,8,3072]{2,1,0:T(8,128)(2,1)S(1)}, bf16[4,8,3072]{2,1,0:T(8,128)(2,1)S(1)}, u32[]{:S(2)}, u32[]{:S(2)}) collective-permute-start(bf16[4,8,3072]{2,1,0:T(8,128)(2,1)S(1)} %pad_maximum_fusion.2), channel_id=1, source_target_pairs={{0,16},{1,17},{2,18},{3,19},{4,20},{5,21},{6,22},{7,23},{8,24},{9,... | collective-permute-start | bytes 589832 | tf_op jit(solution)/shard_map/ppermute | solution.py:76
  14.6 10.1 %collective-permute-start.3 = (bf16[4,8,3072]{2,1,0:T(8,128)(2,1)S(1)}, bf16[4,8,3072]{2,1,0:T(8,128)(2,1)S(1)}, u32[]{:S(2)}, u32[]{:S(2)}) collective-permute-start(bf16[4,8,3072]{2,1,0:T(8,128)(2,1)S(1)} %pad_maximum_fusion.2), channel_id=1, source_target_pairs={{0,8},{1,9},{2,10},{3,11},{4,12},{5,13},{6,14},{7,15},{8,0},{9,1},... | collective-permute-start | bytes 589832 | tf_op jit(solution)/shard_map/ppermute | solution.py:76
  15.2 3.5 %copy-start.11 = (f32[225,8]{0,1:T(8,128)S(1)}, f32[225,8]{0,1:T(8,128)}, u32[]{:S(2)}) copy-start(f32[225,8]{0,1:T(8,128)} %param.30) | copy-start | bytes 21604
  15.2 4.2 %slice-start = ((bf16[2,16,128,256]{3,2,1,0:T(8,128)(2,1)}), bf16[2,1,128,256]{3,2,1,0:T(8,128)(2,1)S(1)}, s32[]{:S(2)}) async-start(bf16[2,16,128,256]{3,2,1,0:T(8,128)(2,1)} %own.3), calls=%async_computation.3 | async-start | bytes 262144 | tf_op jit(solution)/shard_map/slice | solution.py:1257
  15.2 4.9 %slice-start.1 = ((bf16[2,16,128,256]{3,2,1,0:T(8,128)(2,1)}), bf16[2,5,128,256]{3,2,1,0:T(8,128)(2,1)S(1)}, s32[]{:S(2)}) async-start(bf16[2,16,128,256]{3,2,1,0:T(8,128)(2,1)} %own.3), calls=%async_computation.4 | async-start | bytes 1310720 | tf_op jit(solution)/shard_map/slice | solution.py:1256
  26.3 2.4 %collective-permute-start.7 = (bf16[16,8,3072]{2,1,0:T(8,128)(2,1)S(1)}, bf16[16,8,3072]{2,1,0:T(8,128)(2,1)S(1)}, u32[]{:S(2)}, u32[]{:S(2)}) collective-permute-start(bf16[16,8,3072]{2,1,0:T(8,128)(2,1)S(1)} %constant_dynamic-update-slice_fusion), channel_id=1, source_target_pairs={{0,4},{1,5},{2,6},{3,7},{4,0},{5,1},{6,2},{7,3},{8,12},{9,13},{10,... | collective-permute-start | bytes 2359304 | tf_op jit(solution)/shard_map/ppermute | solution.py:76
  28.8 7.9 %copy-start.8 = (s32[32]{0:T(128)S(1)}, s32[32]{0:T(128)}, u32[]{:S(2)}) copy-start(s32[32]{0:T(128)} %constant.52.clone.order) | copy-start | bytes 388
  28.8 61.6 %all-to-all-start = ((bf16[32,144,256]{2,1,0:T(8,128)(2,1)}), bf16[32,144,256]{2,1,0:T(8,128)(2,1)}, u32[]{:S(2)}, u32[]{:S(2)}) async-start(bf16[32,144,256]{2,1,0:T(8,128)(2,1)} %make_copies.1), calls=%async_computation | async-start | bytes 4718592 | tf_op jit(solution)/shard_map/all_to_all | solution.py:106
  34.0 37.7 %collective-permute-start.8 = (bf16[2,6,128,256]{3,2,1,0:T(8,128)(2,1)}, bf16[2,6,128,256]{3,2,1,0:T(8,128)(2,1)}, u32[]{:S(2)}, u32[]{:S(2)}) collective-permute-start(bf16[2,6,128,256]{3,2,1,0:T(8,128)(2,1)} %pad_maximum_fusion), channel_id=1, source_target_pairs={{0,4},{4,8},{8,12},{12,16},{16,20},{20,24},{24,28},{28,0},{1,5},{5... | collective-permute-start | bytes 2359304 | tf_op jit(solution)/shard_map/ppermute | solution.py:118
  34.2 35.4 %collective-permute-start.9 = (bf16[2,2,128,256]{3,2,1,0:T(8,128)(2,1)}, bf16[2,2,128,256]{3,2,1,0:T(8,128)(2,1)}, u32[]{:S(2)}, u32[]{:S(2)}) collective-permute-start(bf16[2,2,128,256]{3,2,1,0:T(8,128)(2,1)} %pad_maximum_fusion.1), channel_id=1, source_target_pairs={{0,28},{4,0},{8,4},{12,8},{16,12},{20,16},{24,20},{28,24},{1,29},{... | collective-permute-start | bytes 786440 | tf_op jit(solution)/shard_map/ppermute | solution.py:118
  37.5 13.9 %copy-start.4 = (bf16[256,768]{1,0:T(8,128)(2,1)}, bf16[256,768]{1,0:T(8,128)(2,1)S(1)}, u32[]{:S(2)}) copy-start(bf16[256,768]{1,0:T(8,128)(2,1)S(1)} %get-tuple-element.76.weight.refs_19_) | copy-start | bytes 1179652
  37.5 13.9 %copy-start.2 = (bf16[256,1024]{1,0:T(8,128)(2,1)}, bf16[256,1024]{1,0:T(8,128)(2,1)S(1)}, u32[]{:S(2)}) copy-start(bf16[256,1024]{1,0:T(8,128)(2,1)S(1)} %get-tuple-element.80.up_w.refs_17_) | copy-start | bytes 1572868
  37.5 13.9 %copy-start.3 = (bf16[1024,256]{1,0:T(8,128)(2,1)}, bf16[1024,256]{1,0:T(8,128)(2,1)S(1)}, u32[]{:S(2)}) copy-start(bf16[1024,256]{1,0:T(8,128)(2,1)S(1)} %get-tuple-element.81.down_w.refs_18_) | copy-start | bytes 1572868
  37.5 13.9 %copy-start.5 = (bf16[256,256]{1,0:T(8,128)(2,1)}, bf16[256,256]{1,0:T(8,128)(2,1)S(1)}, u32[]{:S(2)}) copy-start(bf16[256,256]{1,0:T(8,128)(2,1)S(1)} %get-tuple-element.79.out_w.refs_15_) | copy-start | bytes 393220
  51.3 18.2 %copy-start = (bf16[4096,256]{1,0:T(8,128)(2,1)}, bf16[4096,256]{1,0:T(8,128)(2,1)S(1)}, u32[]{:S(2)}) copy-start(bf16[4096,256]{1,0:T(8,128)(2,1)S(1)} %get-tuple-element.78.mix.refs_8_) | copy-start | bytes 6291460
  85.5 0.6 copy-start.9
  86.1 2.8 %collective-permute-start.10 = (bf16[16,144,256]{2,1,0:T(8,128)(2,1)S(1)}, bf16[16,144,256]{2,1,0:T(8,128)(2,1)S(1)}, u32[]{:S(2)}, u32[]{:S(2)}) collective-permute-start(bf16[16,144,256]{2,1,0:T(8,128)(2,1)S(1)} %bitcast.46), channel_id=1, source_target_pairs={{0,4},{4,0},{8,12},{12,8},{16,20},{20,16},{24,28},{28,24},{1,5},{5... | collective-permute-start | bytes 3538952 | tf_op jit(solution)/shard_map/ppermute | solution.py:96
  90.4 47.0 %collective-permute-start.11 = (bf16[2,5,128,256]{3,2,1,0:T(8,128)(2,1)}, bf16[2,5,128,256]{3,2,1,0:T(8,128)(2,1)S(1)}, u32[]{:S(2)}, u32[]{:S(2)}) collective-permute-start(bf16[2,5,128,256]{3,2,1,0:T(8,128)(2,1)} %get-tuple-element.101), channel_id=1, source_target_pairs={{0,28},{4,0},{8,4},{12,8},{16,12},{20,16},{24,20},{28,24},{1,29},{... | collective-permute-start | bytes 1966088 | tf_op jit(solution)/shard_map/ppermute | solution.py:118
  90.4 52.4 %all-to-all-start.2 = ((bf16[16,144,256]{2,1,0:T(8,128)(2,1)}), bf16[16,144,256]{2,1,0:T(8,128)(2,1)S(1)}, u32[]{:S(2)}, u32[]{:S(2)}) async-start(bf16[16,144,256]{2,1,0:T(8,128)(2,1)} %fusion), calls=%async_computation.2 | async-start | bytes 2359296 | tf_op jit(solution)/shard_map/all_to_all | solution.py:102
  137.4 5.3 %copy-start.10 = (bf16[2,5,128,256]{3,2,1,0:T(8,128)(2,1)}, bf16[2,5,128,256]{3,2,1,0:T(8,128)(2,1)S(1)}, u32[]{:S(2)}) copy-start(bf16[2,5,128,256]{3,2,1,0:T(8,128)(2,1)S(1)} %collective-permute-done.11.sums_below) | copy-start | bytes 1966084
  137.4 2.8 %collective-permute-start.12 = (bf16[16,8,3840]{2,1,0:T(8,128)(2,1)}, bf16[16,8,3840]{2,1,0:T(8,128)(2,1)S(1)}, u32[]{:S(2)}, u32[]{:S(2)}) collective-permute-start(bf16[16,8,3840]{2,1,0:T(8,128)(2,1)} %bitcast.58), channel_id=1, source_target_pairs={{0,4},{4,0},{8,12},{12,8},{16,20},{20,16},{24,28},{28,24},{1,5},{5... | collective-permute-start | bytes 2949128 | tf_op jit(solution)/shard_map/ppermute | solution.py:96
  142.7 7.9 %copy-start.12 = (bf16[2,4,128,256]{3,2,1,0:T(8,128)(2,1)S(1)}, bf16[2,4,128,256]{3,2,1,0:T(8,128)(2,1)}, u32[]{:S(2)}) copy-start(bf16[2,4,128,256]{3,2,1,0:T(8,128)(2,1)} %get-tuple-element.109) | copy-start | bytes 1572868
  142.7 9.9 %copy-start.7 = (s32[7]{0:T(128)S(1)}, s32[7]{0:T(128)}, u32[]{:S(2)}) copy-start(s32[7]{0:T(128)} %copy-done.6) | copy-start | bytes 88
  142.7 33.8 %all-to-all-start.1 = ((bf16[16,8,3840]{2,1,0:T(8,128)(2,1)}), bf16[16,8,3840]{2,1,0:T(8,128)(2,1)S(1)}, u32[]{:S(2)}, u32[]{:S(2)}) async-start(bf16[16,8,3840]{2,1,0:T(8,128)(2,1)} %fusion.1), calls=%async_computation.1 | async-start | bytes 1966080 | tf_op jit(solution)/shard_map/all_to_all | solution.py:102
  150.6 10.9 %copy-start.1 = (bf16[2,16,128,256]{3,2,1,0:T(8,128)(2,1)S(1)}, bf16[2,16,128,256]{3,2,1,0:T(8,128)(2,1)}, u32[]{:S(2)}) copy-start(bf16[2,16,128,256]{3,2,1,0:T(8,128)(2,1)} %get-tuple-element.94.sums) | copy-start | bytes 6291460
  150.6 24.8 %collective-permute-start.13 = (bf16[2,4,128,256]{3,2,1,0:T(8,128)(2,1)S(1)}, bf16[2,4,128,256]{3,2,1,0:T(8,128)(2,1)S(1)}, u32[]{:S(2)}, u32[]{:S(2)}) collective-permute-start(bf16[2,4,128,256]{3,2,1,0:T(8,128)(2,1)S(1)} %copy-done.12), channel_id=1, source_target_pairs={{0,28},{4,0},{8,4},{12,8},{16,12},{20,16},{24,20},{28,24},{1,29},{... | collective-permute-start | bytes 1572872 | tf_op jit(solution)/shard_map/ppermute | solution.py:118
